TPU v7x, 128 devices: a whole 4x4x4 slice. The times are simulated.
128 devices in a mesh: rep: 32 (over x, y, core), opt: 4 (over z).
Axes of the slice: x: 4, y: 4, z: 4, core: 2. Of those that a mesh axis runs over, the one named last changes fastest.
Arguments:
- context: bfloat16 [131072, 1024], P(('rep', 'opt')), may hold values from -12 to 12
- residual_in: bfloat16 [131072, 1024], P(('rep', 'opt')), may hold values from -6 to 6
- cotangent: bfloat16 [131072, 1024], P(('rep', 'opt')), may hold values from -6 to 6
- weight: bfloat16 [1024, 1024], replicated, may hold values from -0.1875 to 0.1875
- master: float32 [1024, 1024], P('opt'), may hold values from -1.875 to 1.875
- moment_first: float32 [1024, 1024], P('opt'), may hold values from -0.004 to 0.004
- moment_second: float32 [1024, 1024], P('opt'), may hold values from 1e-07 to 1e-05
- out_bias: float32 [1024], replicated, may hold values from -4 to 4
- ln_gain: float32 [1024], replicated, may hold values from 0.5 to 1.5
- ln_shift: float32 [1024], replicated, may hold values from -4 to 4
- vector_first: float32 [3, 1024], replicated, may hold values from -0.015625 to 0.015625
- vector_second: float32 [3, 1024], replicated, may hold values from 1e-07 to 1e-05
Outputs:
- d_context: bfloat16 [131072, 1024], P(('rep', 'opt'))
- d_resid: bfloat16 [131072, 1024], P(('rep', 'opt'))
- new_weight: bfloat16 [1024, 1024], replicated
- new_master: float32 [1024, 1024], P('opt')
- new_first: float32 [1024, 1024], P('opt')
- new_second: float32 [1024, 1024], P('opt')
- new_vectors: float32 [3, 1024], replicated
- new_vector_first: float32 [3, 1024], replicated
- new_vector_second: float32 [3, 1024], replicated
All inputs are finite; a program needn't handle non-finite values.
Results may differ from a plain program's by a relative error of at most 0.0085.
Values may be sent and summed in bfloat16 or wider, within the bound.
No kernel may reach another device: no remote copies, remote signals or barrier semaphores. Data moves between devices by JAX's collectives and lax.ppermute only.
A program may use at most 128 MiB of HBM per device.

v0:
```python
import jax
import jax.numpy as jnp
from jax import lax
from jax.sharding import PartitionSpec as P

beta_one = 0.9
beta_two = 0.999
adam_eps = 1e-06
learn_rate = 0.2
decay_rate = 0.01
max_norm = 1.0


def moments(grad, first, second, param, decay):
    first_new = beta_one * first + (1.0 - beta_one) * grad
    second_new = beta_two * second + (1.0 - beta_two) * grad * grad
    update = first_new / (jnp.sqrt(second_new) + adam_eps) + decay * param
    return (first_new, second_new, update)


def on_device(
    context,
    residual_in,
    cotangent,
    weight,
    master,
    moment_first,
    moment_second,
    out_bias,
    ln_gain,
    ln_shift,
    vector_first,
    vector_second,
):
    weight_sq = lax.psum(jnp.sum(master * master), "opt")
    pre = (
        residual_in.astype(jnp.float32)
        + jnp.dot(context, weight, preferred_element_type=jnp.float32)
        + out_bias
    )
    centred = pre - jnp.mean(pre, axis=1, keepdims=True)
    rstd = lax.rsqrt(jnp.mean(centred * centred, axis=1, keepdims=True) + 1e-05)
    normed = centred * rstd
    grad_out = cotangent.astype(jnp.float32)
    scaled = grad_out * ln_gain
    d_pre = rstd * (
        scaled
        - jnp.mean(scaled, axis=1, keepdims=True)
        - normed * jnp.mean(scaled * normed, axis=1, keepdims=True)
    )
    d_resid = d_pre.astype(jnp.bfloat16)
    d_context = lax.dot_general(
        d_resid, weight, (((1,), (1,)), ((), ())), preferred_element_type=jnp.float32
    ).astype(jnp.bfloat16)
    bias_sum, gain_sum, shift_sum = lax.psum(
        (jnp.sum(d_pre, axis=0), jnp.sum(grad_out * normed, axis=0), jnp.sum(grad_out, axis=0)),
        ("rep", "opt"),
    )
    grad_vectors = jnp.stack([bias_sum, gain_sum, shift_sum])
    group_part = lax.psum_scatter(
        lax.dot_general(
            context, d_resid, (((0,), (0,)), ((), ())), preferred_element_type=jnp.float32
        ).astype(jnp.bfloat16),
        "opt",
        scatter_dimension=0,
        tiled=True,
    )
    grad_weight = lax.psum(group_part, "rep").astype(jnp.float32)
    grad_sq_local = jnp.sum(grad_weight * grad_weight)
    grad_sq = lax.psum(grad_sq_local, "opt")
    total = jnp.sqrt(grad_sq + jnp.sum(grad_vectors * grad_vectors))
    factor = 1.0 / jnp.maximum(1.0, total / max_norm)
    new_first, new_second, update = moments(
        grad_weight * factor, moment_first, moment_second, master, decay_rate
    )
    update_sq = lax.psum(jnp.sum(update * update), "opt")
    trust = jnp.sqrt(weight_sq) / jnp.sqrt(update_sq + 1e-06)
    new_master = master - learn_rate * trust * update
    new_weight = lax.all_gather(new_master.astype(jnp.bfloat16), "opt", axis=0, tiled=True)
    vectors = jnp.stack([out_bias, ln_gain, ln_shift])
    new_vector_first, new_vector_second, vector_step = moments(
        grad_vectors * factor, vector_first, vector_second, vectors, 0.0
    )
    vector_trust = jnp.sqrt(jnp.sum(vectors * vectors, axis=1, keepdims=True)) / jnp.sqrt(
        jnp.sum(vector_step * vector_step, axis=1, keepdims=True) + 1e-06
    )
    new_vectors = vectors - learn_rate * vector_trust * vector_step
    return (
        d_context,
        d_resid,
        new_weight,
        new_master,
        new_first,
        new_second,
        new_vectors,
        new_vector_first,
        new_vector_second,
    )


def solution(mesh):
    in_specs = (
        P(("rep", "opt"), None),
        P(("rep", "opt"), None),
        P(("rep", "opt"), None),
        P(),
        P("opt", None),
        P("opt", None),
        P("opt", None),
        P(),
        P(),
        P(),
        P(),
        P(),
    )
    out_specs = (
        P(("rep", "opt"), None),
        P(("rep", "opt"), None),
        P(),
        P("opt", None),
        P("opt", None),
        P("opt", None),
        P(),
        P(),
        P(),
    )
    return jax.shard_map(
        on_device, mesh=mesh, in_specs=in_specs, out_specs=out_specs, check_vma=False
    )
```

profile of v0, /device:TPU:1, one launch (start us, length us, event | category | flops | bytes accessed | tf_op | source)
XLA Modules:
  0.0 247.8 jit_solution(4030557683914423755)
XLA Ops:
  7.2 0.0 copy-start
  7.2 0.0 copy-start.7
  7.2 0.0 reduce-scatter.2.cloned.1.call-start
  7.2 4.1 %copy.22 = bf16[1024,1024]{0,1:T(8,128)(2,1)} copy(bf16[1024,1024]{1,0:T(8,128)(2,1)} %param.14) | data formatting | bytes 4194304 | tf_op args[2]
  11.3 3.9 %copy.21 = bf16[1024,1024]{0,1:T(8,128)(2,1)} copy(bf16[1024,1024]{1,0:T(8,128)(2,1)} %param.13) | data formatting | bytes 4194304 | tf_op args[1]
  15.3 0.0 copy-done
  15.3 0.0 copy-done.7
  15.3 5.0 %fusion.18 = (f32[1024]{0:T(1024)S(1)}, f32[1024,1024]{0,1:T(8,128)S(1)}) fusion(f32[1024]{0:T(1024)S(1)} %copy-done.7, bf16[1024,1024]{1,0:T(8,128)(2,1)S(1)} %copy-done, bf16[1024,1024]{1,0:T(8,128)(2,1)} %param.15, bf16[1024,1024]{0,1:T(8,128)(2,1)} %copy.21), kind=kOutput, calls=%fused_computation.44 | convolution fusion | flops 2151676928 | bytes 10493952 | tf_op jit(solution)/shard_map/dot_general | solution.py:38
  20.3 0.0 copy-start.1
  20.3 0.0 copy-start.4
  20.3 0.5 multiply_reduce_fusion
  20.8 1.1 copy-done.1
  21.9 0.0 copy-done.4
  21.9 1.0 fusion.2
  22.9 2.7 %fusion.11 = (f32[1024]{0:T(1024)S(1)}, f32[1024]{0:T(1024)S(1)}, f32[1024]{0:T(1024)S(1)}, bf16[1024,1024]{0,1:T(8,128)(2,1)S(1)}) fusion(f32[1024]{0:T(1024)S(1)} %get-tuple-element.41, f32[1024,1024]{0,1:T(8,128)S(1)} %get-tuple-element.40, f32[1024]{0:T(1024)S(1)} %broadcast_multiply_fusion.2, f32[1024]{0:T(1024)S(1)} %get-tuple-element.42, ...), kind=kLoop, calls=%fused_computation.26 | loop fusion | flops 13628416 | bytes 8421376 | tf_op jit(solution)/shard_map/reduce_sum | solution.py:56
  25.7 0.0 copy-start.3
  25.7 1.3 copy-done.3
  27.0 3.7 %convert_bitcast_fusion = bf16[1024,1024]{0,1:T(8,128)(2,1)} fusion(bf16[1024,1024]{0,1:T(8,128)(2,1)S(1)} %get-tuple-element.37, bf16[1024,1024]{1,0:T(8,128)(2,1)S(1)} %copy-done), kind=kOutput, calls=%fused_computation.13 | convolution fusion | flops 2148532224 | bytes 6291456 | tf_op jit(solution)/shard_map/dot_general | solution.py:61
  30.7 0.0 reduce-scatter.2.cloned.1.call-update
  30.7 0.0 all-reduce.4.cloned.1.call-start
  30.7 33.3 %reduce-scatter.2.cloned.1.call-done = bf16[256,1024]{0,1:T(8,128)(2,1)} async-done(((bf16[1024,1024]{0,1:T(8,128)(2,1)}), bf16[256,1024]{0,1:T(8,128)(2,1)}) %reduce-scatter.2.cloned.1.call-update) | async-done | bytes 524304 | tf_op jit(solution)/shard_map/reduce_scatter | solution.py:60
  64.0 0.0 all-reduce.4.cloned.1.call-update
  64.0 0.0 all-gather.2.cloned.1.call-start
  64.1 1.6 copy.26
  65.6 2.5 %copy.24 = f32[256,1024]{0,1:T(8,128)} copy(f32[256,1024]{1,0:T(8,128)} %param.18) | data formatting | bytes 2097152 | tf_op args[6]
  68.2 65.3 %all-reduce = (f32[1,1024]{1,0:T(1,128)S(1)}, f32[1,1024]{1,0:T(1,128)S(1)}, f32[1,1024]{1,0:T(1,128)S(1)}) all-reduce(f32[1,1024]{1,0:T(1,128)S(1)} %bitcast.18, f32[1,1024]{1,0:T(1,128)S(1)} %bitcast.17, f32[1,1024]{1,0:T(1,128)S(1)} %bitcast.16), channel_id=1, replica_groups=mesh['rep'=32,'opt'=4] {'rep','opt'}, use_global_device_ids=true, to_apply=%region_15.0 | all-reduce | flops 3072 | bytes 24576 | tf_op jit(solution)/shard_map/psum | solution.py:55
  133.4 0.6 multiply_reduce_fusion.5
  134.1 2.1 multiply_reduce_fusion.2
  136.2 34.3 %all-reduce.4.cloned.1.call-done = bf16[256,1024]{0,1:T(8,128)(2,1)} async-done(((bf16[256,1024]{0,1:T(8,128)(2,1)}), bf16[256,1024]{0,1:T(8,128)(2,1)}) %all-reduce.4.cloned.1.call-update) | async-done | bytes 524304 | tf_op jit(solution)/shard_map/psum | solution.py:68
  170.4 1.9 fusion.9
  172.3 2.5 %copy.23 = f32[256,1024]{0,1:T(8,128)} copy(f32[256,1024]{1,0:T(8,128)} %param.17) | data formatting | bytes 2097152 | tf_op args[5]
  174.9 9.3 %psum.51 = f32[]{:T(128)} all-reduce(f32[]{:T(128)} %fusion.9), channel_id=1, replica_groups=mesh['rep'=32,'opt'=4] {'opt'}, use_global_device_ids=true, to_apply=%region_9.0 | all-reduce | flops 1 | bytes 8 | tf_op jit(solution)/shard_map/psum | solution.py:70
  185.5 4.4 %multiply_reduce_fusion.1 = (f32[]{:T(128)}, f32[256,1024]{0,1:T(8,128)}, f32[256,1024]{0,1:T(8,128)}) fusion(f32[256,1024]{0,1:T(8,128)S(1)} %copy.26, f32[]{:T(128)S(6)} %div.32, bf16[256,1024]{0,1:T(8,128)(2,1)} %all-reduce.4.cloned.1.call-done, f32[256,1024]{0,1:T(8,128)} %copy.24, f32[256,1024]{0,1:T(8,128)} %copy.23), kind=kLoop, calls=%fused_computation.23 | loop fusion | flops 3932159 | bytes 5767176 | tf_op jit(solution)/shard_map/reduce_sum | solution.py:76
  189.9 6.8 %all-reduce.1 = (f32[]{:T(128)}, f32[]{:T(128)}) all-reduce(f32[]{:T(128)} %multiply_reduce_fusion.2, f32[]{:T(128)} %get-tuple-element.34), channel_id=1, replica_groups=mesh['rep'=32,'opt'=4] {'opt'}, use_global_device_ids=true, to_apply=%region_5.0 | all-reduce | flops 2 | bytes 16 | tf_op jit(solution)/shard_map/psum | solution.py:35
  198.1 3.2 %fusion.15 = (bf16[256,1024]{0,1:T(8,128)(2,1)}, f32[256,1024]{0,1:T(8,128)}) fusion(f32[256,1024]{0,1:T(8,128)S(1)} %copy.26, f32[256,1024]{0,1:T(8,128)} %get-tuple-element.36, f32[256,1024]{0,1:T(8,128)} %get-tuple-element.35, f32[]{:T(128)S(6)} %mul.187), kind=kLoop, calls=%fused_computation.43 | loop fusion | flops 1835008 | bytes 4718596 | tf_op jit(solution)/shard_map/convert_element_type | solution.py:79
  201.3 0.0 all-gather.2.cloned.1.call-update
  201.3 3.9 %copy.27 = bf16[1024,1024]{1,0:T(8,128)(2,1)} copy(bf16[1024,1024]{0,1:T(8,128)(2,1)} %copy-done.3) | data formatting | bytes 4194304
  205.2 6.0 %convolution_convert_fusion = bf16[1024,1024]{1,0:T(8,128)(2,1)} fusion(bf16[1024,1024]{0,1:T(8,128)(2,1)} %copy-done.3, bf16[1024,1024]{1,0:T(8,128)(2,1)} %param.15), kind=kOutput, calls=%fused_computation.14 | convolution fusion | flops 2148532224 | bytes 6291456 | tf_op jit(solution)/shard_map/dot_general | solution.py:52
  211.3 2.6 %copy.30 = f32[256,1024]{1,0:T(8,128)} copy(f32[256,1024]{0,1:T(8,128)} %get-tuple-element.36) | data formatting | bytes 2097152
  213.9 0.0 copy-done.2
  213.9 1.3 copy.31
  215.2 2.6 %copy.29 = f32[256,1024]{1,0:T(8,128)} copy(f32[256,1024]{0,1:T(8,128)} %get-tuple-element.33) | data formatting | bytes 2097152
  217.7 0.0 copy-done.5
  217.7 0.0 copy-done.8
  217.7 0.8 multiply_reduce_fusion.3
  218.6 0.7 multiply_subtract_fusion.1
  219.3 18.0 %all-gather.2.cloned.1.call-done = bf16[1024,1024]{0,1:T(8,128)(2,1)} async-done(((bf16[256,1024]{0,1:T(8,128)(2,1)}), bf16[1024,1024]{0,1:T(8,128)(2,1)}) %all-gather.2.cloned.1.call-update) | async-done | bytes 2097168 | tf_op jit(solution)/shard_map/all_gather | solution.py:79
  237.3 3.9 %copy.28 = bf16[1024,1024]{1,0:T(8,128)(2,1)} copy(bf16[1024,1024]{0,1:T(8,128)(2,1)} %all-gather.2.cloned.1.call-done) | data formatting | bytes 4194304
  (9 shorter events, 0.0 us)
Async XLA Ops:
  7.2 8.1 %copy-start = (bf16[1024,1024]{1,0:T(8,128)(2,1)S(1)}, bf16[1024,1024]{1,0:T(8,128)(2,1)}, u32[]{:S(2)}) copy-start(bf16[1024,1024]{1,0:T(8,128)(2,1)} %param.12) | copy-start | bytes 6291460
  7.2 8.1 %copy-start.7 = (f32[1024]{0:T(1024)S(1)}, f32[1024]{0:T(1024)}, u32[]{:S(2)}) copy-start(f32[1024]{0:T(1024)} %param.19) | copy-start | bytes 12292
  7.2 56.8 %reduce-scatter.2.cloned.1.call-start = ((), (), s32[]{:S(2)}) async-start(), calls=%async_computation.1 | async-start | bytes 2621440 | tf_op jit(solution)/shard_map/reduce_scatter | solution.py:60
  20.3 1.6 copy-start.1
  20.3 1.6 copy-start.4
  25.7 1.3 copy-start.3
  30.7 139.7 %all-reduce.4.cloned.1.call-start = ((), (), s32[]{:S(2)}) async-start(), calls=%async_computation.2 | async-start | bytes 1048576 | tf_op jit(solution)/shard_map/psum | solution.py:68
  64.0 173.3 %all-gather.2.cloned.1.call-start = ((), (), s32[]{:S(2)}) async-start(), calls=%async_computation.3 | async-start | bytes 2621440 | tf_op jit(solution)/shard_map/all_gather | solution.py:79
  205.2 8.6 %copy-start.2 = (f32[256,1024]{0,1:T(8,128)S(1)}, f32[256,1024]{0,1:T(8,128)}, u32[]{:S(2)}) copy-start(f32[256,1024]{0,1:T(8,128)} %get-tuple-element.35) | copy-start | bytes 3145732
  211.2 6.5 %copy-start.5 = (f32[3,1024]{1,0:T(4,128)S(1)}, f32[3,1024]{1,0:T(4,128)}, u32[]{:S(2)}) copy-start(f32[3,1024]{1,0:T(4,128)} %param.23) | copy-start | bytes 36868
  211.3 6.5 %copy-start.6 = (f32[3,1024]{1,0:T(4,128)S(1)}, f32[3,1024]{1,0:T(4,128)}, u32[]{:S(2)}) copy-start(f32[3,1024]{1,0:T(4,128)} %param.22) | copy-start | bytes 36868
  211.3 6.5 %copy-start.8 = (f32[1024]{0:T(1024)S(1)}, f32[1024]{0:T(1024)}, u32[]{:S(2)}) copy-start(f32[1024]{0:T(1024)} %param.21) | copy-start | bytes 12292
Sparse Core Ops, SparseCore 0:
  30.8 33.1 reduce-scatter.1
  67.5 102.8 all-reduce.3
  201.4 35.8 all-gather.1
where the time goes:
time: 249 us; the launch traced here: 248 us
  waiting for transfers between devices  85.6 us (34%)
  blocking collectives  81.3 us (33%)
  local copies, waits for them, and re-layouts  31.4 us (13%)
  other arithmetic  18 us (7%)
  between operations  16.6 us (7%)
  matrix products  14.7 us (6%)
    psum x1, blocking collectives, on_device(): lax.psum((jnp.sum(d_pre, axis=0), jnp.sum(grad_out * normed, axis=0), jnp...  65.3 us
    psum x1, waiting for transfers between devices, on_device(): grad_weight = lax.psum(group_part, 'rep').astype(jnp.float32)  34.3 us
    reduce_scatter x1, waiting for transfers between devices, on_device(): lax.psum_scatter(lax.dot_general(context, d_resid, (((0,), (0,)), ((), ()...  33.3 us
    unnamed x28, local copies, waits for them, and re-layouts  31.4 us
    all_gather x1, waiting for transfers between devices, on_device(): lax.all_gather(new_master.astype(jnp.bfloat16), 'opt', axis=0, tiled=True)  18 us
    psum x1, blocking collectives, on_device(): grad_sq = lax.psum(grad_sq_local, 'opt')  9.26 us
    psum x1, blocking collectives, on_device(): weight_sq = lax.psum(jnp.sum(master * master), 'opt')  6.79 us
    dot_general x1, matrix products, on_device(): lax.dot_general(d_resid, weight, (((1,), (1,)), ((), ())), preferred_elem...  6.01 us
  transfers between devices with their start and end apart: 3, of which 3 were waited for; matrix products, arithmetic and copies ran while one was open for 10% of the time, Pallas kernels for 0%

commit v1 on v0

v1 whole, which is shorter than its diff:
```python
import jax
import jax.numpy as jnp
from jax import lax
from jax.experimental import pallas as pl
from jax.experimental.pallas import tpu as pltpu
from jax.sharding import PartitionSpec as P

beta_one = 0.9
beta_two = 0.999
adam_eps = 1e-06
learn_rate = 0.2
decay_rate = 0.01
max_norm = 1.0

D = 1024
BLOCK = 256
F32 = jnp.float32
BF16 = jnp.bfloat16
MIB = 1024 * 1024
AXES = ("rep", "opt")
VMEM = pl.BlockSpec(memory_space=pltpu.VMEM)
SMEM = pl.BlockSpec(memory_space=pltpu.SMEM)
HOPS = (1, 3, 2)


def place(x, y, c, z):
    return (((x % 4) * 4 + y % 4) * 2 + c % 2) * 4 + z % 4


def shift(value, x=0, y=0, c=0, z=0):
    pairs = [
        (place(i, j, k, m), place(i + x, j + y, k + c, m + z))
        for i in range(4)
        for j in range(4)
        for k in range(2)
        for m in range(4)
    ]
    return lax.ppermute(value, AXES, pairs)


def call(kernel, outs, ins, specs=None, scratch=(), cost=None, limit=60, **more):
    return pl.pallas_call(
        kernel,
        out_shape=[jax.ShapeDtypeStruct(shape, dtype) for shape, dtype in outs],
        in_specs=[SMEM] + [VMEM] * (len(ins) - 1) if specs is None else specs,
        out_specs=more.pop("out_specs", [VMEM] * len(outs)),
        scratch_shapes=list(scratch),
        cost_estimate=cost,
        compiler_params=pltpu.CompilerParams(vmem_limit_bytes=limit * MIB),
        **more,
    )(*ins)


def sum_pairs(own, hop1, hop3, hop2):
    return (own.astype(F32) + hop2.astype(F32)) + (hop1.astype(F32) + hop3.astype(F32))


def split_vectors(rows):
    high = rows.astype(BF16).astype(F32)
    return jnp.concatenate([high, rows - high], axis=0).astype(BF16)


def join_vectors(message):
    wide = message.astype(F32)
    return wide[0:8] + wide[8:16]


def backward_kernel(
    at, ctx, res, cot, weight, bias, gain, dres, send, keep, ctxs, dress, pre, sums
):
    step = pl.program_id(0)
    rows = pl.ds(pl.multiple_of(step * BLOCK, BLOCK), BLOCK)
    for m in range(4):
        ctxs[m, rows, :] = ctx[:, m * 256 : (m + 1) * 256]
    pre[...] = jnp.dot(ctx[...], weight[...], preferred_element_type=F32)

    @pl.when(step == 0)
    def _():
        sums[...] = jnp.zeros_like(sums)

    bias_row = bias[...]
    gain_row = gain[...]

    def chunk(i, carry):
        at_rows = pl.ds(pl.multiple_of(i * 16, 16), 16)
        value = pre[at_rows, :] + res[at_rows, :].astype(F32) + bias_row
        grad_out = cot[at_rows, :].astype(F32)
        scaled = grad_out * gain_row
        mean = jnp.sum(value, axis=1, keepdims=True) * (1.0 / D)
        mean_scaled = jnp.sum(scaled, axis=1, keepdims=True) * (1.0 / D)
        centred = value - mean
        var = jnp.sum(centred * centred, axis=1, keepdims=True) * (1.0 / D)
        cross = jnp.sum(scaled * centred, axis=1, keepdims=True) * (1.0 / D)
        rstd = lax.rsqrt(var + 1e-05)
        normed = centred * rstd
        d_pre = rstd * (scaled - mean_scaled - normed * (cross * rstd))
        d_low = d_pre.astype(BF16)
        dres[at_rows, :] = d_low
        dress[pl.ds(pl.multiple_of(step * BLOCK + i * 16, 16), 16), :] = d_low
        moved = grad_out * normed
        sums[0] += d_pre[0:8] + d_pre[8:16]
        sums[1] += moved[0:8] + moved[8:16]
        sums[2] += grad_out[0:8] + grad_out[8:16]
        return carry

    lax.fori_loop(0, BLOCK // 16, chunk, 0, unroll=2)

    @pl.when(step == D // BLOCK - 1)
    def _():
        core = at[2]

        def rows_of(m):
            return lax.dot_general(
                ctxs[m], dress[...], (((0,), (0,)), ((), ())), preferred_element_type=F32
            ).astype(BF16)

        for half in range(2):
            send[half * 256 : (half + 1) * 256, :] = rows_of((1 - core) * 2 + half)
        for half in range(2):
            keep[half * 256 : (half + 1) * 256, :] = rows_of(core * 2 + half)
        total = [jnp.sum(sums[k], axis=0, keepdims=True) for k in range(3)]
        message = split_vectors(jnp.concatenate(total + [jnp.zeros((5, D), F32)], axis=0))
        send[512:528, :] = message
        keep[512:528, :] = message


def backward(at, context, residual_in, cotangent, weight, bias, gain):
    block = pl.BlockSpec((BLOCK, D), lambda i: (i, 0))
    whole = pl.BlockSpec((D, D), lambda i: (0, 0))
    row = pl.BlockSpec((1, D), lambda i: (0, 0))
    half = pl.BlockSpec((528, D), lambda i: (0, 0))
    return call(
        backward_kernel,
        [((D, D), BF16), ((528, D), BF16), ((528, D), BF16)],
        (at, context, residual_in, cotangent, weight, bias, gain),
        specs=[SMEM, block, block, block, whole, row, row],
        out_specs=[block, half, half],
        grid=(D // BLOCK,),
        scratch=[
            pltpu.VMEM((4, D, 256), BF16),
            pltpu.VMEM((D, D), BF16),
            pltpu.VMEM((BLOCK, D), F32),
            pltpu.VMEM((3, 8, D), F32),
        ],
        cost=pl.CostEstimate(flops=4 * D**3, bytes_accessed=14 * MIB, transcendentals=D),
        limit=40,
    )


def context_kernel(dres, weight, out):
    out[...] = lax.dot_general(
        dres[...], weight[...], (((1,), (1,)), ((), ())), preferred_element_type=F32
    ).astype(BF16)


def context_grad(d_resid, weight):
    block = pl.BlockSpec((BLOCK, D), lambda i: (i, 0))
    return call(
        context_kernel,
        [((D, D), BF16)],
        (d_resid, weight),
        specs=[block, pl.BlockSpec((D, D), lambda i: (0, 0))],
        out_specs=[block],
        grid=(D // BLOCK,),
        cost=pl.CostEstimate(flops=2 * D**3, bytes_accessed=6 * MIB, transcendentals=0),
        limit=24,
    )[0]


def pack_kernel(at, master, first, second, out):
    out[0] = master[...].astype(BF16)
    out[1] = first[...].astype(BF16)
    out[2] = second[...].astype(BF16)


def pack_state(at, master, first, second):
    return pl.pallas_call(
        pack_kernel,
        out_shape=jax.ShapeDtypeStruct((3, 128, D), BF16),
        grid_spec=pltpu.PrefetchScalarGridSpec(
            num_scalar_prefetch=1,
            grid=(1,),
            in_specs=[pl.BlockSpec((128, D), lambda i, at: (at[2], 0))] * 3,
            out_specs=pl.BlockSpec((3, 128, D), lambda i, at: (0, 0, 0)),
        ),
        compiler_params=pltpu.CompilerParams(vmem_limit_bytes=16 * MIB),
    )(at, master, first, second)


def state_kernel(at, master, first, second, *rest):
    near, other, out = rest[0:3], rest[3:6], rest[6]
    core, z = at[2], at[3]
    own = pl.ds(pl.multiple_of(z * 256, 256), 256)
    out[0, own, :] = master[...].astype(BF16)
    out[1, own, :] = first[...].astype(BF16)
    out[2, own, :] = second[...].astype(BF16)
    for hop, mine, others in zip(HOPS, near, other):
        base = lax.rem(z + 4 - hop, 4) * 256
        out[:, pl.ds(pl.multiple_of(base + core * 128, 128), 128), :] = mine[...]
        out[:, pl.ds(pl.multiple_of(base + (1 - core) * 128, 128), 128), :] = others[...]


def core_kernel(at, keep, got, *outs):
    a_outs, b_outs = outs[0:4], outs[4:8]
    x, y = at[0], at[1]
    message = split_vectors(join_vectors(keep[512:528, :]) + join_vectors(got[512:528, :]))
    for hop, out in zip((0,) + HOPS, a_outs):
        rows = pl.ds(pl.multiple_of(lax.rem(x + hop, 4) * 64, 64), 64)
        out[0:64, :] = (keep[rows, :].astype(F32) + got[rows, :].astype(F32)).astype(BF16)
        out[64:80, :] = message
    for hop, out in zip((0,) + HOPS, b_outs):
        rows = pl.ds(pl.multiple_of(256 + lax.rem(y + hop, 4) * 64, 64), 64)
        out[...] = (keep[rows, :].astype(F32) + got[rows, :].astype(F32)).astype(BF16)


def second_kernel(at, *refs):
    a_ins, b_ins, a_outs, b_outs = refs[0:4], refs[4:8], refs[8:12], refs[12:16]
    x, y = at[0], at[1]
    message = split_vectors(sum_pairs(*[join_vectors(ref[64:80, :]) for ref in a_ins]))
    for hop, out in zip((0,) + HOPS, a_outs):
        rows = pl.ds(pl.multiple_of(lax.rem(y + hop, 4) * 16, 16), 16)
        out[0:16, :] = sum_pairs(*[ref[rows, :] for ref in a_ins]).astype(BF16)
        out[16:32, :] = message
    for hop, out in zip((0,) + HOPS, b_outs):
        rows = pl.ds(pl.multiple_of(lax.rem(x + hop, 4) * 16, 16), 16)
        out[...] = sum_pairs(*[ref[rows, :] for ref in b_ins]).astype(BF16)


def third_kernel(*refs):
    a_ins, b_ins, out = refs[0:4], refs[4:8], refs[8]
    out[0:16, :] = sum_pairs(*[ref[0:16, :] for ref in a_ins]).astype(BF16)
    out[16:32, :] = sum_pairs(*[ref[...] for ref in b_ins]).astype(BF16)
    out[32:48, :] = split_vectors(sum_pairs(*[join_vectors(ref[16:32, :]) for ref in a_ins]))


def last_kernel(*refs):
    ins, (a_out, b_out, vectors) = refs[0:4], refs[4:7]
    a_out[...] = sum_pairs(*[ref[0:16, :] for ref in ins]).astype(BF16)
    b_out[...] = sum_pairs(*[ref[16:32, :] for ref in ins]).astype(BF16)
    vectors[...] = sum_pairs(*[join_vectors(ref[32:48, :]) for ref in ins])


def lines_kernel(at, *refs):
    a_ins, b_ins, a_out, b_out = refs[0:4], refs[4:8], refs[8], refs[9]
    x, y = at[0], at[1]
    for hop, mine, other in zip((0,) + HOPS, a_ins, b_ins):
        a_out[pl.ds(pl.multiple_of(lax.rem(y + 4 - hop, 4) * 16, 16), 16), :] = mine[...]
        b_out[pl.ds(pl.multiple_of(lax.rem(x + 4 - hop, 4) * 16, 16), 16), :] = other[...]


def step_of(grad, first, second, param, decay):
    first_new = beta_one * first + (1.0 - beta_one) * grad
    second_new = beta_two * second + (1.0 - beta_two) * grad * grad
    update = first_new / (jnp.sqrt(second_new) + adam_eps) + decay * param
    return first_new, second_new, update


def lamb_kernel(at, *refs):
    pieces, refs = refs[0:16], refs[16:]
    vec_grad, state, master, first, second, vectors, vec_first, vec_second = refs[0:8]
    weight_out, master_out, first_out, second_out = refs[8:12]
    vec_out, vec_first_out, vec_second_out = refs[12:15]
    grad, update = refs[15:17]
    x, y, core, z = at[0], at[1], at[2], at[3]

    for which in range(2):
        base = lax.rem(core + which, 2) * 512
        for n, hop in enumerate((0,) + HOPS):
            a_at = base + lax.rem(x + 4 - hop, 4) * 64
            b_at = base + 256 + lax.rem(y + 4 - hop, 4) * 64
            grad[pl.ds(pl.multiple_of(a_at, 64), 64), :] = pieces[which * 8 + n][...]
            grad[pl.ds(pl.multiple_of(b_at, 64), 64), :] = pieces[which * 8 + 4 + n][...]

    def fold(value):
        return value[0:8] + value[8:16]

    zero = jnp.zeros((8, D), F32)

    def square(i, total):
        g = grad[pl.ds(pl.multiple_of(i * 16, 16), 16), :].astype(F32)
        return total + fold(g * g)

    grad_sq = jnp.sum(lax.fori_loop(0, D // 16, square, zero, unroll=4))
    grad_vectors = vec_grad[0:3, :]
    total = jnp.sqrt(
        jnp.full((1, 1), grad_sq + jnp.sum(grad_vectors * grad_vectors), F32)
    )
    factor = 1.0 / jnp.maximum(1.0, total / max_norm)

    def full(i, totals):
        rows = pl.ds(pl.multiple_of(i * 16, 16), 16)
        g = grad[rows, :].astype(F32) * factor
        w = state[0, rows, :].astype(F32)
        _, _, u = step_of(
            g, state[1, rows, :].astype(F32), state[2, rows, :].astype(F32), w, decay_rate
        )
        update[rows, :] = u
        return totals[0] + fold(u * u), totals[1] + fold(w * w)

    update_sq, weight_sq = lax.fori_loop(0, D // 16, full, (zero, zero), unroll=2)
    update_sq = jnp.full((1, 1), jnp.sum(update_sq), F32)
    weight_sq = jnp.full((1, 1), jnp.sum(weight_sq), F32)
    rate = learn_rate * (jnp.sqrt(weight_sq) / jnp.sqrt(update_sq + 1e-06))

    def finish(i, carry):
        rows = pl.ds(pl.multiple_of(i * 16, 16), 16)
        weight_out[rows, :] = (state[0, rows, :].astype(F32) - rate * update[rows, :]).astype(BF16)
        return carry

    lax.fori_loop(0, D // 16, finish, 0, unroll=2)

    def shard(i, carry):
        rows = pl.ds(pl.multiple_of(i * 16, 16), 16)
        g = grad[pl.ds(pl.multiple_of(z * 256 + i * 16, 16), 16), :].astype(F32) * factor
        w = master[rows, :]
        first_new, second_new, u = step_of(g, first[rows, :], second[rows, :], w, decay_rate)
        first_out[rows, :] = first_new
        second_out[rows, :] = second_new
        master_out[rows, :] = w - rate * u
        return carry

    lax.fori_loop(0, 256 // 16, shard, 0, unroll=2)

    params = vectors[...]
    first_new, second_new, u = step_of(
        grad_vectors * factor, vec_first[...], vec_second[...], params, 0.0
    )
    trust = jnp.sqrt(jnp.sum(params * params, axis=1, keepdims=True)) / jnp.sqrt(
        jnp.sum(u * u, axis=1, keepdims=True) + 1e-06
    )
    vec_out[...] = params - learn_rate * trust * u
    vec_first_out[...] = first_new
    vec_second_out[...] = second_new


def on_device(
    context,
    residual_in,
    cotangent,
    weight,
    master,
    moment_first,
    moment_second,
    out_bias,
    ln_gain,
    ln_shift,
    vector_first,
    vector_second,
):
    rep, z = lax.axis_index("rep"), lax.axis_index("opt")
    at = jnp.stack([rep // 8, (rep // 2) % 4, rep % 2, z]).astype(jnp.int32)

    half_state = pack_state(at, master, moment_first, moment_second)
    near = [shift(half_state, z=hop) for hop in HOPS]

    d_resid, send, keep = backward(
        at,
        context,
        residual_in,
        cotangent,
        weight,
        out_bias.reshape(1, D),
        ln_gain.reshape(1, D),
    )
    got = shift(send, c=1)
    d_context = context_grad(d_resid, weight)

    outs = call(core_kernel, [((80, D), BF16)] * 4 + [((64, D), BF16)] * 4, (at, keep, got))
    a, b = outs[0:4], outs[4:8]
    a = [a[0]] + [shift(v, x=hop) for hop, v in zip(HOPS, a[1:])]
    b = [b[0]] + [shift(v, y=hop) for hop, v in zip(HOPS, b[1:])]

    outs = call(second_kernel, [((32, D), BF16)] * 4 + [((16, D), BF16)] * 4, (at, *a, *b))
    a, b = outs[0:4], outs[4:8]
    a = [a[0]] + [shift(v, y=hop) for hop, v in zip(HOPS, a[1:])]
    b = [b[0]] + [shift(v, x=hop) for hop, v in zip(HOPS, b[1:])]

    (message,) = call(third_kernel, [((48, D), BF16)], (*a, *b), specs=[VMEM] * 8)
    parts = [message] + [shift(message, z=hop) for hop in HOPS]
    a_own, b_own, vec_grad = call(
        last_kernel,
        [((16, D), BF16), ((16, D), BF16), ((8, D), F32)],
        parts,
        specs=[VMEM] * 4,
    )

    a = [a_own] + [shift(a_own, y=hop) for hop in HOPS]
    b = [b_own] + [shift(b_own, x=hop) for hop in HOPS]
    a_line, b_line = call(lines_kernel, [((64, D), BF16)] * 2, (at, *a, *b))
    a = [a_line] + [shift(a_line, x=hop) for hop in HOPS]
    b = [b_line] + [shift(b_line, y=hop) for hop in HOPS]
    pieces = a + b
    pieces = pieces + [shift(v, c=1) for v in pieces]

    other = [shift(v, c=1) for v in near]
    (state,) = call(
        state_kernel,
        [((3, D, D), BF16)],
        (at, master, moment_first, moment_second, *near, *other),
        limit=32,
    )

    vectors = jnp.stack([out_bias, ln_gain, ln_shift])
    shard = ((256, D), F32)
    rows = ((3, D), F32)
    outs = call(
        lamb_kernel,
        [((D, D), BF16), shard, shard, shard, rows, rows, rows],
        (
            at,
            *pieces,
            vec_grad,
            state,
            master,
            moment_first,
            moment_second,
            vectors,
            vector_first,
            vector_second,
        ),
        scratch=[pltpu.VMEM((D, D), BF16), pltpu.VMEM((D, D), F32)],
        limit=40,
    )
    return (d_context, d_resid, *outs)


def solution(mesh):
    tokens, copied, shard = P(("rep", "opt"), None), P(), P("opt", None)
    return jax.shard_map(
        on_device,
        mesh=mesh,
        in_specs=(tokens,) * 3 + (copied,) + (shard,) * 3 + (copied,) * 5,
        out_specs=(tokens, tokens, copied) + (shard,) * 3 + (copied,) * 3,
        check_vma=False,
    )
```

time: 249 us -> 180 us (0.72)
  blocking collectives: 81.3 us -> 0 us
  starting transfers between devices: 0.12 us -> 62.9 us
  Pallas kernels: 0 us -> 41.5 us
  waiting for transfers between devices: 85.6 us -> 59.9 us
  other arithmetic: 18 us -> 0.09 us
  local copies, waits for them, and re-layouts: 31.4 us -> 14.2 us
  between operations: 16.6 us -> 0.97 us
  matrix products: 14.7 us -> 0 us
    psum x3 -> x0, blocking collectives: 81.3 us -> none  [the longest x1 65.3 us: on_device(): lax.psum((jnp.sum(d_pre, axis=0), jnp.sum(grad_out * normed, axis=0), jnp...]
    ppermute x0 -> x42, starting transfers between devices: none -> 62.9 us  [shift(): return lax.ppermute(value, AXES, pairs)]
    ppermute x0 -> x42, waiting for transfers between devices: none -> 59.9 us  [shift(): return lax.ppermute(value, AXES, pairs)]
    pallas_call x0 -> x10, Pallas kernels: none -> 41.5 us  [the longest x9 40 us: call(): pl.pallas_call(kernel, out_shape=[jax.ShapeDtypeStruct(shape, dtype) for...]
    psum x1 -> x0, waiting for transfers between devices: 34.3 us -> none  [on_device(): grad_weight = lax.psum(group_part, 'rep').astype(jnp.float32)]
    reduce_scatter x1 -> x0, waiting for transfers between devices: 33.3 us -> none  [on_device(): lax.psum_scatter(lax.dot_general(context, d_resid, (((0,), (0,)), ((), ()...]
    all_gather x1 -> x0, waiting for transfers between devices: 18 us -> none  [on_device(): lax.all_gather(new_master.astype(jnp.bfloat16), 'opt', axis=0, tiled=True)]
    unnamed x28 -> x82, local copies, waits for them, and re-layouts: 31.4 us -> 14.2 us
  transfers between devices with their start and end apart: 3 -> 42, of which waited for: 3 -> 18; matrix products, arithmetic and copies ran while one was open for 10% -> 0% of each run, Pallas kernels for 0% -> 10%
where the time goes in v1:
time: 180 us
  starting transfers between devices  62.9 us (35%)
  waiting for transfers between devices  59.9 us (33%)
  Pallas kernels  41.5 us (23%)
  local copies, waits for them, and re-layouts  14.2 us (8%)
    ppermute x42, starting transfers between devices, shift(): return lax.ppermute(value, AXES, pairs)  62.9 us
    ppermute x42, waiting for transfers between devices, shift(): return lax.ppermute(value, AXES, pairs)  59.9 us
    pallas_call x9, Pallas kernels, call(): pl.pallas_call(kernel, out_shape=[jax.ShapeDtypeStruct(shape, dtype) for...  40 us
    unnamed x82, local copies, waits for them, and re-layouts  14.2 us
  transfers between devices with their start and end apart: 42, of which 18 were waited for; matrix products, arithmetic and copies ran while one was open for 0% of the time, Pallas kernels for 10%

profile of v1, /device:TPU:1, one launch (start us, length us, event | category | flops | bytes accessed | tf_op | source)
XLA Modules:
  0.0 179.5 jit_solution(16204265062230244000)
XLA Ops:
  2.1 1.6 copy-done.15
  3.7 1.6 copy-done.16
  5.3 1.6 copy-done.17
  6.9 1.6 copy-done.18
  8.5 13.9 %shard_map.187 = (bf16[1024,1024]{1,0:T(8,128)(2,1)}, bf16[528,1024]{1,0:T(8,128)(2,1)S(1)}, bf16[528,1024]{1,0:T(8,128)(2,1)S(1)}) custom-call(s32[4]{0:T(128)S(1)} %pad_add_fusion.at, bf16[1024,1024]{1,0:T(8,128)(2,1)S(1)} %copy-done.15, bf16[1024,1024]{1,0:T(8,128)(2,1)S(1)} %copy-done.16, bf16[1024,1024]{1,0:T(8,128)(2,1)S(1)} %copy-done.17, ...), custom_call_target="tpu_custom_call" | custom-call | flops 4294967296 | bytes 14680064 | tf_op jit(solution)/shard_map/pallas_call | solution.py:42
  23.4 1.4 collective-permute-start
  24.8 1.5 shard_map.194
  26.3 3.7 %collective-permute-start.38 = (bf16[3,128,1024]{2,1,0:T(8,128)(2,1)}, bf16[3,128,1024]{2,1,0:T(8,128)(2,1)S(1)}, u32[]{:S(2)}, u32[]{:S(2)}) collective-permute-start(bf16[3,128,1024]{2,1,0:T(8,128)(2,1)} %shard_map.194), channel_id=1, source_target_pairs={{0,2},{1,3},{2,0},{3,1},{4,6},{5,7},{6,4},{7,5},{8,10},{9,11},{10,... | collective-permute-start | bytes 2359304 | tf_op jit(solution)/shard_map/ppermute | solution.py:38
  32.5 2.7 %shard_map.189 = (bf16[80,1024]{1,0:T(8,128)(2,1)}, bf16[80,1024]{1,0:T(8,128)(2,1)}, bf16[80,1024]{1,0:T(8,128)(2,1)}, bf16[80,1024]{1,0:T(8,128)(2,1)}, bf16[6...) custom-call(s32[4]{0:T(128)} %copy-done.7, ...), custom_call_target="tpu_custom_call" | custom-call | tf_op jit(solution)/shard_map/pallas_call | solution.py:42
  35.1 1.3 collective-permute-start.4
  37.7 10.5 %collective-permute-done.38.rest_2_ = bf16[3,128,1024]{2,1,0:T(8,128)(2,1)S(1)} collective-permute-done((bf16[3,128,1024]{2,1,0:T(8,128)(2,1)}, bf16[3,128,1024]{2,1,0:T(8,128)(2,1)S(1)}, u32[]{:S(2)}, u32[]{:S(2)}) %collective-permute-start.38) | collective-permute-done | bytes 786464 | tf_op jit(solution)/shard_map/ppermute | solution.py:38
  48.2 2.7 %collective-permute-start.5 = (bf16[64,1024]{1,0:T(8,128)(2,1)}, bf16[64,1024]{1,0:T(8,128)(2,1)S(1)}, u32[]{:S(2)}, u32[]{:S(2)}) collective-permute-start(bf16[64,1024]{1,0:T(8,128)(2,1)} %get-tuple-element.49), channel_id=1, source_target_pairs={{0,24},{1,25},{2,26},{3,27},{4,28},{5,29},{6,30},{7,31},{8,0},{9,1... | collective-permute-start | bytes 393224 | tf_op jit(solution)/shard_map/ppermute | solution.py:38
  50.9 14.8 %collective-permute-done.37.rest_1_ = bf16[3,128,1024]{2,1,0:T(8,128)(2,1)} collective-permute-done((bf16[3,128,1024]{2,1,0:T(8,128)(2,1)}, bf16[3,128,1024]{2,1,0:T(8,128)(2,1)}, u32[]{:S(2)}, u32[]{:S(2)}) %collective-permute-start.37) | collective-permute-done | bytes 786464 | tf_op jit(solution)/shard_map/ppermute | solution.py:38
  66.5 3.0 %collective-permute-start.6 = (bf16[64,1024]{1,0:T(8,128)(2,1)}, bf16[64,1024]{1,0:T(8,128)(2,1)S(1)}, u32[]{:S(2)}, u32[]{:S(2)}) collective-permute-start(bf16[64,1024]{1,0:T(8,128)(2,1)} %get-tuple-element.50), channel_id=1, source_target_pairs={{0,16},{1,17},{2,18},{3,19},{4,20},{5,21},{6,22},{7,23},{8,24},{9,... | collective-permute-start | bytes 393224 | tf_op jit(solution)/shard_map/ppermute | solution.py:38
  70.2 2.8 %collective-permute-done.6.refs_7_ = bf16[64,1024]{1,0:T(8,128)(2,1)S(1)} collective-permute-done((bf16[64,1024]{1,0:T(8,128)(2,1)}, bf16[64,1024]{1,0:T(8,128)(2,1)S(1)}, u32[]{:S(2)}, u32[]{:S(2)}) %collective-permute-start.6) | collective-permute-done | bytes 131104 | tf_op jit(solution)/shard_map/ppermute | solution.py:38
  72.9 2.5 %collective-permute-start.2 = (bf16[80,1024]{1,0:T(8,128)(2,1)}, bf16[80,1024]{1,0:T(8,128)(2,1)}, u32[]{:S(2)}, u32[]{:S(2)}) collective-permute-start(bf16[80,1024]{1,0:T(8,128)(2,1)} %get-tuple-element.45), channel_id=1, source_target_pairs={{0,96},{1,97},{2,98},{3,99},{4,100},{5,101},{6,102},{7,103},{8,104... | collective-permute-start | bytes 491528 | tf_op jit(solution)/shard_map/ppermute | solution.py:38
  76.0 3.2 %collective-permute-done.2.refs_2_ = bf16[80,1024]{1,0:T(8,128)(2,1)} collective-permute-done((bf16[80,1024]{1,0:T(8,128)(2,1)}, bf16[80,1024]{1,0:T(8,128)(2,1)}, u32[]{:S(2)}, u32[]{:S(2)}) %collective-permute-start.2) | collective-permute-done | bytes 163872 | tf_op jit(solution)/shard_map/ppermute | solution.py:38
  79.2 2.3 %collective-permute-done.3.refs_3_ = bf16[80,1024]{1,0:T(8,128)(2,1)} collective-permute-done((bf16[80,1024]{1,0:T(8,128)(2,1)}, bf16[80,1024]{1,0:T(8,128)(2,1)}, u32[]{:S(2)}, u32[]{:S(2)}) %collective-permute-start.3) | collective-permute-done | bytes 163872 | tf_op jit(solution)/shard_map/ppermute | solution.py:38
  81.5 2.1 %shard_map.190 = (bf16[32,1024]{1,0:T(8,128)(2,1)}, bf16[32,1024]{1,0:T(8,128)(2,1)}, bf16[32,1024]{1,0:T(8,128)(2,1)}, bf16[32,1024]{1,0:T(8,128)(2,1)}, bf16[1...) custom-call(s32[4]{0:T(128)} %copy-done.7, ...), custom_call_target="tpu_custom_call" | custom-call | tf_op jit(solution)/shard_map/pallas_call | solution.py:42
  83.6 1.6 collective-permute-start.10
  86.4 1.5 collective-permute-done.10.refs_5_
  87.9 1.3 collective-permute-start.7
  90.4 3.3 %collective-permute-done.12.refs_7_ = bf16[16,1024]{1,0:T(8,128)(2,1)S(1)} collective-permute-done((bf16[16,1024]{1,0:T(8,128)(2,1)}, bf16[16,1024]{1,0:T(8,128)(2,1)S(1)}, u32[]{:S(2)}, u32[]{:S(2)}) %collective-permute-start.12) | collective-permute-done | bytes 32800 | tf_op jit(solution)/shard_map/ppermute | solution.py:38
  93.7 1.8 %collective-permute-start.8 = (bf16[32,1024]{1,0:T(8,128)(2,1)}, bf16[32,1024]{1,0:T(8,128)(2,1)S(1)}, u32[]{:S(2)}, u32[]{:S(2)}) collective-permute-start(bf16[32,1024]{1,0:T(8,128)(2,1)} %get-tuple-element.53), channel_id=1, source_target_pairs={{0,24},{1,25},{2,26},{3,27},{4,28},{5,29},{6,30},{7,31},{8,0},{9,1... | collective-permute-start | bytes 196616 | tf_op jit(solution)/shard_map/ppermute | solution.py:38
  97.2 3.2 %collective-permute-done.9.refs_3_ = bf16[32,1024]{1,0:T(8,128)(2,1)S(1)} collective-permute-done((bf16[32,1024]{1,0:T(8,128)(2,1)}, bf16[32,1024]{1,0:T(8,128)(2,1)S(1)}, u32[]{:S(2)}, u32[]{:S(2)}) %collective-permute-start.9) | collective-permute-done | bytes 65568 | tf_op jit(solution)/shard_map/ppermute | solution.py:38
  101.0 1.7 shard_map.191.refs_0_
  102.6 3.5 %collective-permute-start.15 = (bf16[48,1024]{1,0:T(8,128)(2,1)}, bf16[48,1024]{1,0:T(8,128)(2,1)S(1)}, u32[]{:S(2)}, u32[]{:S(2)}) collective-permute-start(bf16[48,1024]{1,0:T(8,128)(2,1)} %shard_map.191.refs_0_), channel_id=1, source_target_pairs={{0,2},{1,3},{2,0},{3,1},{4,6},{5,7},{6,4},{7,5},{8,10},{9,11},{10,... | collective-permute-start | bytes 294920 | tf_op jit(solution)/shard_map/ppermute | solution.py:38
  108.4 1.6 collective-permute-start.13
  110.0 3.4 %collective-permute-done.13.refs_1_ = bf16[48,1024]{1,0:T(8,128)(2,1)} collective-permute-done((bf16[48,1024]{1,0:T(8,128)(2,1)}, bf16[48,1024]{1,0:T(8,128)(2,1)}, u32[]{:S(2)}, u32[]{:S(2)}) %collective-permute-start.13) | collective-permute-done | bytes 98336 | tf_op jit(solution)/shard_map/ppermute | solution.py:38
  113.4 1.7 shard_map.192
  115.1 1.6 collective-permute-start.18
  117.4 2.2 %collective-permute-done.18.refs_3_ = bf16[16,1024]{1,0:T(8,128)(2,1)S(1)} collective-permute-done((bf16[16,1024]{1,0:T(8,128)(2,1)}, bf16[16,1024]{1,0:T(8,128)(2,1)S(1)}, u32[]{:S(2)}, u32[]{:S(2)}) %collective-permute-start.18) | collective-permute-done | bytes 32800 | tf_op jit(solution)/shard_map/ppermute | solution.py:38
  119.6 2.6 %collective-permute-start.21 = (bf16[16,1024]{1,0:T(8,128)(2,1)}, bf16[16,1024]{1,0:T(8,128)(2,1)S(1)}, u32[]{:S(2)}, u32[]{:S(2)}) collective-permute-start(bf16[16,1024]{1,0:T(8,128)(2,1)} %get-tuple-element.60.refs_4_), channel_id=1, source_target_pairs={{0,64},{1,65},{2,66},{3,67},{4,68},{5,69},{6,70},{7,71},{8,72},{9,... | collective-permute-start | bytes 98312 | tf_op jit(solution)/shard_map/ppermute | solution.py:38
  122.2 1.5 collective-permute-done.16.refs_1_
  123.7 2.7 %collective-permute-start.20 = (bf16[16,1024]{1,0:T(8,128)(2,1)}, bf16[16,1024]{1,0:T(8,128)(2,1)S(1)}, u32[]{:S(2)}, u32[]{:S(2)}) collective-permute-start(bf16[16,1024]{1,0:T(8,128)(2,1)} %get-tuple-element.60.refs_4_), channel_id=1, source_target_pairs={{0,96},{1,97},{2,98},{3,99},{4,100},{5,101},{6,102},{7,103},{8,104... | collective-permute-start | bytes 98312 | tf_op jit(solution)/shard_map/ppermute | solution.py:38
  126.4 1.3 collective-permute-done.20.refs_6_
  127.7 2.8 %collective-permute-done.19.refs_5_ = bf16[16,1024]{1,0:T(8,128)(2,1)S(1)} collective-permute-done((bf16[16,1024]{1,0:T(8,128)(2,1)}, bf16[16,1024]{1,0:T(8,128)(2,1)S(1)}, u32[]{:S(2)}, u32[]{:S(2)}) %collective-permute-start.19) | collective-permute-done | bytes 32800 | tf_op jit(solution)/shard_map/ppermute | solution.py:38
  131.2 1.6 shard_map.193
  132.8 11.8 %collective-permute-start.28 = (bf16[64,1024]{1,0:T(8,128)(2,1)}, bf16[64,1024]{1,0:T(8,128)(2,1)S(1)}, u32[]{:S(2)}, u32[]{:S(2)}) collective-permute-start(bf16[64,1024]{1,0:T(8,128)(2,1)} %get-tuple-element.61.refs_0_), channel_id=1, source_target_pairs={{0,4},{1,5},{2,6},{3,7},{4,0},{5,1},{6,2},{7,3},{8,12},{9,13},{10,... | collective-permute-start | bytes 393224 | tf_op jit(solution)/shard_map/ppermute | solution.py:38
  148.1 3.3 %collective-permute-done.24.refs_3_ = bf16[64,1024]{1,0:T(8,128)(2,1)S(1)} collective-permute-done((bf16[64,1024]{1,0:T(8,128)(2,1)}, bf16[64,1024]{1,0:T(8,128)(2,1)S(1)}, u32[]{:S(2)}, u32[]{:S(2)}) %collective-permute-start.24) | collective-permute-done | bytes 131104 | tf_op jit(solution)/shard_map/ppermute | solution.py:38
  152.9 1.7 collective-permute-done.22.refs_1_
  155.6 2.3 %collective-permute-start.35 = (bf16[64,1024]{1,0:T(8,128)(2,1)S(1)}, bf16[64,1024]{1,0:T(8,128)(2,1)S(1)}, u32[]{:S(2)}, u32[]{:S(2)}) collective-permute-start(bf16[64,1024]{1,0:T(8,128)(2,1)S(1)} %collective-permute-done.27.refs_7_), channel_id=1, source_target_pairs={{0,4},{1,5},{2,6},{3,7},{4,0},{5,1},{6,2},{7,3},{8,12},{9,13},{10,... | collective-permute-start | bytes 393224 | tf_op jit(solution)/shard_map/ppermute | solution.py:38
  157.9 1.9 %collective-permute-start.34 = (bf16[64,1024]{1,0:T(8,128)(2,1)S(1)}, bf16[64,1024]{1,0:T(8,128)(2,1)S(1)}, u32[]{:S(2)}, u32[]{:S(2)}) collective-permute-start(bf16[64,1024]{1,0:T(8,128)(2,1)S(1)} %collective-permute-done.26.refs_6_), channel_id=1, source_target_pairs={{0,4},{1,5},{2,6},{3,7},{4,0},{5,1},{6,2},{7,3},{8,12},{9,13},{10,... | collective-permute-start | bytes 393224 | tf_op jit(solution)/shard_map/ppermute | solution.py:38
  159.8 1.6 copy-done.19
  161.4 1.6 copy-done.20
  163.0 3.9 %shard_map.188 = bf16[1024,1024]{1,0:T(8,128)(2,1)} custom-call(bf16[1024,1024]{1,0:T(8,128)(2,1)S(1)} %copy-done.20, bf16[1024,1024]{1,0:T(8,128)(2,1)S(1)} %copy-done.19), custom_call_target="tpu_custom_call" | custom-call | flops 2147483648 | bytes 6291456 | tf_op jit(solution)/shard_map/pallas_call | solution.py:42
  166.9 2.6 %shard_map.195.refs_17_ = bf16[3,1024,1024]{2,1,0:T(8,128)(2,1)S(1)} custom-call(s32[4]{0:T(128)S(1)} %copy-done.8, f32[256,1024]{1,0:T(8,128)S(1)} %copy-done, f32[256,1024]{1,0:T(8,128)S(1)} %copy-done.1, f32[256,1024]{1,0:T(8,128)S(1)} %copy-done.2, bf16[3,128,1024]{2,1,0:T(8,128)(2,1)} %collective-permute-done.36.rest_0_, ...), custom_call_target="tpu_custom_call" | custom-call | tf_op jit(solution)/shard_map/pallas_call | solution.py:42
  169.7 9.8 %shard_map.196 = (bf16[1024,1024]{1,0:T(8,128)(2,1)}, f32[256,1024]{1,0:T(8,128)}, f32[256,1024]{1,0:T(8,128)}, f32[256,1024]{1,0:T(8,128)}, f32[3,1024]{1,0:T(4...) custom-call(s32[4]{0:T(128)S(1)} %copy-done.8, bf16[64,1024]{1,0:T(8,128)(2,1)S(1)} %copy-done.4, ...), custom_call_target="tpu_custom_call" | custom-call | tf_op jit(solution)/shard_map/pallas_call | solution.py:42
  (130 shorter events, 22.5 us)
Async XLA Ops:
  0.8 24.1 %copy-start.7 = (s32[4]{0:T(128)}, s32[4]{0:T(128)S(1)}, u32[]{:S(2)}) copy-start(s32[4]{0:T(128)S(1)} %pad_add_fusion.at) | copy-start | bytes 52
  8.5 16.3 %copy-start = (f32[256,1024]{1,0:T(8,128)S(1)}, f32[256,1024]{1,0:T(8,128)}, u32[]{:S(2)}) copy-start(f32[256,1024]{1,0:T(8,128)} %refs_18_.1) | copy-start | bytes 3145732
  8.5 16.3 %copy-start.1 = (f32[256,1024]{1,0:T(8,128)S(1)}, f32[256,1024]{1,0:T(8,128)}, u32[]{:S(2)}) copy-start(f32[256,1024]{1,0:T(8,128)} %refs_19_.1) | copy-start | bytes 3145732
  8.5 16.3 %copy-start.2 = (f32[256,1024]{1,0:T(8,128)S(1)}, f32[256,1024]{1,0:T(8,128)}, u32[]{:S(2)}) copy-start(f32[256,1024]{1,0:T(8,128)} %refs_20_.1) | copy-start | bytes 3145732
  23.4 8.1 %collective-permute-start = (bf16[528,1024]{1,0:T(8,128)(2,1)S(1)}, bf16[528,1024]{1,0:T(8,128)(2,1)S(1)}, u32[]{:S(2)}, u32[]{:S(2)}) collective-permute-start(bf16[528,1024]{1,0:T(8,128)(2,1)S(1)} %get-tuple-element.42), channel_id=1, source_target_pairs={{0,4},{1,5},{2,6},{3,7},{4,0},{5,1},{6,2},{7,3},{8,12},{9,13},{10,... | collective-permute-start | bytes 3244040 | tf_op jit(solution)/shard_map/ppermute | solution.py:38
  26.3 21.8 %collective-permute-start.38 = (bf16[3,128,1024]{2,1,0:T(8,128)(2,1)}, bf16[3,128,1024]{2,1,0:T(8,128)(2,1)S(1)}, u32[]{:S(2)}, u32[]{:S(2)}) collective-permute-start(bf16[3,128,1024]{2,1,0:T(8,128)(2,1)} %shard_map.194), channel_id=1, source_target_pairs={{0,2},{1,3},{2,0},{3,1},{4,6},{5,7},{6,4},{7,5},{8,10},{9,11},{10,... | collective-permute-start | bytes 2359304 | tf_op jit(solution)/shard_map/ppermute | solution.py:38
  30.0 35.6 %collective-permute-start.37 = (bf16[3,128,1024]{2,1,0:T(8,128)(2,1)}, bf16[3,128,1024]{2,1,0:T(8,128)(2,1)}, u32[]{:S(2)}, u32[]{:S(2)}) collective-permute-start(bf16[3,128,1024]{2,1,0:T(8,128)(2,1)} %shard_map.194), channel_id=1, source_target_pairs={{0,3},{1,0},{2,1},{3,2},{4,7},{5,4},{6,5},{7,6},{8,11},{9,8},{10,9... | collective-permute-start | bytes 2359304 | tf_op jit(solution)/shard_map/ppermute | solution.py:38
  30.4 36.0 %collective-permute-start.36 = (bf16[3,128,1024]{2,1,0:T(8,128)(2,1)}, bf16[3,128,1024]{2,1,0:T(8,128)(2,1)}, u32[]{:S(2)}, u32[]{:S(2)}) collective-permute-start(bf16[3,128,1024]{2,1,0:T(8,128)(2,1)} %shard_map.194), channel_id=1, source_target_pairs={{0,1},{1,2},{2,3},{3,0},{4,5},{5,6},{6,7},{7,4},{8,9},{9,10},{10,1... | collective-permute-start | bytes 2359304 | tf_op jit(solution)/shard_map/ppermute | solution.py:38
  35.1 31.3 %collective-permute-start.4 = (bf16[64,1024]{1,0:T(8,128)(2,1)}, bf16[64,1024]{1,0:T(8,128)(2,1)S(1)}, u32[]{:S(2)}, u32[]{:S(2)}) collective-permute-start(bf16[64,1024]{1,0:T(8,128)(2,1)} %get-tuple-element.48), channel_id=1, source_target_pairs={{0,8},{1,9},{2,10},{3,11},{4,12},{5,13},{6,14},{7,15},{8,16},{9,17... | collective-permute-start | bytes 393224 | tf_op jit(solution)/shard_map/ppermute | solution.py:38
  36.4 39.0 %collective-permute-start.1 = (bf16[80,1024]{1,0:T(8,128)(2,1)}, bf16[80,1024]{1,0:T(8,128)(2,1)S(1)}, u32[]{:S(2)}, u32[]{:S(2)}) collective-permute-start(bf16[80,1024]{1,0:T(8,128)(2,1)} %get-tuple-element.44), channel_id=1, source_target_pairs={{0,32},{1,33},{2,34},{3,35},{4,36},{5,37},{6,38},{7,39},{8,40},{9,... | collective-permute-start | bytes 491528 | tf_op jit(solution)/shard_map/ppermute | solution.py:38
  48.2 21.3 %collective-permute-start.5 = (bf16[64,1024]{1,0:T(8,128)(2,1)}, bf16[64,1024]{1,0:T(8,128)(2,1)S(1)}, u32[]{:S(2)}, u32[]{:S(2)}) collective-permute-start(bf16[64,1024]{1,0:T(8,128)(2,1)} %get-tuple-element.49), channel_id=1, source_target_pairs={{0,24},{1,25},{2,26},{3,27},{4,28},{5,29},{6,30},{7,31},{8,0},{9,1... | collective-permute-start | bytes 393224 | tf_op jit(solution)/shard_map/ppermute | solution.py:38
  65.7 79.0 %collective-permute-start.41 = (bf16[3,128,1024]{2,1,0:T(8,128)(2,1)S(1)}, bf16[3,128,1024]{2,1,0:T(8,128)(2,1)}, u32[]{:S(2)}, u32[]{:S(2)}) collective-permute-start(bf16[3,128,1024]{2,1,0:T(8,128)(2,1)S(1)} %collective-permute-done.38.rest_2_), channel_id=1, source_target_pairs={{0,4},{1,5},{2,6},{3,7},{4,0},{5,1},{6,2},{7,3},{8,12},{9,13},{10,... | collective-permute-start | bytes 2359304 | tf_op jit(solution)/shard_map/ppermute | solution.py:38
  66.5 79.1 %collective-permute-start.40 = (bf16[3,128,1024]{2,1,0:T(8,128)(2,1)}, bf16[3,128,1024]{2,1,0:T(8,128)(2,1)}, u32[]{:S(2)}, u32[]{:S(2)}) collective-permute-start(bf16[3,128,1024]{2,1,0:T(8,128)(2,1)} %collective-permute-done.37.rest_1_), channel_id=1, source_target_pairs={{0,4},{1,5},{2,6},{3,7},{4,0},{5,1},{6,2},{7,3},{8,12},{9,13},{10,... | collective-permute-start | bytes 2359304 | tf_op jit(solution)/shard_map/ppermute | solution.py:38
  66.5 6.5 %collective-permute-start.6 = (bf16[64,1024]{1,0:T(8,128)(2,1)}, bf16[64,1024]{1,0:T(8,128)(2,1)S(1)}, u32[]{:S(2)}, u32[]{:S(2)}) collective-permute-start(bf16[64,1024]{1,0:T(8,128)(2,1)} %get-tuple-element.50), channel_id=1, source_target_pairs={{0,16},{1,17},{2,18},{3,19},{4,20},{5,21},{6,22},{7,23},{8,24},{9,... | collective-permute-start | bytes 393224 | tf_op jit(solution)/shard_map/ppermute | solution.py:38
  69.5 76.6 %collective-permute-start.39 = (bf16[3,128,1024]{2,1,0:T(8,128)(2,1)}, bf16[3,128,1024]{2,1,0:T(8,128)(2,1)}, u32[]{:S(2)}, u32[]{:S(2)}) collective-permute-start(bf16[3,128,1024]{2,1,0:T(8,128)(2,1)} %collective-permute-done.36.rest_0_), channel_id=1, source_target_pairs={{0,4},{1,5},{2,6},{3,7},{4,0},{5,1},{6,2},{7,3},{8,12},{9,13},{10,... | collective-permute-start | bytes 2359304 | tf_op jit(solution)/shard_map/ppermute | solution.py:38
  72.9 6.3 %collective-permute-start.2 = (bf16[80,1024]{1,0:T(8,128)(2,1)}, bf16[80,1024]{1,0:T(8,128)(2,1)}, u32[]{:S(2)}, u32[]{:S(2)}) collective-permute-start(bf16[80,1024]{1,0:T(8,128)(2,1)} %get-tuple-element.45), channel_id=1, source_target_pairs={{0,96},{1,97},{2,98},{3,99},{4,100},{5,101},{6,102},{7,103},{8,104... | collective-permute-start | bytes 491528 | tf_op jit(solution)/shard_map/ppermute | solution.py:38
  75.4 6.1 %collective-permute-start.3 = (bf16[80,1024]{1,0:T(8,128)(2,1)}, bf16[80,1024]{1,0:T(8,128)(2,1)}, u32[]{:S(2)}, u32[]{:S(2)}) collective-permute-start(bf16[80,1024]{1,0:T(8,128)(2,1)} %get-tuple-element.46), channel_id=1, source_target_pairs={{0,64},{1,65},{2,66},{3,67},{4,68},{5,69},{6,70},{7,71},{8,72},{9,... | collective-permute-start | bytes 491528 | tf_op jit(solution)/shard_map/ppermute | solution.py:38
  83.6 4.2 %collective-permute-start.10 = (bf16[16,1024]{1,0:T(8,128)(2,1)}, bf16[16,1024]{1,0:T(8,128)(2,1)S(1)}, u32[]{:S(2)}, u32[]{:S(2)}) collective-permute-start(bf16[16,1024]{1,0:T(8,128)(2,1)} %get-tuple-element.56), channel_id=1, source_target_pairs={{0,32},{1,33},{2,34},{3,35},{4,36},{5,37},{6,38},{7,39},{8,40},{9,... | collective-permute-start | bytes 98312 | tf_op jit(solution)/shard_map/ppermute | solution.py:38
  85.2 3.9 %collective-permute-start.11 = (bf16[16,1024]{1,0:T(8,128)(2,1)}, bf16[16,1024]{1,0:T(8,128)(2,1)S(1)}, u32[]{:S(2)}, u32[]{:S(2)}) collective-permute-start(bf16[16,1024]{1,0:T(8,128)(2,1)} %get-tuple-element.57), channel_id=1, source_target_pairs={{0,96},{1,97},{2,98},{3,99},{4,100},{5,101},{6,102},{7,103},{8,104... | collective-permute-start | bytes 98312 | tf_op jit(solution)/shard_map/ppermute | solution.py:38
  87.9 12.5 %copy-start.37 = (bf16[16,1024]{1,0:T(8,128)(2,1)}, bf16[16,1024]{1,0:T(8,128)(2,1)S(1)}, u32[]{:S(2)}) copy-start(bf16[16,1024]{1,0:T(8,128)(2,1)S(1)} %collective-permute-done.10.refs_5_) | copy-start | bytes 98308
  87.9 7.6 %collective-permute-start.7 = (bf16[32,1024]{1,0:T(8,128)(2,1)}, bf16[32,1024]{1,0:T(8,128)(2,1)S(1)}, u32[]{:S(2)}, u32[]{:S(2)}) collective-permute-start(bf16[32,1024]{1,0:T(8,128)(2,1)} %get-tuple-element.52), channel_id=1, source_target_pairs={{0,8},{1,9},{2,10},{3,11},{4,12},{5,13},{6,14},{7,15},{8,16},{9,17... | collective-permute-start | bytes 196616 | tf_op jit(solution)/shard_map/ppermute | solution.py:38
  89.2 11.2 %copy-start.38 = (bf16[16,1024]{1,0:T(8,128)(2,1)}, bf16[16,1024]{1,0:T(8,128)(2,1)S(1)}, u32[]{:S(2)}) copy-start(bf16[16,1024]{1,0:T(8,128)(2,1)S(1)} %collective-permute-done.11.refs_6_) | copy-start | bytes 98308
  89.2 4.5 %collective-permute-start.12 = (bf16[16,1024]{1,0:T(8,128)(2,1)}, bf16[16,1024]{1,0:T(8,128)(2,1)S(1)}, u32[]{:S(2)}, u32[]{:S(2)}) collective-permute-start(bf16[16,1024]{1,0:T(8,128)(2,1)} %get-tuple-element.58), channel_id=1, source_target_pairs={{0,64},{1,65},{2,66},{3,67},{4,68},{5,69},{6,70},{7,71},{8,72},{9,... | collective-permute-start | bytes 98312 | tf_op jit(solution)/shard_map/ppermute | solution.py:38
  93.7 3.5 %collective-permute-start.8 = (bf16[32,1024]{1,0:T(8,128)(2,1)}, bf16[32,1024]{1,0:T(8,128)(2,1)S(1)}, u32[]{:S(2)}, u32[]{:S(2)}) collective-permute-start(bf16[32,1024]{1,0:T(8,128)(2,1)} %get-tuple-element.53), channel_id=1, source_target_pairs={{0,24},{1,25},{2,26},{3,27},{4,28},{5,29},{6,30},{7,31},{8,0},{9,1... | collective-permute-start | bytes 196616 | tf_op jit(solution)/shard_map/ppermute | solution.py:38
  95.5 4.8 %collective-permute-start.9 = (bf16[32,1024]{1,0:T(8,128)(2,1)}, bf16[32,1024]{1,0:T(8,128)(2,1)S(1)}, u32[]{:S(2)}, u32[]{:S(2)}) collective-permute-start(bf16[32,1024]{1,0:T(8,128)(2,1)} %get-tuple-element.54), channel_id=1, source_target_pairs={{0,16},{1,17},{2,18},{3,19},{4,20},{5,21},{6,22},{7,23},{8,24},{9,... | collective-permute-start | bytes 196616 | tf_op jit(solution)/shard_map/ppermute | solution.py:38
  102.6 5.7 %collective-permute-start.15 = (bf16[48,1024]{1,0:T(8,128)(2,1)}, bf16[48,1024]{1,0:T(8,128)(2,1)S(1)}, u32[]{:S(2)}, u32[]{:S(2)}) collective-permute-start(bf16[48,1024]{1,0:T(8,128)(2,1)} %shard_map.191.refs_0_), channel_id=1, source_target_pairs={{0,2},{1,3},{2,0},{3,1},{4,6},{5,7},{6,4},{7,5},{8,10},{9,11},{10,... | collective-permute-start | bytes 294920 | tf_op jit(solution)/shard_map/ppermute | solution.py:38
  106.2 3.8 %collective-permute-start.14 = (bf16[48,1024]{1,0:T(8,128)(2,1)}, bf16[48,1024]{1,0:T(8,128)(2,1)S(1)}, u32[]{:S(2)}, u32[]{:S(2)}) collective-permute-start(bf16[48,1024]{1,0:T(8,128)(2,1)} %shard_map.191.refs_0_), channel_id=1, source_target_pairs={{0,3},{1,0},{2,1},{3,2},{4,7},{5,4},{6,5},{7,6},{8,11},{9,8},{10,9... | collective-permute-start | bytes 294920 | tf_op jit(solution)/shard_map/ppermute | solution.py:38
  108.4 5.0 %collective-permute-start.13 = (bf16[48,1024]{1,0:T(8,128)(2,1)}, bf16[48,1024]{1,0:T(8,128)(2,1)}, u32[]{:S(2)}, u32[]{:S(2)}) collective-permute-start(bf16[48,1024]{1,0:T(8,128)(2,1)} %shard_map.191.refs_0_), channel_id=1, source_target_pairs={{0,1},{1,2},{2,3},{3,0},{4,5},{5,6},{6,7},{7,4},{8,9},{9,10},{10,1... | collective-permute-start | bytes 294920 | tf_op jit(solution)/shard_map/ppermute | solution.py:38
  115.1 4.5 %collective-permute-start.18 = (bf16[16,1024]{1,0:T(8,128)(2,1)}, bf16[16,1024]{1,0:T(8,128)(2,1)S(1)}, u32[]{:S(2)}, u32[]{:S(2)}) collective-permute-start(bf16[16,1024]{1,0:T(8,128)(2,1)} %get-tuple-element.59.refs_0_), channel_id=1, source_target_pairs={{0,16},{1,17},{2,18},{3,19},{4,20},{5,21},{6,22},{7,23},{8,24},{9,... | collective-permute-start | bytes 98312 | tf_op jit(solution)/shard_map/ppermute | solution.py:38
  116.6 3.0 %collective-permute-start.17 = (bf16[16,1024]{1,0:T(8,128)(2,1)}, bf16[16,1024]{1,0:T(8,128)(2,1)S(1)}, u32[]{:S(2)}, u32[]{:S(2)}) collective-permute-start(bf16[16,1024]{1,0:T(8,128)(2,1)} %get-tuple-element.59.refs_0_), channel_id=1, source_target_pairs={{0,24},{1,25},{2,26},{3,27},{4,28},{5,29},{6,30},{7,31},{8,0},{9,1... | collective-permute-start | bytes 98312 | tf_op jit(solution)/shard_map/ppermute | solution.py:38
  119.6 4.2 %collective-permute-start.16 = (bf16[16,1024]{1,0:T(8,128)(2,1)}, bf16[16,1024]{1,0:T(8,128)(2,1)S(1)}, u32[]{:S(2)}, u32[]{:S(2)}) collective-permute-start(bf16[16,1024]{1,0:T(8,128)(2,1)} %get-tuple-element.59.refs_0_), channel_id=1, source_target_pairs={{0,8},{1,9},{2,10},{3,11},{4,12},{5,13},{6,14},{7,15},{8,16},{9,17... | collective-permute-start | bytes 98312 | tf_op jit(solution)/shard_map/ppermute | solution.py:38
  119.6 6.8 %collective-permute-start.21 = (bf16[16,1024]{1,0:T(8,128)(2,1)}, bf16[16,1024]{1,0:T(8,128)(2,1)S(1)}, u32[]{:S(2)}, u32[]{:S(2)}) collective-permute-start(bf16[16,1024]{1,0:T(8,128)(2,1)} %get-tuple-element.60.refs_4_), channel_id=1, source_target_pairs={{0,64},{1,65},{2,66},{3,67},{4,68},{5,69},{6,70},{7,71},{8,72},{9,... | collective-permute-start | bytes 98312 | tf_op jit(solution)/shard_map/ppermute | solution.py:38
  123.7 4.0 %collective-permute-start.20 = (bf16[16,1024]{1,0:T(8,128)(2,1)}, bf16[16,1024]{1,0:T(8,128)(2,1)S(1)}, u32[]{:S(2)}, u32[]{:S(2)}) collective-permute-start(bf16[16,1024]{1,0:T(8,128)(2,1)} %get-tuple-element.60.refs_4_), channel_id=1, source_target_pairs={{0,96},{1,97},{2,98},{3,99},{4,100},{5,101},{6,102},{7,103},{8,104... | collective-permute-start | bytes 98312 | tf_op jit(solution)/shard_map/ppermute | solution.py:38
  126.4 4.2 %collective-permute-start.19 = (bf16[16,1024]{1,0:T(8,128)(2,1)}, bf16[16,1024]{1,0:T(8,128)(2,1)S(1)}, u32[]{:S(2)}, u32[]{:S(2)}) collective-permute-start(bf16[16,1024]{1,0:T(8,128)(2,1)} %get-tuple-element.60.refs_4_), channel_id=1, source_target_pairs={{0,32},{1,33},{2,34},{3,35},{4,36},{5,37},{6,38},{7,39},{8,40},{9,... | collective-permute-start | bytes 98312 | tf_op jit(solution)/shard_map/ppermute | solution.py:38
  132.8 14.0 %collective-permute-start.28 = (bf16[64,1024]{1,0:T(8,128)(2,1)}, bf16[64,1024]{1,0:T(8,128)(2,1)S(1)}, u32[]{:S(2)}, u32[]{:S(2)}) collective-permute-start(bf16[64,1024]{1,0:T(8,128)(2,1)} %get-tuple-element.61.refs_0_), channel_id=1, source_target_pairs={{0,4},{1,5},{2,6},{3,7},{4,0},{5,1},{6,2},{7,3},{8,12},{9,13},{10,... | collective-permute-start | bytes 393224 | tf_op jit(solution)/shard_map/ppermute | solution.py:38
  144.6 6.8 %collective-permute-start.24 = (bf16[64,1024]{1,0:T(8,128)(2,1)}, bf16[64,1024]{1,0:T(8,128)(2,1)S(1)}, u32[]{:S(2)}, u32[]{:S(2)}) collective-permute-start(bf16[64,1024]{1,0:T(8,128)(2,1)} %get-tuple-element.61.refs_0_), channel_id=1, source_target_pairs={{0,64},{1,65},{2,66},{3,67},{4,68},{5,69},{6,70},{7,71},{8,72},{9,... | collective-permute-start | bytes 393224 | tf_op jit(solution)/shard_map/ppermute | solution.py:38
  144.7 7.5 %collective-permute-start.23 = (bf16[64,1024]{1,0:T(8,128)(2,1)}, bf16[64,1024]{1,0:T(8,128)(2,1)S(1)}, u32[]{:S(2)}, u32[]{:S(2)}) collective-permute-start(bf16[64,1024]{1,0:T(8,128)(2,1)} %get-tuple-element.61.refs_0_), channel_id=1, source_target_pairs={{0,96},{1,97},{2,98},{3,99},{4,100},{5,101},{6,102},{7,103},{8,104... | collective-permute-start | bytes 393224 | tf_op jit(solution)/shard_map/ppermute | solution.py:38
  145.6 9.0 %collective-permute-start.22 = (bf16[64,1024]{1,0:T(8,128)(2,1)}, bf16[64,1024]{1,0:T(8,128)(2,1)S(1)}, u32[]{:S(2)}, u32[]{:S(2)}) collective-permute-start(bf16[64,1024]{1,0:T(8,128)(2,1)} %get-tuple-element.61.refs_0_), channel_id=1, source_target_pairs={{0,32},{1,33},{2,34},{3,35},{4,36},{5,37},{6,38},{7,39},{8,40},{9,... | collective-permute-start | bytes 393224 | tf_op jit(solution)/shard_map/ppermute | solution.py:38
  146.1 9.0 %collective-permute-start.32 = (bf16[64,1024]{1,0:T(8,128)(2,1)}, bf16[64,1024]{1,0:T(8,128)(2,1)S(1)}, u32[]{:S(2)}, u32[]{:S(2)}) collective-permute-start(bf16[64,1024]{1,0:T(8,128)(2,1)} %get-tuple-element.62.refs_4_), channel_id=1, source_target_pairs={{0,4},{1,5},{2,6},{3,7},{4,0},{5,1},{6,2},{7,3},{8,12},{9,13},{10,... | collective-permute-start | bytes 393224 | tf_op jit(solution)/shard_map/ppermute | solution.py:38
  146.8 8.3 %collective-permute-start.27 = (bf16[64,1024]{1,0:T(8,128)(2,1)}, bf16[64,1024]{1,0:T(8,128)(2,1)S(1)}, u32[]{:S(2)}, u32[]{:S(2)}) collective-permute-start(bf16[64,1024]{1,0:T(8,128)(2,1)} %get-tuple-element.62.refs_4_), channel_id=1, source_target_pairs={{0,16},{1,17},{2,18},{3,19},{4,20},{5,21},{6,22},{7,23},{8,24},{9,... | collective-permute-start | bytes 393224 | tf_op jit(solution)/shard_map/ppermute | solution.py:38
  151.5 4.1 %collective-permute-start.26 = (bf16[64,1024]{1,0:T(8,128)(2,1)}, bf16[64,1024]{1,0:T(8,128)(2,1)S(1)}, u32[]{:S(2)}, u32[]{:S(2)}) collective-permute-start(bf16[64,1024]{1,0:T(8,128)(2,1)} %get-tuple-element.62.refs_4_), channel_id=1, source_target_pairs={{0,24},{1,25},{2,26},{3,27},{4,28},{5,29},{6,30},{7,31},{8,0},{9,1... | collective-permute-start | bytes 393224 | tf_op jit(solution)/shard_map/ppermute | solution.py:38
  152.2 5.7 %collective-permute-start.25 = (bf16[64,1024]{1,0:T(8,128)(2,1)}, bf16[64,1024]{1,0:T(8,128)(2,1)S(1)}, u32[]{:S(2)}, u32[]{:S(2)}) collective-permute-start(bf16[64,1024]{1,0:T(8,128)(2,1)} %get-tuple-element.62.refs_4_), channel_id=1, source_target_pairs={{0,8},{1,9},{2,10},{3,11},{4,12},{5,13},{6,14},{7,15},{8,16},{9,17... | collective-permute-start | bytes 393224 | tf_op jit(solution)/shard_map/ppermute | solution.py:38
  154.6 5.2 %collective-permute-start.31 = (bf16[64,1024]{1,0:T(8,128)(2,1)S(1)}, bf16[64,1024]{1,0:T(8,128)(2,1)S(1)}, u32[]{:S(2)}, u32[]{:S(2)}) collective-permute-start(bf16[64,1024]{1,0:T(8,128)(2,1)S(1)} %collective-permute-done.24.refs_3_), channel_id=1, source_target_pairs={{0,4},{1,5},{2,6},{3,7},{4,0},{5,1},{6,2},{7,3},{8,12},{9,13},{10,... | collective-permute-start | bytes 393224 | tf_op jit(solution)/shard_map/ppermute | solution.py:38
  155.1 14.5 %collective-permute-start.30 = (bf16[64,1024]{1,0:T(8,128)(2,1)S(1)}, bf16[64,1024]{1,0:T(8,128)(2,1)S(1)}, u32[]{:S(2)}, u32[]{:S(2)}) collective-permute-start(bf16[64,1024]{1,0:T(8,128)(2,1)S(1)} %collective-permute-done.23.refs_2_), channel_id=1, source_target_pairs={{0,4},{1,5},{2,6},{3,7},{4,0},{5,1},{6,2},{7,3},{8,12},{9,13},{10,... | collective-permute-start | bytes 393224 | tf_op jit(solution)/shard_map/ppermute | solution.py:38
  155.1 14.5 %collective-permute-start.29 = (bf16[64,1024]{1,0:T(8,128)(2,1)S(1)}, bf16[64,1024]{1,0:T(8,128)(2,1)S(1)}, u32[]{:S(2)}, u32[]{:S(2)}) collective-permute-start(bf16[64,1024]{1,0:T(8,128)(2,1)S(1)} %collective-permute-done.22.refs_1_), channel_id=1, source_target_pairs={{0,4},{1,5},{2,6},{3,7},{4,0},{5,1},{6,2},{7,3},{8,12},{9,13},{10,... | collective-permute-start | bytes 393224 | tf_op jit(solution)/shard_map/ppermute | solution.py:38
  155.6 14.0 %collective-permute-start.35 = (bf16[64,1024]{1,0:T(8,128)(2,1)S(1)}, bf16[64,1024]{1,0:T(8,128)(2,1)S(1)}, u32[]{:S(2)}, u32[]{:S(2)}) collective-permute-start(bf16[64,1024]{1,0:T(8,128)(2,1)S(1)} %collective-permute-done.27.refs_7_), channel_id=1, source_target_pairs={{0,4},{1,5},{2,6},{3,7},{4,0},{5,1},{6,2},{7,3},{8,12},{9,13},{10,... | collective-permute-start | bytes 393224 | tf_op jit(solution)/shard_map/ppermute | solution.py:38
  157.9 11.7 %collective-permute-start.34 = (bf16[64,1024]{1,0:T(8,128)(2,1)S(1)}, bf16[64,1024]{1,0:T(8,128)(2,1)S(1)}, u32[]{:S(2)}, u32[]{:S(2)}) collective-permute-start(bf16[64,1024]{1,0:T(8,128)(2,1)S(1)} %collective-permute-done.26.refs_6_), channel_id=1, source_target_pairs={{0,4},{1,5},{2,6},{3,7},{4,0},{5,1},{6,2},{7,3},{8,12},{9,13},{10,... | collective-permute-start | bytes 393224 | tf_op jit(solution)/shard_map/ppermute | solution.py:38
  159.8 9.8 %collective-permute-start.33 = (bf16[64,1024]{1,0:T(8,128)(2,1)S(1)}, bf16[64,1024]{1,0:T(8,128)(2,1)S(1)}, u32[]{:S(2)}, u32[]{:S(2)}) collective-permute-start(bf16[64,1024]{1,0:T(8,128)(2,1)S(1)} %collective-permute-done.25.refs_5_), channel_id=1, source_target_pairs={{0,4},{1,5},{2,6},{3,7},{4,0},{5,1},{6,2},{7,3},{8,12},{9,13},{10,... | collective-permute-start | bytes 393224 | tf_op jit(solution)/shard_map/ppermute | solution.py:38
  (35 other events, 126.6 us)

commit v2 on v1

v2 whole, which is shorter than its diff:
```python
import functools

import jax
import jax.numpy as jnp
from jax import lax
from jax.experimental import pallas as pl
from jax.experimental.pallas import tpu as pltpu
from jax.sharding import Mesh, PartitionSpec as P

beta_one = 0.9
beta_two = 0.999
adam_eps = 1e-06
learn_rate = 0.2
decay_rate = 0.01
max_norm = 1.0

D = 1024
BLOCK = 256
F32 = jnp.float32
BF16 = jnp.bfloat16
MIB = 1024 * 1024
AXES = ("x", "y", "c", "z")
PLANE = ("x", "y")
VMEM = pl.BlockSpec(memory_space=pltpu.VMEM)
ANY = pl.BlockSpec(memory_space=pl.ANY)
ROWS = 32
PIECE = 272


def place(x, y, c, z):
    return (((x % 4) * 4 + y % 4) * 2 + c % 2) * 4 + z % 4


def permute(value, to):
    pairs = [
        (place(x, y, c, z), place(*to(x, y, c, z)))
        for x in range(4)
        for y in range(4)
        for c in range(2)
        for z in range(4)
    ]
    return lax.ppermute(value, AXES, pairs)


def other_core(value):
    return permute(value, lambda x, y, c, z: (x, y, 1 - c, z))


def next_shard(value):
    return permute(value, lambda x, y, c, z: (x, y, c, z + 1 - 2 * c))


def exchange(value, axes):
    return lax.all_to_all(value, axes, split_axis=0, concat_axis=0, tiled=True)


def call(kernel, outs, ins, specs=None, scratch=(), cost=None, limit=58, **more):
    return pl.pallas_call(
        kernel,
        out_shape=[jax.ShapeDtypeStruct(shape, dtype) for shape, dtype in outs],
        in_specs=[VMEM] * len(ins) if specs is None else specs,
        out_specs=more.pop("out_specs", [VMEM] * len(outs)),
        scratch_shapes=list(scratch),
        cost_estimate=cost,
        compiler_params=pltpu.CompilerParams(vmem_limit_bytes=limit * MIB),
        **more,
    )(*ins)


def split_vectors(rows):
    high = rows.astype(BF16).astype(F32)
    return jnp.concatenate([high, rows - high], axis=0).astype(BF16)


def join_vectors(message):
    wide = message.astype(F32)
    return wide[0:8] + wide[8:16]


def backward_kernel(
    ctx,
    res,
    cot,
    weight,
    bias,
    gain,
    master,
    first,
    second,
    dres,
    send,
    keep,
    packed,
    ctxs,
    dress,
    pre,
    sums,
):
    step = pl.program_id(0)
    packed[0, 0] = master[...].astype(BF16)
    packed[0, 1] = first[...].astype(BF16)
    packed[0, 2] = second[...].astype(BF16)
    rows = pl.ds(pl.multiple_of(step * BLOCK, BLOCK), BLOCK)
    for shard in range(4):
        for core in range(2):
            start = 256 * shard + 128 * core
            side = 128 * (shard % 2)
            ctxs[2 * core + shard // 2, rows, side : side + 128] = ctx[:, start : start + 128]
    pre[...] = jnp.dot(ctx[...], weight[...], preferred_element_type=F32)

    @pl.when(step == 0)
    def _():
        sums[...] = jnp.zeros_like(sums)

    bias_row = bias[...]
    gain_row = gain[...]

    def chunk(i, carry):
        at_rows = pl.ds(pl.multiple_of(i * 16, 16), 16)
        value = pre[at_rows, :] + res[at_rows, :].astype(F32) + bias_row
        grad_out = cot[at_rows, :].astype(F32)
        scaled = grad_out * gain_row
        mean = jnp.sum(value, axis=1, keepdims=True) * (1.0 / D)
        mean_scaled = jnp.sum(scaled, axis=1, keepdims=True) * (1.0 / D)
        centred = value - mean
        var = jnp.sum(centred * centred, axis=1, keepdims=True) * (1.0 / D)
        cross = jnp.sum(scaled * centred, axis=1, keepdims=True) * (1.0 / D)
        rstd = lax.rsqrt(var + 1e-05)
        normed = centred * rstd
        d_pre = rstd * (scaled - mean_scaled - normed * (cross * rstd))
        d_low = d_pre.astype(BF16)
        dres[at_rows, :] = d_low
        dress[pl.ds(pl.multiple_of(step * BLOCK + i * 16, 16), 16), :] = d_low
        moved = grad_out * normed
        sums[0] += d_pre[0:8] + d_pre[8:16]
        sums[1] += moved[0:8] + moved[8:16]
        sums[2] += grad_out[0:8] + grad_out[8:16]
        return carry

    lax.fori_loop(0, BLOCK // 16, chunk, 0, unroll=2)

    @pl.when(step == D // BLOCK - 1)
    def _():
        core = lax.axis_index("c")

        def rows_of(m):
            return lax.dot_general(
                ctxs[m], dress[...], (((0,), (0,)), ((), ())), preferred_element_type=F32
            ).astype(BF16)

        for half in range(2):
            send[half * 256 : (half + 1) * 256, :] = rows_of((1 - core) * 2 + half)
        for half in range(2):
            keep[half * 256 : (half + 1) * 256, :] = rows_of(core * 2 + half)
        total = [jnp.sum(sums[k], axis=0, keepdims=True) for k in range(3)]
        message = split_vectors(jnp.concatenate(total + [jnp.zeros((5, D), F32)], axis=0))
        send[512:528, :] = message
        keep[512:528, :] = message


def backward(context, residual_in, cotangent, weight, bias, gain, master, first, second):
    block = pl.BlockSpec((BLOCK, D), lambda i: (i, 0))
    state = pl.BlockSpec((64, D), lambda i: (i, 0))
    pack = pl.BlockSpec((1, 3, 64, D), lambda i: (i // 2, 0, i % 2, 0))
    whole = pl.BlockSpec((D, D), lambda i: (0, 0))
    row = pl.BlockSpec((1, D), lambda i: (0, 0))
    half = pl.BlockSpec((528, D), lambda i: (0, 0))
    return call(
        backward_kernel,
        [((D, D), BF16), ((528, D), BF16), ((528, D), BF16), ((2, 3, 128, D), BF16)],
        (context, residual_in, cotangent, weight, bias, gain, master, first, second),
        specs=[block, block, block, whole, row, row, state, state, state],
        out_specs=[block, half, half, pack],
        grid=(D // BLOCK,),
        scratch=[
            pltpu.VMEM((4, D, 256), BF16),
            pltpu.VMEM((D, D), BF16),
            pltpu.VMEM((BLOCK, D), F32),
            pltpu.VMEM((3, 8, D), F32),
        ],
        cost=pl.CostEstimate(flops=4 * D**3, bytes_accessed=14 * MIB, transcendentals=D),
    )


def context_kernel(dres, weight, out):
    out[...] = lax.dot_general(
        dres[...], weight[...], (((1,), (1,)), ((), ())), preferred_element_type=F32
    ).astype(BF16)


def context_grad(d_resid, weight):
    block = pl.BlockSpec((BLOCK, D), lambda i: (i, 0))
    return call(
        context_kernel,
        [((D, D), BF16)],
        (d_resid, weight),
        specs=[block, pl.BlockSpec((D, D), lambda i: (0, 0))],
        out_specs=[block],
        grid=(D // BLOCK,),
        cost=pl.CostEstimate(flops=2 * D**3, bytes_accessed=6 * MIB, transcendentals=0),
    )[0]


def core_kernel(keep, got, out):
    message = split_vectors(join_vectors(keep[512:528, :]) + join_vectors(got[512:528, :]))
    for j in range(16):
        rows = slice(ROWS * j, ROWS * (j + 1))
        total = (keep[rows, :].astype(F32) + got[rows, :].astype(F32)).astype(BF16)
        for k in range(8):
            out[j, ROWS * k : ROWS * (k + 1), :] = total[:, 128 * k : 128 * (k + 1)]
        k = j % 8
        out[j, 256:PIECE, :] = message[:, 128 * k : 128 * (k + 1)]


def sum_kernel(n, copies, got, *rest):
    out = rest[-1]
    for at in range(0, 256, 32):
        rows = slice(at, at + 32)
        total = got[0, rows, :].astype(F32)
        for j in range(1, n):
            total = total + got[j, rows, :].astype(F32)
        total = total.astype(BF16)
        for j in range(copies):
            out[j, rows, :] = total
    total = join_vectors(got[0, 256:PIECE, :])
    for j in range(1, n):
        total = total + join_vectors(got[j, 256:PIECE, :])
    message = split_vectors(total)
    for j in range(copies):
        out[j, 256:PIECE, :] = message


def step_of(grad, first, second, param, decay):
    first_new = beta_one * first + (1.0 - beta_one) * grad
    second_new = beta_two * second + (1.0 - beta_two) * grad * grad
    update = first_new / (jnp.sqrt(second_new) + adam_eps) + decay * param
    return first_new, second_new, update


def lamb_kernel(
    mine,
    others,
    near,
    near_other,
    far,
    far_other,
    master,
    first,
    second,
    vectors,
    vec_first,
    vec_second,
    weight_out,
    master_out,
    first_out,
    second_out,
    vec_out,
    vec_first_out,
    vec_second_out,
    grad,
    update,
    sums,
):
    core, z = lax.axis_index("c"), lax.axis_index("z")
    for which, pieces in enumerate((mine, others)):
        half = 128 * lax.rem(core + which, 2)
        for j in range(16):
            rows = pl.ds(pl.multiple_of(256 * (j // 4) + ROWS * (j % 4) + half, ROWS), ROWS)
            for k in range(8):
                block = pieces[j, ROWS * k : ROWS * (k + 1), :]
                grad[rows, 128 * k : 128 * (k + 1)] = block
    grad_vectors = jnp.concatenate(
        [join_vectors(mine[k, 256:PIECE, :]) for k in range(8)], axis=1
    )[0:3]

    def fold(value):
        return value[0:8] + value[8:16]

    zero = jnp.zeros((8, D), F32)

    def square(i, total):
        g = grad[pl.ds(pl.multiple_of(i * 16, 16), 16), :].astype(F32)
        return total + fold(g * g)

    grad_sq = jnp.sum(lax.fori_loop(0, D // 16, square, zero, unroll=4))
    total = jnp.sqrt(
        jnp.full((1, 1), grad_sq + jnp.sum(grad_vectors * grad_vectors), F32)
    )
    factor = 1.0 / jnp.maximum(1.0, total / max_norm)

    def from_pack(pack):
        return lambda rows: tuple(pack[n, rows, :].astype(F32) for n in range(3))

    def from_shard(base):
        def load(rows):
            rows = pl.ds(base + rows.start, rows.size)
            return tuple(
                ref[rows, :].astype(BF16).astype(F32) for ref in (master, first, second)
            )

        return load

    side = 1 - 2 * core
    blocks = (
        (z, 0, from_shard(0)),
        (z, 1, from_shard(128)),
        (z - side, core, from_pack(near.at[core])),
        (z - side, 1 - core, from_pack(near.at[1 - core])),
        (z + side, 1 - core, from_pack(near_other.at[1 - core])),
        (z + side, core, from_pack(near_other.at[core])),
        (z + 2, core, from_pack(far)),
        (z + 2, 1 - core, from_pack(far_other)),
    )
    blocks = [(lax.rem(s + 4, 4) * 2 + half, load) for s, half, load in blocks]

    for index, load in blocks:

        def full(i, totals):
            rows = pl.ds(pl.multiple_of(i * 16, 16), 16)
            place_at = pl.ds(pl.multiple_of(index * 128 + i * 16, 16), 16)
            w, m, v = load(rows)
            _, _, u = step_of(grad[place_at, :].astype(F32) * factor, m, v, w, decay_rate)
            update[place_at, :] = u
            return totals[0] + fold(u * u), totals[1] + fold(w * w)

        update_sq, weight_sq = lax.fori_loop(0, 8, full, (zero, zero), unroll=2)
        sums[index, 0] = update_sq
        sums[index, 1] = weight_sq

    update_sq, weight_sq = sums[0, 0], sums[0, 1]
    for index in range(1, 8):
        update_sq = update_sq + sums[index, 0]
        weight_sq = weight_sq + sums[index, 1]
    update_sq = jnp.full((1, 1), jnp.sum(update_sq), F32)
    weight_sq = jnp.full((1, 1), jnp.sum(weight_sq), F32)
    rate = learn_rate * (jnp.sqrt(weight_sq) / jnp.sqrt(update_sq + 1e-06))

    for index, load in blocks:

        def finish(i, carry):
            rows = pl.ds(pl.multiple_of(i * 16, 16), 16)
            place_at = pl.ds(pl.multiple_of(index * 128 + i * 16, 16), 16)
            weight_out[place_at, :] = (load(rows)[0] - rate * update[place_at, :]).astype(BF16)
            return carry

        lax.fori_loop(0, 8, finish, 0, unroll=2)

    def shard(i, carry):
        rows = pl.ds(pl.multiple_of(i * 16, 16), 16)
        g = grad[pl.ds(pl.multiple_of(z * 256 + i * 16, 16), 16), :].astype(F32) * factor
        w = master[rows, :]
        first_new, second_new, u = step_of(g, first[rows, :], second[rows, :], w, decay_rate)
        first_out[rows, :] = first_new
        second_out[rows, :] = second_new
        master_out[rows, :] = w - rate * u
        return carry

    lax.fori_loop(0, 256 // 16, shard, 0, unroll=2)

    params = vectors[...]
    first_new, second_new, u = step_of(
        grad_vectors * factor, vec_first[...], vec_second[...], params, 0.0
    )
    trust = jnp.sqrt(jnp.sum(params * params, axis=1, keepdims=True)) / jnp.sqrt(
        jnp.sum(u * u, axis=1, keepdims=True) + 1e-06
    )
    vec_out[...] = params - learn_rate * trust * u
    vec_first_out[...] = first_new
    vec_second_out[...] = second_new


def on_device(
    context,
    residual_in,
    cotangent,
    weight,
    master,
    moment_first,
    moment_second,
    out_bias,
    ln_gain,
    ln_shift,
    vector_first,
    vector_second,
):
    d_resid, send, keep, packed = backward(
        context,
        residual_in,
        cotangent,
        weight,
        out_bias.reshape(1, D),
        ln_gain.reshape(1, D),
        master,
        moment_first,
        moment_second,
    )
    got = other_core(send)
    near = next_shard(packed)
    d_context = context_grad(d_resid, weight)

    (pieces,) = call(core_kernel, [((16, PIECE, 128), BF16)], (keep, got), limit=8)
    pieces = exchange(pieces, PLANE)
    (pieces,) = call(
        functools.partial(sum_kernel, 16, 4),
        [((4, PIECE, 128), BF16)],
        (pieces, near, d_context),
        specs=[VMEM, ANY, ANY],
        limit=8,
    )
    far = next_shard(lax.dynamic_index_in_dim(near, lax.axis_index("c"), keepdims=False))
    pieces = exchange(pieces, "z")
    (pieces,) = call(
        functools.partial(sum_kernel, 4, 16),
        [((16, PIECE, 128), BF16)],
        (pieces, far),
        specs=[VMEM, ANY],
        limit=8,
    )
    near_other, far_other = other_core(near), other_core(far)
    mine = exchange(pieces, PLANE)
    others = other_core(mine)

    vectors = jnp.stack([out_bias, ln_gain, ln_shift])
    shard = ((256, D), F32)
    rows = ((3, D), F32)
    outs = call(
        lamb_kernel,
        [((D, D), BF16), shard, shard, shard, rows, rows, rows],
        (
            mine,
            others,
            near,
            near_other,
            far,
            far_other,
            master,
            moment_first,
            moment_second,
            vectors,
            vector_first,
            vector_second,
        ),
        specs=[VMEM] * 12,
        scratch=[
            pltpu.VMEM((D, D), BF16),
            pltpu.VMEM((D, D), F32),
            pltpu.VMEM((8, 2, 8, D), F32),
        ],
        limit=40,
    )
    return (d_context, d_resid, *outs)


def solution(mesh):
    mesh = Mesh(mesh.devices.reshape(4, 4, 2, 4), AXES)
    tokens, copied, shard = P(AXES, None), P(), P("z", None)
    return jax.shard_map(
        on_device,
        mesh=mesh,
        in_specs=(tokens,) * 3 + (copied,) + (shard,) * 3 + (copied,) * 5,
        out_specs=(tokens, tokens, copied) + (shard,) * 3 + (copied,) * 3,
        check_vma=False,
    )
```

time: 180 us -> 106 us (0.59)
  starting transfers between devices: 62.9 us -> 26.4 us
  waiting for transfers between devices: 59.9 us -> 25.9 us
  blocking collectives: 0 us -> 7.97 us
  Pallas kernels: 41.5 us -> 35.1 us
  local copies, waits for them, and re-layouts: 14.2 us -> 9.46 us
    ppermute x42 -> x6, starting transfers between devices: 62.9 us -> 13.9 us  [permute(): return lax.ppermute(value, AXES, pairs)]
    ppermute x42 -> x6, waiting for transfers between devices: 59.9 us -> 11.9 us  [permute(): return lax.ppermute(value, AXES, pairs)]
    all_to_all x0 -> x2, waiting for transfers between devices: none -> 14.1 us  [exchange(): return lax.all_to_all(value, axes, split_axis=0, concat_axis=0, tiled=True)]
    all_to_all x0 -> x2, starting transfers between devices: none -> 12.5 us  [exchange(): return lax.all_to_all(value, axes, split_axis=0, concat_axis=0, tiled=True)]
    all_to_all x0 -> x1, blocking collectives: none -> 7.97 us  [exchange(): return lax.all_to_all(value, axes, split_axis=0, concat_axis=0, tiled=True)]
    unnamed x82 -> x24, local copies, waits for them, and re-layouts: 14.2 us -> 8.53 us
    pallas_call x9 -> x6, Pallas kernels: 40 us -> 35.1 us  [call(): pl.pallas_call(kernel, out_shape=[jax.ShapeDtypeStruct(shape, dtype) for...]
  transfers between devices with their start and end apart: 42 -> 8, of which waited for: 18 -> 5; matrix products, arithmetic and copies ran while one was open for 0% -> 1% of each run, Pallas kernels for 10% -> 6%
where the time goes in v2:
time: 106 us
  Pallas kernels  35.1 us (33%)
  starting transfers between devices  26.4 us (25%)
  waiting for transfers between devices  25.9 us (24%)
  local copies, waits for them, and re-layouts  9.46 us (9%)
  blocking collectives  7.97 us (8%)
    pallas_call x6, Pallas kernels, call(): pl.pallas_call(kernel, out_shape=[jax.ShapeDtypeStruct(shape, dtype) for...  35.1 us
    all_to_all x2, waiting for transfers between devices, exchange(): return lax.all_to_all(value, axes, split_axis=0, concat_axis=0, tiled=True)  14.1 us
    ppermute x6, starting transfers between devices, permute(): return lax.ppermute(value, AXES, pairs)  13.9 us
    all_to_all x2, starting transfers between devices, exchange(): return lax.all_to_all(value, axes, split_axis=0, concat_axis=0, tiled=True)  12.5 us
    ppermute x6, waiting for transfers between devices, permute(): return lax.ppermute(value, AXES, pairs)  11.9 us
    unnamed x24, local copies, waits for them, and re-layouts  8.53 us
    all_to_all x1, blocking collectives, exchange(): return lax.all_to_all(value, axes, split_axis=0, concat_axis=0, tiled=True)  7.97 us
  transfers between devices with their start and end apart: 8, of which 5 were waited for; matrix products, arithmetic and copies ran while one was open for 1% of the time, Pallas kernels for 6%

profile of v2, /device:TPU:1, one launch (start us, length us, event | category | flops | bytes accessed | tf_op | source)
XLA Modules:
  0.0 105.5 jit_solution(14431969976677117231)
XLA Ops:
  0.6 17.4 %shard_map.187 = (bf16[1024,1024]{1,0:T(8,128)(2,1)}, bf16[528,1024]{1,0:T(8,128)(2,1)}, bf16[528,1024]{1,0:T(8,128)(2,1)}, bf16[2,3,128,1024]{3,2,1,0:T(8,128)(2,1)}) custom-call(bf16[1024,1024]{1,0:T(8,128)(2,1)} %ctx.1, bf16[1024,1024]{1,0:T(8,128)(2,1)} %res.1, bf16[1024,1024]{1,0:T(8,128)(2,1)} %cot.1, bf16[1024,1024]{1,0:T(8,128)(2,1)} %weight.3, ...), custom_call_target="tpu_custom_call" | custom-call | flops 4294967296 | bytes 14680064 | tf_op jit(solution)/shard_map/pallas_call | solution.py:58
  18.1 4.7 %collective-permute-start.1 = (bf16[2,3,128,1024]{3,2,1,0:T(8,128)(2,1)}, bf16[2,3,128,1024]{3,2,1,0:T(8,128)(2,1)S(1)}, u32[]{:S(2)}, u32[]{:S(2)}) collective-permute-start(bf16[2,3,128,1024]{3,2,1,0:T(8,128)(2,1)} %get-tuple-element.23), channel_id=1, source_target_pairs={{0,1},{1,2},{2,3},{3,0},{4,7},{5,4},{6,5},{7,6},{8,9},{9,10},{10,1... | collective-permute-start | bytes 4718600 | tf_op jit(solution)/shard_map/ppermute | solution.py:42
  22.8 0.0 collective-permute-start
  22.8 2.9 %collective-permute-done.got = bf16[528,1024]{1,0:T(8,128)(2,1)S(1)} collective-permute-done((bf16[528,1024]{1,0:T(8,128)(2,1)}, bf16[528,1024]{1,0:T(8,128)(2,1)S(1)}, u32[]{:S(2)}, u32[]{:S(2)}) %collective-permute-start) | collective-permute-done | bytes 1081376 | tf_op jit(solution)/shard_map/ppermute | solution.py:42
  25.7 0.0 copy-start.3
  25.7 1.2 %copy-done.3 = bf16[528,1024]{1,0:T(8,128)(2,1)S(1)} copy-done((bf16[528,1024]{1,0:T(8,128)(2,1)S(1)}, bf16[528,1024]{1,0:T(8,128)(2,1)}, u32[]{:S(2)}) %copy-start.3) | copy-done | bytes 1081368
  26.9 0.3 shard_map.189
  27.2 0.0 copy-start
  27.2 1.0 copy-done
  28.2 6.7 %all-to-all-start = ((bf16[16,272,128]{2,1,0:T(8,128)(2,1)}), bf16[16,272,128]{2,1,0:T(8,128)(2,1)S(1)}, u32[]{:S(2)}, u32[]{:S(2)}) async-start(bf16[16,272,128]{2,1,0:T(8,128)(2,1)} %copy-done), calls=%async_computation | async-start | bytes 2228224 | tf_op jit(solution)/shard_map/all_to_all | solution.py:54
  34.9 5.5 %collective-permute-done.1.rest_0_.near = bf16[2,3,128,1024]{3,2,1,0:T(8,128)(2,1)S(1)} collective-permute-done((bf16[2,3,128,1024]{3,2,1,0:T(8,128)(2,1)}, bf16[2,3,128,1024]{3,2,1,0:T(8,128)(2,1)S(1)}, u32[]{:S(2)}, u32[]{:S(2)}) %collective-permute-start.1) | collective-permute-done | bytes 1572896 | tf_op jit(solution)/shard_map/ppermute | solution.py:42
  40.4 0.9 dynamic-slice_bitcast_fusion
  41.4 3.0 %collective-permute-start.2 = (bf16[3,128,1024]{2,1,0:T(8,128)(2,1)}, bf16[3,128,1024]{2,1,0:T(8,128)(2,1)S(1)}, u32[]{:S(2)}, u32[]{:S(2)}) collective-permute-start(bf16[3,128,1024]{2,1,0:T(8,128)(2,1)} %dynamic-slice_bitcast_fusion), channel_id=1, source_target_pairs={{0,1},{1,2},{2,3},{3,0},{4,7},{5,4},{6,5},{7,6},{8,9},{9,10},{10,1... | collective-permute-start | bytes 2359304 | tf_op jit(solution)/shard_map/ppermute | solution.py:42
  44.4 6.1 %shard_map.188.rest_1_ = bf16[1024,1024]{1,0:T(8,128)(2,1)} custom-call(bf16[1024,1024]{1,0:T(8,128)(2,1)} %get-tuple-element.12.dres, bf16[1024,1024]{1,0:T(8,128)(2,1)} %weight.3), custom_call_target="tpu_custom_call" | custom-call | flops 2147483648 | bytes 6291456 | tf_op jit(solution)/shard_map/pallas_call | solution.py:58
  50.5 1.4 %all-to-all-done.got = bf16[16,272,128]{2,1,0:T(8,128)(2,1)S(1)} async-done(((bf16[16,272,128]{2,1,0:T(8,128)(2,1)}), bf16[16,272,128]{2,1,0:T(8,128)(2,1)S(1)}, u32[]{:S(2)}, u32[]{:S(2)}) %all-to-all-start) | async-done | bytes 1114144 | tf_op jit(solution)/shard_map/all_to_all | solution.py:54
  51.9 0.0 copy-start.2
  51.9 1.6 %copy-done.2 = bf16[1024,1024]{1,0:T(8,128)(2,1)S(1)} copy-done((bf16[1024,1024]{1,0:T(8,128)(2,1)S(1)}, bf16[1024,1024]{1,0:T(8,128)(2,1)}, u32[]{:S(2)}) %copy-start.2) | copy-done | bytes 2097176
  53.5 0.2 shard_map.190
  53.7 8.0 %all_to_all.15.got = bf16[4,272,128]{2,1,0:T(8,128)(2,1)S(1)} all-to-all(bf16[4,272,128]{2,1,0:T(8,128)(2,1)S(1)} %shard_map.190), channel_id=1, replica_groups=mesh['x'=4,'y'=4,'c'=2,'z'=4] {'z'}, dimensions={0} | all-to-all | bytes 557056 | tf_op jit(solution)/shard_map/all_to_all | solution.py:54
  61.6 0.0 collective-permute-done.2.rest_0_.far
  61.6 0.1 shard_map.191
  61.7 0.0 copy-start.1
  61.7 1.0 copy-done.1
  62.7 0.0 copy-start.9
  62.7 0.0 copy-start.10
  62.7 0.0 copy-start.11
  62.7 0.0 copy-start.7
  62.7 0.0 copy-start.8
  62.7 5.8 %all-to-all-start.2 = ((bf16[16,272,128]{2,1,0:T(8,128)(2,1)}), bf16[16,272,128]{2,1,0:T(8,128)(2,1)S(1)}, u32[]{:S(2)}, u32[]{:S(2)}) async-start(bf16[16,272,128]{2,1,0:T(8,128)(2,1)} %copy-done.1), calls=%async_computation.2 | async-start | bytes 2228224 | tf_op jit(solution)/shard_map/all_to_all | solution.py:54
  68.5 2.6 %collective-permute-start.4 = (bf16[2,3,128,1024]{3,2,1,0:T(8,128)(2,1)S(1)}, bf16[2,3,128,1024]{3,2,1,0:T(8,128)(2,1)}, u32[]{:S(2)}, u32[]{:S(2)}) collective-permute-start(bf16[2,3,128,1024]{3,2,1,0:T(8,128)(2,1)S(1)} %collective-permute-done.1.rest_0_.near), channel_id=1, source_target_pairs={{0,4},{1,5},{2,6},{3,7},{4,0},{5,1},{6,2},{7,3},{8,12},{9,13},{10,... | collective-permute-start | bytes 4718600 | tf_op jit(solution)/shard_map/ppermute | solution.py:42
  71.1 12.6 %all-to-all-done.2.mine = bf16[16,272,128]{2,1,0:T(8,128)(2,1)S(1)} async-done(((bf16[16,272,128]{2,1,0:T(8,128)(2,1)}), bf16[16,272,128]{2,1,0:T(8,128)(2,1)S(1)}, u32[]{:S(2)}, u32[]{:S(2)}) %all-to-all-start.2) | async-done | bytes 1114144 | tf_op jit(solution)/shard_map/all_to_all | solution.py:54
  83.7 3.6 %collective-permute-start.3 = (bf16[16,272,128]{2,1,0:T(8,128)(2,1)S(1)}, bf16[16,272,128]{2,1,0:T(8,128)(2,1)S(1)}, u32[]{:S(2)}, u32[]{:S(2)}) collective-permute-start(bf16[16,272,128]{2,1,0:T(8,128)(2,1)S(1)} %all-to-all-done.2.mine), channel_id=1, source_target_pairs={{0,4},{1,5},{2,6},{3,7},{4,0},{5,1},{6,2},{7,3},{8,12},{9,13},{10,... | collective-permute-start | bytes 3342344 | tf_op jit(solution)/shard_map/ppermute | solution.py:42
  87.3 0.0 collective-permute-start.5
  87.3 0.0 copy-done.9
  87.3 0.0 copy-done.10
  87.3 0.0 copy-done.11
  87.3 3.5 %collective-permute-done.5.far_other = bf16[3,128,1024]{2,1,0:T(8,128)(2,1)S(1)} collective-permute-done((bf16[3,128,1024]{2,1,0:T(8,128)(2,1)S(1)}, bf16[3,128,1024]{2,1,0:T(8,128)(2,1)S(1)}, u32[]{:S(2)}, u32[]{:S(2)}) %collective-permute-start.5) | collective-permute-done | bytes 786464 | tf_op jit(solution)/shard_map/ppermute | solution.py:42
  90.8 0.0 collective-permute-done.4.near_other
  90.8 0.0 collective-permute-done.3.others
  90.8 0.0 copy-done.7
  90.8 0.0 copy-done.8
  90.8 0.0 copy-start.4
  90.8 1.2 %copy-done.4 = f32[256,1024]{1,0:T(8,128)S(1)} copy-done((f32[256,1024]{1,0:T(8,128)S(1)}, f32[256,1024]{1,0:T(8,128)}, u32[]{:S(2)}) %copy-start.4) | copy-done | bytes 1048600
  92.0 0.0 copy-start.5
  92.0 1.2 %copy-done.5 = f32[256,1024]{1,0:T(8,128)S(1)} copy-done((f32[256,1024]{1,0:T(8,128)S(1)}, f32[256,1024]{1,0:T(8,128)}, u32[]{:S(2)}) %copy-start.5) | copy-done | bytes 1048600
  93.3 0.0 copy-start.6
  93.3 1.2 %copy-done.6 = f32[256,1024]{1,0:T(8,128)S(1)} copy-done((f32[256,1024]{1,0:T(8,128)S(1)}, f32[256,1024]{1,0:T(8,128)}, u32[]{:S(2)}) %copy-start.6) | copy-done | bytes 1048600
  94.5 11.1 %shard_map.192 = (bf16[1024,1024]{1,0:T(8,128)(2,1)}, f32[256,1024]{1,0:T(8,128)}, f32[256,1024]{1,0:T(8,128)}, f32[256,1024]{1,0:T(8,128)}, f32[3,1024]{1,0:T(4...) custom-call(bf16[16,272,128]{2,1,0:T(8,128)(2,1)S(1)} %all-to-all-done.2.mine, ...), custom_call_target="tpu_custom_call" | custom-call | tf_op jit(solution)/shard_map/pallas_call | solution.py:58
  (1 shorter events, 0.0 us)
Async XLA Ops:
  18.1 22.3 %collective-permute-start.1 = (bf16[2,3,128,1024]{3,2,1,0:T(8,128)(2,1)}, bf16[2,3,128,1024]{3,2,1,0:T(8,128)(2,1)S(1)}, u32[]{:S(2)}, u32[]{:S(2)}) collective-permute-start(bf16[2,3,128,1024]{3,2,1,0:T(8,128)(2,1)} %get-tuple-element.23), channel_id=1, source_target_pairs={{0,1},{1,2},{2,3},{3,0},{4,7},{5,4},{6,5},{7,6},{8,9},{9,10},{10,1... | collective-permute-start | bytes 4718600 | tf_op jit(solution)/shard_map/ppermute | solution.py:42
  22.8 2.9 %collective-permute-start = (bf16[528,1024]{1,0:T(8,128)(2,1)}, bf16[528,1024]{1,0:T(8,128)(2,1)S(1)}, u32[]{:S(2)}, u32[]{:S(2)}) collective-permute-start(bf16[528,1024]{1,0:T(8,128)(2,1)} %get-tuple-element.22), channel_id=1, source_target_pairs={{0,4},{1,5},{2,6},{3,7},{4,0},{5,1},{6,2},{7,3},{8,12},{9,13},{10,... | collective-permute-start | bytes 3244040 | tf_op jit(solution)/shard_map/ppermute | solution.py:42
  25.7 1.2 %copy-start.3 = (bf16[528,1024]{1,0:T(8,128)(2,1)S(1)}, bf16[528,1024]{1,0:T(8,128)(2,1)}, u32[]{:S(2)}) copy-start(bf16[528,1024]{1,0:T(8,128)(2,1)} %get-tuple-element.21.keep) | copy-start | bytes 3244036
  27.2 1.0 copy-start
  28.2 23.7 %all-to-all-start = ((bf16[16,272,128]{2,1,0:T(8,128)(2,1)}), bf16[16,272,128]{2,1,0:T(8,128)(2,1)S(1)}, u32[]{:S(2)}, u32[]{:S(2)}) async-start(bf16[16,272,128]{2,1,0:T(8,128)(2,1)} %copy-done), calls=%async_computation | async-start | bytes 2228224 | tf_op jit(solution)/shard_map/all_to_all | solution.py:54
  41.4 20.3 %collective-permute-start.2 = (bf16[3,128,1024]{2,1,0:T(8,128)(2,1)}, bf16[3,128,1024]{2,1,0:T(8,128)(2,1)S(1)}, u32[]{:S(2)}, u32[]{:S(2)}) collective-permute-start(bf16[3,128,1024]{2,1,0:T(8,128)(2,1)} %dynamic-slice_bitcast_fusion), channel_id=1, source_target_pairs={{0,1},{1,2},{2,3},{3,0},{4,7},{5,4},{6,5},{7,6},{8,9},{9,10},{10,1... | collective-permute-start | bytes 2359304 | tf_op jit(solution)/shard_map/ppermute | solution.py:42
  51.9 1.6 %copy-start.2 = (bf16[1024,1024]{1,0:T(8,128)(2,1)S(1)}, bf16[1024,1024]{1,0:T(8,128)(2,1)}, u32[]{:S(2)}) copy-start(bf16[1024,1024]{1,0:T(8,128)(2,1)} %shard_map.188.rest_1_) | copy-start | bytes 6291460
  61.7 1.0 copy-start.1
  62.7 24.6 %copy-start.9 = (f32[1024]{0:T(1024)S(1)}, f32[1024]{0:T(1024)}, u32[]{:S(2)}) copy-start(f32[1024]{0:T(1024)} %param.19) | copy-start | bytes 12292
  62.7 24.6 %copy-start.10 = (f32[1024]{0:T(1024)S(1)}, f32[1024]{0:T(1024)}, u32[]{:S(2)}) copy-start(f32[1024]{0:T(1024)} %param.20) | copy-start | bytes 12292
  62.7 24.6 %copy-start.11 = (f32[1024]{0:T(1024)S(1)}, f32[1024]{0:T(1024)}, u32[]{:S(2)}) copy-start(f32[1024]{0:T(1024)} %param.21) | copy-start | bytes 12292
  62.7 28.1 %copy-start.7 = (f32[3,1024]{1,0:T(4,128)S(1)}, f32[3,1024]{1,0:T(4,128)}, u32[]{:S(2)}) copy-start(f32[3,1024]{1,0:T(4,128)} %vec_first.1) | copy-start | bytes 36868
  62.7 28.1 %copy-start.8 = (f32[3,1024]{1,0:T(4,128)S(1)}, f32[3,1024]{1,0:T(4,128)}, u32[]{:S(2)}) copy-start(f32[3,1024]{1,0:T(4,128)} %vec_second.1) | copy-start | bytes 36868
  62.7 21.0 %all-to-all-start.2 = ((bf16[16,272,128]{2,1,0:T(8,128)(2,1)}), bf16[16,272,128]{2,1,0:T(8,128)(2,1)S(1)}, u32[]{:S(2)}, u32[]{:S(2)}) async-start(bf16[16,272,128]{2,1,0:T(8,128)(2,1)} %copy-done.1), calls=%async_computation.2 | async-start | bytes 2228224 | tf_op jit(solution)/shard_map/all_to_all | solution.py:54
  68.5 22.3 %collective-permute-start.4 = (bf16[2,3,128,1024]{3,2,1,0:T(8,128)(2,1)S(1)}, bf16[2,3,128,1024]{3,2,1,0:T(8,128)(2,1)}, u32[]{:S(2)}, u32[]{:S(2)}) collective-permute-start(bf16[2,3,128,1024]{3,2,1,0:T(8,128)(2,1)S(1)} %collective-permute-done.1.rest_0_.near), channel_id=1, source_target_pairs={{0,4},{1,5},{2,6},{3,7},{4,0},{5,1},{6,2},{7,3},{8,12},{9,13},{10,... | collective-permute-start | bytes 4718600 | tf_op jit(solution)/shard_map/ppermute | solution.py:42
  83.7 7.1 %collective-permute-start.3 = (bf16[16,272,128]{2,1,0:T(8,128)(2,1)S(1)}, bf16[16,272,128]{2,1,0:T(8,128)(2,1)S(1)}, u32[]{:S(2)}, u32[]{:S(2)}) collective-permute-start(bf16[16,272,128]{2,1,0:T(8,128)(2,1)S(1)} %all-to-all-done.2.mine), channel_id=1, source_target_pairs={{0,4},{1,5},{2,6},{3,7},{4,0},{5,1},{6,2},{7,3},{8,12},{9,13},{10,... | collective-permute-start | bytes 3342344 | tf_op jit(solution)/shard_map/ppermute | solution.py:42
  87.3 3.5 %collective-permute-start.5 = (bf16[3,128,1024]{2,1,0:T(8,128)(2,1)S(1)}, bf16[3,128,1024]{2,1,0:T(8,128)(2,1)S(1)}, u32[]{:S(2)}, u32[]{:S(2)}) collective-permute-start(bf16[3,128,1024]{2,1,0:T(8,128)(2,1)S(1)} %collective-permute-done.2.rest_0_.far), channel_id=1, source_target_pairs={{0,4},{1,5},{2,6},{3,7},{4,0},{5,1},{6,2},{7,3},{8,12},{9,13},{10,... | collective-permute-start | bytes 2359304 | tf_op jit(solution)/shard_map/ppermute | solution.py:42
  90.8 1.2 %copy-start.4 = (f32[256,1024]{1,0:T(8,128)S(1)}, f32[256,1024]{1,0:T(8,128)}, u32[]{:S(2)}) copy-start(f32[256,1024]{1,0:T(8,128)} %master.3) | copy-start | bytes 3145732
  92.0 1.2 %copy-start.5 = (f32[256,1024]{1,0:T(8,128)S(1)}, f32[256,1024]{1,0:T(8,128)}, u32[]{:S(2)}) copy-start(f32[256,1024]{1,0:T(8,128)} %first.3) | copy-start | bytes 3145732
  93.3 1.2 %copy-start.6 = (f32[256,1024]{1,0:T(8,128)S(1)}, f32[256,1024]{1,0:T(8,128)}, u32[]{:S(2)}) copy-start(f32[256,1024]{1,0:T(8,128)} %second.3) | copy-start | bytes 3145732

commit v3 on v2

v3 whole, which is shorter than its diff:
```python
import functools

import jax
import jax.numpy as jnp
from jax import lax
from jax.experimental import pallas as pl
from jax.experimental.pallas import tpu as pltpu
from jax.sharding import Mesh, PartitionSpec as P

beta_one = 0.9
beta_two = 0.999
adam_eps = 1e-06
learn_rate = 0.2
decay_rate = 0.01
max_norm = 1.0

D = 1024
BLOCK = 256
F32 = jnp.float32
BF16 = jnp.bfloat16
MIB = 1024 * 1024
AXES = ("x", "y", "c", "z")
PLANE = ("x", "y")
VMEM = pl.BlockSpec(memory_space=pltpu.VMEM)
ANY = pl.BlockSpec(memory_space=pl.ANY)
HBM = pl.BlockSpec(memory_space=pltpu.HBM)
DMA = pltpu.SemaphoreType.DMA
ROWS = 32
PIECE = 272


def place(x, y, c, z):
    return (((x % 4) * 4 + y % 4) * 2 + c % 2) * 4 + z % 4


def permute(value, to):
    pairs = [
        (place(x, y, c, z), place(*to(x, y, c, z)))
        for x in range(4)
        for y in range(4)
        for c in range(2)
        for z in range(4)
    ]
    return lax.ppermute(value, AXES, pairs)


def other_core(value):
    return permute(value, lambda x, y, c, z: (x, y, 1 - c, z))


def next_shard(value):
    return permute(value, lambda x, y, c, z: (x, y, c, z + 1 - 2 * c))


def exchange(value, axes):
    return lax.all_to_all(value, axes, split_axis=0, concat_axis=0, tiled=True)


def call(kernel, outs, ins, specs=None, scratch=(), cost=None, limit=58, **more):
    return pl.pallas_call(
        kernel,
        out_shape=[jax.ShapeDtypeStruct(shape, dtype) for shape, dtype in outs],
        in_specs=[VMEM] * len(ins) if specs is None else specs,
        out_specs=more.pop("out_specs", [VMEM] * len(outs)),
        scratch_shapes=list(scratch),
        cost_estimate=cost,
        compiler_params=pltpu.CompilerParams(vmem_limit_bytes=limit * MIB),
        **more,
    )(*ins)


def split_vectors(rows):
    high = rows.astype(BF16).astype(F32)
    return jnp.concatenate([high, rows - high], axis=0).astype(BF16)


def join_vectors(message):
    wide = message.astype(F32)
    return wide[0:8] + wide[8:16]


def start(source, target, semaphore):
    copy = pltpu.make_async_copy(source, target, semaphore)
    copy.start()
    return copy


def fold(value):
    return value[0:8] + value[8:16]


def layer_norm_rows(value, cotangent, gain_row):
    grad_out = cotangent.astype(F32)
    scaled = grad_out * gain_row
    mean = jnp.sum(value, axis=1, keepdims=True) * (1.0 / D)
    mean_scaled = jnp.sum(scaled, axis=1, keepdims=True) * (1.0 / D)
    centred = value - mean
    var = jnp.sum(centred * centred, axis=1, keepdims=True) * (1.0 / D)
    cross = jnp.sum(scaled * centred, axis=1, keepdims=True) * (1.0 / D)
    rstd = lax.rsqrt(var + 1e-05)
    slope = rstd * rstd * cross
    d_pre = rstd * ((scaled - mean_scaled) - centred * slope)
    return d_pre, grad_out * (centred * rstd), grad_out


def backward_kernel(
    ctx_hbm,
    res_hbm,
    cot_hbm,
    weight_hbm,
    bias,
    gain,
    master_hbm,
    first_hbm,
    second_hbm,
    dres_hbm,
    send,
    keep,
    packed,
    ctx,
    res,
    cot,
    weight,
    dres,
    pre,
    state,
    sums,
    token_sems,
    weight_sem,
    state_sems,
    out_sems,
):
    blocks = D // BLOCK
    tokens = ((ctx_hbm, ctx), (res_hbm, res), (cot_hbm, cot))

    def rows_of_block(b):
        return pl.ds(b * BLOCK, BLOCK)

    def fetch(b, n):
        source, target = tokens[n]
        rows = rows_of_block(b)
        return start(source.at[rows], target.at[rows], token_sems.at[n, b])

    def product(b):
        pre[b % 2] = jnp.dot(
            ctx[rows_of_block(b), :], weight[...], preferred_element_type=F32
        )

    first_ctx = fetch(0, 0)
    weight_copy = start(weight_hbm, weight, weight_sem)
    copies = [[first_ctx, fetch(0, 1), fetch(0, 2)]]
    bias_row = bias[...]
    gain_row = gain[...]
    sums[...] = jnp.zeros_like(sums)
    weight_copy.wait()
    copies[0][0].wait()
    copies += [[fetch(b, n) for n in range(3)] for b in range(1, blocks)]
    product(0)
    outs = []
    for b in range(blocks):
        copies[b][1].wait()
        copies[b][2].wait()
        if b == 2:
            shards = (master_hbm, first_hbm, second_hbm)
            state_copies = [start(r, state.at[n], state_sems.at[n]) for n, r in enumerate(shards)]
        if b + 1 < blocks:
            copies[b + 1][0].wait()
            product(b + 1)
        for i in range(0, BLOCK, 64):
            totals = None
            for j in range(i, i + 64, 16):
                rows = pl.ds(b * BLOCK + j, 16)
                value = pre[b % 2, j : j + 16, :] + res[rows, :].astype(F32) + bias_row
                parts = layer_norm_rows(value, cot[rows, :], gain_row)
                dres[rows, :] = parts[0].astype(BF16)
                parts = [fold(part) for part in parts]
                totals = parts if totals is None else [p + q for p, q in zip(totals, parts)]
            for k in range(3):
                sums[k] += totals[k]
        rows = rows_of_block(b)
        outs.append(start(dres.at[rows], dres_hbm.at[rows], out_sems.at[b]))

    for n, copy in enumerate(state_copies):
        copy.wait()
        for half in range(2):
            packed[half, n] = state[n, 128 * half : 128 * half + 128, :].astype(BF16)

    core = lax.axis_index("c")

    def grad_rows(which, half):
        columns = [
            pl.ds(pl.multiple_of(256 * shard + 128 * which, 128), 128)
            for shard in (2 * half, 2 * half + 1)
        ]
        left = jnp.concatenate([ctx[:, cols] for cols in columns], axis=1)
        return lax.dot_general(
            left, dres[...], (((0,), (0,)), ((), ())), preferred_element_type=F32
        ).astype(BF16)

    for half in range(2):
        send[256 * half : 256 * half + 256, :] = grad_rows(1 - core, half)
    for half in range(2):
        keep[256 * half : 256 * half + 256, :] = grad_rows(core, half)
    total = [jnp.sum(sums[k], axis=0, keepdims=True) for k in range(3)]
    message = split_vectors(jnp.concatenate(total + [jnp.zeros((5, D), F32)], axis=0))
    send[512:528, :] = message
    keep[512:528, :] = message
    for copy in outs:
        copy.wait()


def backward(context, residual_in, cotangent, weight, bias, gain, master, first, second):
    whole = pltpu.VMEM((D, D), BF16)
    return call(
        backward_kernel,
        [((D, D), BF16), ((528, D), BF16), ((528, D), BF16), ((2, 3, 128, D), BF16)],
        (context, residual_in, cotangent, weight, bias, gain, master, first, second),
        specs=[HBM] * 4 + [VMEM] * 2 + [HBM] * 3,
        out_specs=[HBM, VMEM, VMEM, VMEM],
        scratch=[whole] * 5
        + [
            pltpu.VMEM((2, BLOCK, D), F32),
            pltpu.VMEM((3, 256, D), F32),
            pltpu.VMEM((3, 8, D), F32),
            DMA((3, D // BLOCK)),
            DMA,
            DMA((3,)),
            DMA((D // BLOCK,)),
        ],
        cost=pl.CostEstimate(flops=4 * D**3, bytes_accessed=0, transcendentals=0),
        limit=58,
    )


def context_kernel(dres, weight, out, token):
    token[...] = jnp.zeros_like(token)
    out[...] = lax.dot_general(
        dres[...], weight[...], (((1,), (1,)), ((), ())), preferred_element_type=F32
    ).astype(BF16)


def context_grad(d_resid, weight):
    block = pl.BlockSpec((BLOCK, D), lambda i: (i, 0))
    return call(
        context_kernel,
        [((D, D), BF16), ((8, 128), F32)],
        (d_resid, weight),
        specs=[block, pl.BlockSpec((D, D), lambda i: (0, 0))],
        out_specs=[block, pl.BlockSpec((8, 128), lambda i: (0, 0))],
        grid=(D // BLOCK,),
        cost=pl.CostEstimate(flops=2 * D**3, bytes_accessed=0, transcendentals=0),
        limit=24,
    )


def pass_kernel(packed, out):
    pass


def core_kernel(keep, got, out):
    message = split_vectors(join_vectors(keep[512:528, :]) + join_vectors(got[512:528, :]))
    for j in range(16):
        rows = slice(ROWS * j, ROWS * (j + 1))
        total = (keep[rows, :].astype(F32) + got[rows, :].astype(F32)).astype(BF16)
        for k in range(8):
            out[j, ROWS * k : ROWS * (k + 1), :] = total[:, 128 * k : 128 * (k + 1)]
        k = j % 8
        out[j, 256:PIECE, :] = message[:, 128 * k : 128 * (k + 1)]


def sum_kernel(n, copies, got, *rest):
    out = rest[-1]
    for at in range(0, 256, 32):
        rows = slice(at, at + 32)
        total = got[0, rows, :].astype(F32)
        for j in range(1, n):
            total = total + got[j, rows, :].astype(F32)
        total = total.astype(BF16)
        for j in range(copies):
            out[j, rows, :] = total
    total = join_vectors(got[0, 256:PIECE, :])
    for j in range(1, n):
        total = total + join_vectors(got[j, 256:PIECE, :])
    message = split_vectors(total)
    for j in range(copies):
        out[j, 256:PIECE, :] = message


def step_of(grad, first, second, param, decay):
    first_new = beta_one * first + (1.0 - beta_one) * grad
    second_new = beta_two * second + (1.0 - beta_two) * (grad * grad)
    scale = second_new * lax.rsqrt(second_new) + adam_eps
    inverse = pl.reciprocal(scale, approx=True)
    inverse = inverse * (2.0 - scale * inverse)
    update = first_new * inverse
    return first_new, second_new, update if decay == 0.0 else update + decay * param


def stage_kernel(
    near, near_other, far, far_other, master, first, second, state, shards, weight_sq
):
    core, z = lax.axis_index("c"), lax.axis_index("z")
    side = 1 - 2 * core
    shards[0] = master[...]
    shards[1] = first[...]
    shards[2] = second[...]
    own = pl.ds(pl.multiple_of(256 * z, 256), 256)
    for n, shard in enumerate((master, first, second)):
        state[n, own, :] = shard[...].astype(BF16)
    blocks = (
        (z - side, core, near.at[core]),
        (z - side, 1 - core, near.at[1 - core]),
        (z + side, 1 - core, near_other.at[1 - core]),
        (z + side, core, near_other.at[core]),
        (z + 2, core, far),
        (z + 2, 1 - core, far_other),
    )
    for shard, half, block in blocks:
        at = 256 * lax.rem(shard + 4, 4) + 128 * half
        state[:, pl.ds(pl.multiple_of(at, 128), 128), :] = block[...]

    def square(i, total):
        wide = state[0, pl.ds(pl.multiple_of(i * 32, 32), 32), :].astype(F32)
        wide = wide * wide
        return total + (fold(wide[0:16]) + fold(wide[16:32]))

    weight_sq[...] = lax.fori_loop(0, D // 32, square, jnp.zeros((8, D), F32), unroll=2)


def half_kernel(pieces, weight_sq, token, half):
    squares = jnp.zeros((16, 128), F32)
    for j in range(16):
        for k in range(8):
            block = pieces[j, ROWS * k : ROWS * (k + 1), :]
            half[ROWS * j : ROWS * (j + 1), 128 * k : 128 * (k + 1)] = block
            wide = block.astype(F32)
            wide = wide * wide
            squares = squares + (wide[0:16] + wide[16:32])
    vectors = jnp.concatenate(
        [join_vectors(pieces[k, 256:PIECE, :]) for k in range(8)], axis=1
    )
    row = jnp.full((1, D), jnp.sum(squares), F32)
    half[512:528, :] = split_vectors(
        jnp.concatenate([vectors[0:3], row, jnp.zeros((4, D), F32)], axis=0)
    )


def lamb_kernel(
    mine,
    others,
    state_hbm,
    shard_hbm,
    weight_sq,
    vectors,
    vec_first,
    vec_second,
    weight_hbm,
    master_hbm,
    first_hbm,
    second_hbm,
    vec_out,
    vec_first_out,
    vec_second_out,
    update,
    own_update,
    sums,
    shard_out,
    weight,
    state,
    shard,
    state_sems,
    shard_sem,
    out_sems,
):
    shard_copy = start(shard_hbm, shard, shard_sem)
    state_copies = []
    for n in range(4):
        rows = pl.ds(256 * n, 256)
        state_copies.append(start(state_hbm.at[:, rows], state.at[:, rows], state_sems.at[n]))
    core, z = lax.axis_index("c"), lax.axis_index("z")
    halves = (mine, others)
    tails = [join_vectors(half[512:528, :]) for half in halves]
    grad_vectors = tails[0][0:3]
    total = jnp.sqrt(
        tails[0][3:4, 0:1]
        + tails[1][3:4, 0:1]
        + jnp.full((1, 1), jnp.sum(grad_vectors * grad_vectors), F32)
    )
    factor = 1.0 / jnp.maximum(1.0, total / max_norm)
    sums[...] = jnp.zeros_like(sums)
    shard_copy.wait()

    for which, half in enumerate(halves):
        side = lax.rem(core + which, 2)

        def own(i, carry):
            rows = pl.ds(pl.multiple_of(i * 16 + 128 * side, 16), 16)
            at = pl.ds(pl.multiple_of(128 * z + i * 16, 16), 16)
            first_new, second_new, u = step_of(
                half[at, :].astype(F32) * factor,
                shard[1, rows, :],
                shard[2, rows, :],
                shard[0, rows, :],
                decay_rate,
            )
            shard_out[1, rows, :] = first_new
            shard_out[2, rows, :] = second_new
            own_update[rows, :] = u
            return carry

        lax.fori_loop(0, 8, own, 0, unroll=2)
    outs = [
        start(shard_out.at[n], ref, out_sems.at[n])
        for n, ref in ((1, first_hbm), (2, second_hbm))
    ]

    for shard_at in range(4):
        state_copies[shard_at].wait()
        for which, half in enumerate(halves):
            side = lax.rem(core + which, 2)

            def full(i, total):
                part = pl.multiple_of(i * 16, 16)
                at = pl.ds(pl.multiple_of(256 * shard_at + 128 * side + part, 16), 16)
                g = half[pl.ds(128 * shard_at + part, 16), :].astype(F32) * factor
                w, m, v = [state[n, at, :].astype(F32) for n in range(3)]
                u = step_of(g, m, v, w, decay_rate)[2]
                update[at, :] = u
                return total + fold(u * u)

            sums[side] = lax.fori_loop(0, 8, full, sums[side], unroll=2)

    update_sq = jnp.full((1, 1), jnp.sum(sums[0] + sums[1]), F32)
    norm = jnp.sqrt(jnp.full((1, 1), jnp.sum(weight_sq[...]), F32))
    rate = learn_rate * (norm / jnp.sqrt(update_sq + 1e-06))

    def finish_shard(i, carry):
        rows = pl.ds(pl.multiple_of(i * 32, 32), 32)
        shard_out[0, rows, :] = shard[0, rows, :] - rate * own_update[rows, :]
        return carry

    lax.fori_loop(0, 8, finish_shard, 0, unroll=2)
    outs.append(start(shard_out.at[0], master_hbm, out_sems.at[0]))
    for part in range(4):

        def finish(i, carry):
            rows = pl.ds(pl.multiple_of(part * 256 + i * 32, 32), 32)
            weight[rows, :] = (state[0, rows, :].astype(F32) - rate * update[rows, :]).astype(BF16)
            return carry

        lax.fori_loop(0, 8, finish, 0, unroll=2)
        rows = pl.ds(part * 256, 256)
        outs.append(start(weight.at[rows], weight_hbm.at[rows], out_sems.at[3 + part]))

    params = vectors[...]
    first_new, second_new, u = step_of(
        grad_vectors * factor, vec_first[...], vec_second[...], params, 0.0
    )
    trust = jnp.sqrt(jnp.sum(params * params, axis=1, keepdims=True)) / jnp.sqrt(
        jnp.sum(u * u, axis=1, keepdims=True) + 1e-06
    )
    vec_out[...] = params - learn_rate * trust * u
    vec_first_out[...] = first_new
    vec_second_out[...] = second_new
    for copy in outs:
        copy.wait()


def on_device(
    context,
    residual_in,
    cotangent,
    weight,
    master,
    moment_first,
    moment_second,
    out_bias,
    ln_gain,
    ln_shift,
    vector_first,
    vector_second,
):
    d_resid, send, keep, packed = backward(
        context,
        residual_in,
        cotangent,
        weight,
        out_bias.reshape(1, D),
        ln_gain.reshape(1, D),
        master,
        moment_first,
        moment_second,
    )
    got = other_core(send)
    (packed,) = call(
        pass_kernel,
        [((2, 3, 128, D), BF16)],
        (packed,),
        specs=[ANY],
        out_specs=[ANY],
        input_output_aliases={0: 0},
        cost=pl.CostEstimate(flops=4 * D**3, bytes_accessed=0, transcendentals=0),
        limit=58,
    )
    near = next_shard(packed)
    d_context, token = context_grad(d_resid, weight)

    (pieces,) = call(core_kernel, [((16, PIECE, 128), BF16)], (keep, got), limit=8)
    pieces = exchange(pieces, PLANE)
    (pieces,) = call(
        functools.partial(sum_kernel, 16, 4),
        [((4, PIECE, 128), BF16)],
        (pieces,),
        limit=8,
    )
    far = next_shard(lax.dynamic_index_in_dim(near, lax.axis_index("c"), keepdims=False))
    pieces = exchange(pieces, "z")
    (pieces,) = call(
        functools.partial(sum_kernel, 4, 16),
        [((16, PIECE, 128), BF16)],
        (pieces,),
        limit=8,
    )
    near_other, far_other = other_core(near), other_core(far)
    pieces = exchange(pieces, PLANE)
    shard = ((256, D), F32)
    rows = ((3, D), F32)
    state, shards, weight_sq = call(
        stage_kernel,
        [((3, D, D), BF16), ((3, 256, D), F32), ((8, D), F32)],
        (near, near_other, far, far_other, master, moment_first, moment_second),
        cost=pl.CostEstimate(flops=D**3, bytes_accessed=16 * MIB, transcendentals=0),
        limit=58,
    )
    (mine,) = call(
        half_kernel,
        [((528, D), BF16)],
        (pieces, weight_sq, token),
        specs=[VMEM, ANY, ANY],
        limit=8,
    )
    others = other_core(mine)

    vectors = jnp.stack([out_bias, ln_gain, ln_shift])
    outs = call(
        lamb_kernel,
        [((D, D), BF16), shard, shard, shard, rows, rows, rows],
        (mine, others, state, shards, weight_sq, vectors, vector_first, vector_second),
        specs=[VMEM] * 2 + [HBM] * 2 + [VMEM] * 4,
        out_specs=[HBM] * 4 + [VMEM] * 3,
        scratch=[
            pltpu.VMEM((D, D), F32),
            pltpu.VMEM((256, D), F32),
            pltpu.VMEM((2, 8, D), F32),
            pltpu.VMEM((3, 256, D), F32),
            pltpu.VMEM((D, D), BF16),
            pltpu.VMEM((3, D, D), BF16),
            pltpu.VMEM((3, 256, D), F32),
            DMA((4,)),
            DMA,
            DMA((7,)),
        ],
        limit=50,
    )
    return (d_context, d_resid, *outs)


def solution(mesh):
    mesh = Mesh(mesh.devices.reshape(4, 4, 2, 4), AXES)
    tokens, copied, shard = P(AXES, None), P(), P("z", None)
    return jax.shard_map(
        on_device,
        mesh=mesh,
        in_specs=(tokens,) * 3 + (copied,) + (shard,) * 3 + (copied,) * 5,
        out_specs=(tokens, tokens, copied) + (shard,) * 3 + (copied,) * 3,
        check_vma=False,
    )
```

time: 106 us -> 95.7 us (0.903)
  waiting for transfers between devices: 25.9 us -> 16 us
  local copies, waits for them, and re-layouts: 9.46 us -> 5.31 us
  Pallas kernels: 35.1 us -> 38.8 us
    all_to_all x2, waiting for transfers between devices: 14.1 us -> 4.04 us  [exchange(): return lax.all_to_all(value, axes, split_axis=0, concat_axis=0, tiled=True)]
    unnamed x24 -> x20, local copies, waits for them, and re-layouts: 8.53 us -> 3.25 us
    pallas_call x6 -> x9, Pallas kernels: 35.1 us -> 38.8 us  [call(): pl.pallas_call(kernel, out_shape=[jax.ShapeDtypeStruct(shape, dtype) for...]
    squeeze x1, local copies, waits for them, and re-layouts: 0.93 us -> 2.06 us  [on_device(): lax.dynamic_index_in_dim(near, lax.axis_index('c'), keepdims=False)]
  transfers between devices with their start and end apart: 8 -> 8, of which waited for: 5 -> 3; matrix products, arithmetic and copies ran while one was open for 1% -> 2% of each run, Pallas kernels for 6% -> 15%
where the time goes in v3:
time: 95.7 us; the launch traced here: 95.2 us
  Pallas kernels  38.8 us (41%)
  starting transfers between devices  26 us (27%)
  waiting for transfers between devices  16 us (17%)
  blocking collectives  8.37 us (9%)
  local copies, waits for them, and re-layouts  5.31 us (6%)
    pallas_call x9, Pallas kernels, call(): pl.pallas_call(kernel, out_shape=[jax.ShapeDtypeStruct(shape, dtype) for...  38.8 us
    ppermute x6, starting transfers between devices, permute(): return lax.ppermute(value, AXES, pairs)  13.1 us
    all_to_all x2, starting transfers between devices, exchange(): return lax.all_to_all(value, axes, split_axis=0, concat_axis=0, tiled=True)  12.9 us
    ppermute x6, waiting for transfers between devices, permute(): return lax.ppermute(value, AXES, pairs)  12 us
    all_to_all x1, blocking collectives, exchange(): return lax.all_to_all(value, axes, split_axis=0, concat_axis=0, tiled=True)  8.37 us
    all_to_all x2, waiting for transfers between devices, exchange(): return lax.all_to_all(value, axes, split_axis=0, concat_axis=0, tiled=True)  4.04 us
    unnamed x20, local copies, waits for them, and re-layouts  3.25 us
    squeeze x1, local copies, waits for them, and re-layouts, on_device(): lax.dynamic_index_in_dim(near, lax.axis_index('c'), keepdims=False)  2.06 us
  transfers between devices with their start and end apart: 8, of which 3 were waited for; matrix products, arithmetic and copies ran while one was open for 2% of the time, Pallas kernels for 15%

profile of v3, /device:TPU:1, one launch (start us, length us, event | category | flops | bytes accessed | tf_op | source)
XLA Modules:
  0.0 95.2 jit_solution(2417563871375206172)
XLA Ops:
  0.6 13.3 %shard_map.187 = (bf16[1024,1024]{1,0:T(8,128)(2,1)}, bf16[528,1024]{1,0:T(8,128)(2,1)}, bf16[528,1024]{1,0:T(8,128)(2,1)}, bf16[2,3,128,1024]{3,2,1,0:T(8,128)(2,1)}) custom-call(bf16[1024,1024]{1,0:T(8,128)(2,1)} %ctx_hbm.1, bf16[1024,1024]{1,0:T(8,128)(2,1)} %res_hbm.1, bf16[1024,1024]{1,0:T(8,128)(2,1)} %cot_hbm.1, bf16[1024,1024]{1,0:T(8,128)(2,1)} %weight.1, ...), custom_call_target="tpu_custom_call" | custom-call | flops 4294967296 | tf_op jit(solution)/shard_map/pallas_call | solution.py:60
  13.9 1.5 %collective-permute-start = (bf16[528,1024]{1,0:T(8,128)(2,1)}, bf16[528,1024]{1,0:T(8,128)(2,1)S(1)}, u32[]{:S(2)}, u32[]{:S(2)}) collective-permute-start(bf16[528,1024]{1,0:T(8,128)(2,1)} %get-tuple-element.28), channel_id=1, source_target_pairs={{0,4},{1,5},{2,6},{3,7},{4,0},{5,1},{6,2},{7,3},{8,12},{9,13},{10,... | collective-permute-start | bytes 3244040 | tf_op jit(solution)/shard_map/ppermute | solution.py:44
  15.4 0.0 copy-start
  15.4 3.8 %collective-permute-start.1 = (bf16[2,3,128,1024]{3,2,1,0:T(8,128)(2,1)}, bf16[2,3,128,1024]{3,2,1,0:T(8,128)(2,1)}, u32[]{:S(2)}, u32[]{:S(2)}) collective-permute-start(bf16[2,3,128,1024]{3,2,1,0:T(8,128)(2,1)} %shard_map.192), channel_id=1, source_target_pairs={{0,1},{1,2},{2,3},{3,0},{4,7},{5,4},{6,5},{7,6},{8,9},{9,10},{10,1... | collective-permute-start | bytes 4718600 | tf_op jit(solution)/shard_map/ppermute | solution.py:44
  19.3 0.0 collective-permute-done.got
  19.3 0.0 copy-done
  19.3 1.2 %shard_map.189 = bf16[16,272,128]{2,1,0:T(8,128)(2,1)} custom-call(bf16[528,1024]{1,0:T(8,128)(2,1)S(1)} %copy-done, bf16[528,1024]{1,0:T(8,128)(2,1)S(1)} %collective-permute-done.got), custom_call_target="tpu_custom_call" | custom-call | tf_op jit(solution)/shard_map/pallas_call | solution.py:60
  20.5 6.8 %all-to-all-start = ((bf16[16,272,128]{2,1,0:T(8,128)(2,1)}), bf16[16,272,128]{2,1,0:T(8,128)(2,1)S(1)}, u32[]{:S(2)}, u32[]{:S(2)}) async-start(bf16[16,272,128]{2,1,0:T(8,128)(2,1)} %shard_map.189), calls=%async_computation | async-start | bytes 2228224 | tf_op jit(solution)/shard_map/all_to_all | solution.py:56
  27.3 9.7 %collective-permute-done.1.near = bf16[2,3,128,1024]{3,2,1,0:T(8,128)(2,1)} collective-permute-done((bf16[2,3,128,1024]{3,2,1,0:T(8,128)(2,1)}, bf16[2,3,128,1024]{3,2,1,0:T(8,128)(2,1)}, u32[]{:S(2)}, u32[]{:S(2)}) %collective-permute-start.1) | collective-permute-done | bytes 1572896 | tf_op jit(solution)/shard_map/ppermute | solution.py:44
  37.0 2.1 %dynamic-slice_bitcast_fusion = bf16[3,128,1024]{2,1,0:T(8,128)(2,1)} fusion(bf16[2,3,128,1024]{3,2,1,0:T(8,128)(2,1)} %collective-permute-done.1.near, s32[]{:T(128)S(6)} %select_n.4), kind=kLoop, calls=%fused_computation | loop fusion | bytes 1572868 | tf_op jit(solution)/shard_map/jit(dynamic_index_in_dim)/squeeze | solution.py:516
  39.0 3.3 %collective-permute-start.3 = (bf16[3,128,1024]{2,1,0:T(8,128)(2,1)}, bf16[3,128,1024]{2,1,0:T(8,128)(2,1)}, u32[]{:S(2)}, u32[]{:S(2)}) collective-permute-start(bf16[3,128,1024]{2,1,0:T(8,128)(2,1)} %dynamic-slice_bitcast_fusion), channel_id=1, source_target_pairs={{0,1},{1,2},{2,3},{3,0},{4,7},{5,4},{6,5},{7,6},{8,9},{9,10},{10,1... | collective-permute-start | bytes 2359304 | tf_op jit(solution)/shard_map/ppermute | solution.py:44
  42.3 0.0 collective-permute-start.2
  42.3 4.0 %all-to-all-done.got = bf16[16,272,128]{2,1,0:T(8,128)(2,1)S(1)} async-done(((bf16[16,272,128]{2,1,0:T(8,128)(2,1)}), bf16[16,272,128]{2,1,0:T(8,128)(2,1)S(1)}, u32[]{:S(2)}, u32[]{:S(2)}) %all-to-all-start) | async-done | bytes 1114144 | tf_op jit(solution)/shard_map/all_to_all | solution.py:56
  46.4 0.2 shard_map.190
  46.5 8.4 %all_to_all.15.got = bf16[4,272,128]{2,1,0:T(8,128)(2,1)S(1)} all-to-all(bf16[4,272,128]{2,1,0:T(8,128)(2,1)S(1)} %shard_map.190), channel_id=1, replica_groups=mesh['x'=4,'y'=4,'c'=2,'z'=4] {'z'}, dimensions={0} | all-to-all | bytes 557056 | tf_op jit(solution)/shard_map/all_to_all | solution.py:56
  54.9 0.0 copy-start.4
  54.9 1.1 %shard_map.191 = bf16[16,272,128]{2,1,0:T(8,128)(2,1)} custom-call(bf16[4,272,128]{2,1,0:T(8,128)(2,1)S(1)} %all_to_all.15.got), custom_call_target="tpu_custom_call" | custom-call | tf_op jit(solution)/shard_map/pallas_call | solution.py:60
  56.0 6.2 %all-to-all-start.2 = ((bf16[16,272,128]{2,1,0:T(8,128)(2,1)}), bf16[16,272,128]{2,1,0:T(8,128)(2,1)S(1)}, u32[]{:S(2)}, u32[]{:S(2)}) async-start(bf16[16,272,128]{2,1,0:T(8,128)(2,1)} %shard_map.191), calls=%async_computation.2 | async-start | bytes 2228224 | tf_op jit(solution)/shard_map/all_to_all | solution.py:56
  62.1 0.0 collective-permute-done.3.far
  62.2 3.1 %collective-permute-start.4 = (bf16[3,128,1024]{2,1,0:T(8,128)(2,1)}, bf16[3,128,1024]{2,1,0:T(8,128)(2,1)S(1)}, u32[]{:S(2)}, u32[]{:S(2)}) collective-permute-start(bf16[3,128,1024]{2,1,0:T(8,128)(2,1)} %collective-permute-done.3.far), channel_id=1, source_target_pairs={{0,4},{1,5},{2,6},{3,7},{4,0},{5,1},{6,2},{7,3},{8,12},{9,13},{10,... | collective-permute-start | bytes 2359304 | tf_op jit(solution)/shard_map/ppermute | solution.py:44
  65.3 0.0 copy-done.4
  65.3 0.0 copy-start.5
  65.3 1.6 %copy-done.5 = bf16[1024,1024]{1,0:T(8,128)(2,1)S(1)} copy-done((bf16[1024,1024]{1,0:T(8,128)(2,1)S(1)}, bf16[1024,1024]{1,0:T(8,128)(2,1)}, u32[]{:S(2)}) %copy-start.5) | copy-done | bytes 2097176
  66.9 3.8 %shard_map.188 = (bf16[1024,1024]{1,0:T(8,128)(2,1)}, f32[8,128]{1,0:T(8,128)S(1)}) custom-call(bf16[1024,1024]{1,0:T(8,128)(2,1)S(1)} %copy-done.5, bf16[1024,1024]{1,0:T(8,128)(2,1)S(1)} %copy-done.4), custom_call_target="tpu_custom_call" | custom-call | flops 2147483648 | tf_op jit(solution)/shard_map/pallas_call | solution.py:60
  70.7 0.0 collective-permute-done.4.far_other
  70.7 0.0 copy-start.6
  70.7 0.0 collective-permute-done.2.near_other
  70.7 0.9 copy-done.6
  71.6 0.0 copy-start.7
  71.6 0.0 copy-start.8
  71.6 0.0 copy-start.9
  71.6 0.0 copy-start.2
  71.6 0.0 copy-start.3
  71.6 8.1 %shard_map.193 = (bf16[3,1024,1024]{2,1,0:T(8,128)(2,1)}, f32[3,256,1024]{2,1,0:T(8,128)}, f32[8,1024]{1,0:T(8,128)}) custom-call(bf16[2,3,128,1024]{3,2,1,0:T(8,128)(2,1)} %collective-permute-done.1.near, bf16[2,3,128,1024]{3,2,1,0:T(8,128)(2,1)} %collective-permute-done.2.near_other, bf16[3,128,1024]{2,1,0:T(8,128)(2,1)} %collective-permute-done.3.far, ...), custom_call_target="tpu_custom_call" | custom-call | flops 1073741824 | bytes 16777216 | tf_op jit(solution)/shard_map/pallas_call | solution.py:60
  79.8 0.0 all-to-all-done.2.pieces
  79.8 0.0 copy-start.1
  79.8 0.8 copy-done.1
  80.5 0.4 shard_map.194.mine
  81.0 1.3 %collective-permute-start.5 = (bf16[528,1024]{1,0:T(8,128)(2,1)S(1)}, bf16[528,1024]{1,0:T(8,128)(2,1)S(1)}, u32[]{:S(2)}, u32[]{:S(2)}) collective-permute-start(bf16[528,1024]{1,0:T(8,128)(2,1)S(1)} %shard_map.194.mine), channel_id=1, source_target_pairs={{0,4},{1,5},{2,6},{3,7},{4,0},{5,1},{6,2},{7,3},{8,12},{9,13},{10,... | collective-permute-start | bytes 3244040 | tf_op jit(solution)/shard_map/ppermute | solution.py:44
  82.2 0.0 copy-done.7
  82.2 0.0 copy-done.8
  82.2 0.0 copy-done.9
  82.3 2.3 %collective-permute-done.5.others = bf16[528,1024]{1,0:T(8,128)(2,1)S(1)} collective-permute-done((bf16[528,1024]{1,0:T(8,128)(2,1)S(1)}, bf16[528,1024]{1,0:T(8,128)(2,1)S(1)}, u32[]{:S(2)}, u32[]{:S(2)}) %collective-permute-start.5) | collective-permute-done | bytes 1081376 | tf_op jit(solution)/shard_map/ppermute | solution.py:44
  84.6 0.0 copy-done.2
  84.6 0.0 copy-done.3
  84.6 10.7 %shard_map.195 = (bf16[1024,1024]{1,0:T(8,128)(2,1)}, f32[256,1024]{1,0:T(8,128)}, f32[256,1024]{1,0:T(8,128)}, f32[256,1024]{1,0:T(8,128)}, f32[3,1024]{1,0:T(4...) custom-call(bf16[528,1024]{1,0:T(8,128)(2,1)S(1)} %shard_map.194.mine, bf16[528,1024]{1,0:T(8,128)(2,1)S(1)} %collective-permute-done.5.others, ...), custom_call_target="tpu_custom_call" | custom-call | tf_op jit(solution)/shard_map/pallas_call | solution.py:60
  (2 shorter events, 0.0 us)
Async XLA Ops:
  13.9 5.3 %collective-permute-start = (bf16[528,1024]{1,0:T(8,128)(2,1)}, bf16[528,1024]{1,0:T(8,128)(2,1)S(1)}, u32[]{:S(2)}, u32[]{:S(2)}) collective-permute-start(bf16[528,1024]{1,0:T(8,128)(2,1)} %get-tuple-element.28), channel_id=1, source_target_pairs={{0,4},{1,5},{2,6},{3,7},{4,0},{5,1},{6,2},{7,3},{8,12},{9,13},{10,... | collective-permute-start | bytes 3244040 | tf_op jit(solution)/shard_map/ppermute | solution.py:44
  15.4 3.9 %copy-start = (bf16[528,1024]{1,0:T(8,128)(2,1)S(1)}, bf16[528,1024]{1,0:T(8,128)(2,1)}, u32[]{:S(2)}) copy-start(bf16[528,1024]{1,0:T(8,128)(2,1)} %get-tuple-element.27.keep) | copy-start | bytes 3244036
  15.4 21.5 %collective-permute-start.1 = (bf16[2,3,128,1024]{3,2,1,0:T(8,128)(2,1)}, bf16[2,3,128,1024]{3,2,1,0:T(8,128)(2,1)}, u32[]{:S(2)}, u32[]{:S(2)}) collective-permute-start(bf16[2,3,128,1024]{3,2,1,0:T(8,128)(2,1)} %shard_map.192), channel_id=1, source_target_pairs={{0,1},{1,2},{2,3},{3,0},{4,7},{5,4},{6,5},{7,6},{8,9},{9,10},{10,1... | collective-permute-start | bytes 4718600 | tf_op jit(solution)/shard_map/ppermute | solution.py:44
  20.5 25.8 %all-to-all-start = ((bf16[16,272,128]{2,1,0:T(8,128)(2,1)}), bf16[16,272,128]{2,1,0:T(8,128)(2,1)S(1)}, u32[]{:S(2)}, u32[]{:S(2)}) async-start(bf16[16,272,128]{2,1,0:T(8,128)(2,1)} %shard_map.189), calls=%async_computation | async-start | bytes 2228224 | tf_op jit(solution)/shard_map/all_to_all | solution.py:56
  39.0 23.1 %collective-permute-start.3 = (bf16[3,128,1024]{2,1,0:T(8,128)(2,1)}, bf16[3,128,1024]{2,1,0:T(8,128)(2,1)}, u32[]{:S(2)}, u32[]{:S(2)}) collective-permute-start(bf16[3,128,1024]{2,1,0:T(8,128)(2,1)} %dynamic-slice_bitcast_fusion), channel_id=1, source_target_pairs={{0,1},{1,2},{2,3},{3,0},{4,7},{5,4},{6,5},{7,6},{8,9},{9,10},{10,1... | collective-permute-start | bytes 2359304 | tf_op jit(solution)/shard_map/ppermute | solution.py:44
  42.3 28.4 %collective-permute-start.2 = (bf16[2,3,128,1024]{3,2,1,0:T(8,128)(2,1)}, bf16[2,3,128,1024]{3,2,1,0:T(8,128)(2,1)}, u32[]{:S(2)}, u32[]{:S(2)}) collective-permute-start(bf16[2,3,128,1024]{3,2,1,0:T(8,128)(2,1)} %collective-permute-done.1.near), channel_id=1, source_target_pairs={{0,4},{1,5},{2,6},{3,7},{4,0},{5,1},{6,2},{7,3},{8,12},{9,13},{10,... | collective-permute-start | bytes 4718600 | tf_op jit(solution)/shard_map/ppermute | solution.py:44
  54.9 10.4 %copy-start.4 = (bf16[1024,1024]{1,0:T(8,128)(2,1)S(1)}, bf16[1024,1024]{1,0:T(8,128)(2,1)}, u32[]{:S(2)}) copy-start(bf16[1024,1024]{1,0:T(8,128)(2,1)} %weight.1) | copy-start | bytes 6291460
  56.0 23.8 %all-to-all-start.2 = ((bf16[16,272,128]{2,1,0:T(8,128)(2,1)}), bf16[16,272,128]{2,1,0:T(8,128)(2,1)S(1)}, u32[]{:S(2)}, u32[]{:S(2)}) async-start(bf16[16,272,128]{2,1,0:T(8,128)(2,1)} %shard_map.191), calls=%async_computation.2 | async-start | bytes 2228224 | tf_op jit(solution)/shard_map/all_to_all | solution.py:56
  62.2 8.6 %collective-permute-start.4 = (bf16[3,128,1024]{2,1,0:T(8,128)(2,1)}, bf16[3,128,1024]{2,1,0:T(8,128)(2,1)S(1)}, u32[]{:S(2)}, u32[]{:S(2)}) collective-permute-start(bf16[3,128,1024]{2,1,0:T(8,128)(2,1)} %collective-permute-done.3.far), channel_id=1, source_target_pairs={{0,4},{1,5},{2,6},{3,7},{4,0},{5,1},{6,2},{7,3},{8,12},{9,13},{10,... | collective-permute-start | bytes 2359304 | tf_op jit(solution)/shard_map/ppermute | solution.py:44
  65.3 1.6 %copy-start.5 = (bf16[1024,1024]{1,0:T(8,128)(2,1)S(1)}, bf16[1024,1024]{1,0:T(8,128)(2,1)}, u32[]{:S(2)}) copy-start(bf16[1024,1024]{1,0:T(8,128)(2,1)} %get-tuple-element.17.dres) | copy-start | bytes 6291460
  70.7 0.9 copy-start.6
  71.6 10.6 %copy-start.7 = (f32[1024]{0:T(1024)S(1)}, f32[1024]{0:T(1024)}, u32[]{:S(2)}) copy-start(f32[1024]{0:T(1024)} %param.19) | copy-start | bytes 12292
  71.6 10.6 %copy-start.8 = (f32[1024]{0:T(1024)S(1)}, f32[1024]{0:T(1024)}, u32[]{:S(2)}) copy-start(f32[1024]{0:T(1024)} %param.20) | copy-start | bytes 12292
  71.6 10.6 %copy-start.9 = (f32[1024]{0:T(1024)S(1)}, f32[1024]{0:T(1024)}, u32[]{:S(2)}) copy-start(f32[1024]{0:T(1024)} %param.21) | copy-start | bytes 12292
  71.6 13.0 %copy-start.2 = (f32[3,1024]{1,0:T(4,128)S(1)}, f32[3,1024]{1,0:T(4,128)}, u32[]{:S(2)}) copy-start(f32[3,1024]{1,0:T(4,128)} %vec_first.1) | copy-start | bytes 36868
  71.6 13.0 %copy-start.3 = (f32[3,1024]{1,0:T(4,128)S(1)}, f32[3,1024]{1,0:T(4,128)}, u32[]{:S(2)}) copy-start(f32[3,1024]{1,0:T(4,128)} %vec_second.1) | copy-start | bytes 36868
  79.8 0.8 copy-start.1
  81.0 3.6 %collective-permute-start.5 = (bf16[528,1024]{1,0:T(8,128)(2,1)S(1)}, bf16[528,1024]{1,0:T(8,128)(2,1)S(1)}, u32[]{:S(2)}, u32[]{:S(2)}) collective-permute-start(bf16[528,1024]{1,0:T(8,128)(2,1)S(1)} %shard_map.194.mine), channel_id=1, source_target_pairs={{0,4},{1,5},{2,6},{3,7},{4,0},{5,1},{6,2},{7,3},{8,12},{9,13},{10,... | collective-permute-start | bytes 3244040 | tf_op jit(solution)/shard_map/ppermute | solution.py:44

commit v4 on v3

--- a/solution.py
+++ b/solution.py
@@ -16,6 +16,7 @@
 
 D = 1024
 BLOCK = 256
+carried = (1.0, beta_one, beta_two)
 F32 = jnp.float32
 BF16 = jnp.bfloat16
 MIB = 1024 * 1024
@@ -114,6 +115,9 @@
     first_hbm,
     second_hbm,
     dres_hbm,
+    send_hbm,
+    keep_hbm,
+    packed_hbm,
     send,
     keep,
     packed,
@@ -183,7 +187,9 @@
     for n, copy in enumerate(state_copies):
         copy.wait()
         for half in range(2):
-            packed[half, n] = state[n, 128 * half : 128 * half + 128, :].astype(BF16)
+            rows = slice(128 * half, 128 * half + 128)
+            packed[half, n] = (state[n, rows, :] * carried[n]).astype(BF16)
+    outs.append(start(packed, packed_hbm, out_sems.at[blocks]))
 
     core = lax.axis_index("c")
 
@@ -197,14 +203,15 @@
             left, dres[...], (((0,), (0,)), ((), ())), preferred_element_type=F32
         ).astype(BF16)
 
-    for half in range(2):
-        send[256 * half : 256 * half + 256, :] = grad_rows(1 - core, half)
-    for half in range(2):
-        keep[256 * half : 256 * half + 256, :] = grad_rows(core, half)
     total = [jnp.sum(sums[k], axis=0, keepdims=True) for k in range(3)]
     message = split_vectors(jnp.concatenate(total + [jnp.zeros((5, D), F32)], axis=0))
-    send[512:528, :] = message
-    keep[512:528, :] = message
+    halves = ((send, send_hbm, 1 - core), (keep, keep_hbm, core))
+    for n, (half, target, which) in enumerate(halves):
+        half[512:528, :] = message
+        for part in range(2):
+            half[256 * part : 256 * part + 256, :] = grad_rows(which, part)
+            rows = pl.ds(256 * part, 256 + 16 * part)
+            outs.append(start(half.at[rows], target.at[rows], out_sems.at[blocks + 1 + 2 * n + part]))
     for copy in outs:
         copy.wait()
 
@@ -216,8 +223,10 @@
         [((D, D), BF16), ((528, D), BF16), ((528, D), BF16), ((2, 3, 128, D), BF16)],
         (context, residual_in, cotangent, weight, bias, gain, master, first, second),
         specs=[HBM] * 4 + [VMEM] * 2 + [HBM] * 3,
-        out_specs=[HBM, VMEM, VMEM, VMEM],
-        scratch=[whole] * 5
+        out_specs=[HBM] * 4,
+        scratch=[pltpu.VMEM((528, D), BF16)] * 2
+        + [pltpu.VMEM((2, 3, 128, D), BF16)]
+        + [whole] * 5
         + [
             pltpu.VMEM((2, BLOCK, D), F32),
             pltpu.VMEM((3, 256, D), F32),
@@ -225,7 +234,7 @@
             DMA((3, D // BLOCK)),
             DMA,
             DMA((3,)),
-            DMA((D // BLOCK,)),
+            DMA((D // BLOCK + 5,)),
         ],
         cost=pl.CostEstimate(flops=4 * D**3, bytes_accessed=0, transcendentals=0),
         limit=58,
@@ -253,8 +262,12 @@
     )
 
 
-def pass_kernel(packed, out):
+def pass_kernel(value, out):
     pass
+
+
+def token_kernel(value, token):
+    token[...] = jnp.zeros_like(token)
 
 
 def core_kernel(keep, got, out):
@@ -297,16 +310,14 @@
 
 
 def stage_kernel(
-    near, near_other, far, far_other, master, first, second, state, shards, weight_sq
+    near, near_other, far, far_other, master, first, second, w_out, m_out, v_out, weight_sq
 ):
     core, z = lax.axis_index("c"), lax.axis_index("z")
     side = 1 - 2 * core
-    shards[0] = master[...]
-    shards[1] = first[...]
-    shards[2] = second[...]
     own = pl.ds(pl.multiple_of(256 * z, 256), 256)
-    for n, shard in enumerate((master, first, second)):
-        state[n, own, :] = shard[...].astype(BF16)
+    state = (w_out, m_out, v_out)
+    for out, shard, scale in zip(state, (master, first, second), carried):
+        out[own, :] = (shard[...] * scale).astype(BF16)
     blocks = (
         (z - side, core, near.at[core]),
         (z - side, 1 - core, near.at[1 - core]),
@@ -317,17 +328,19 @@
     )
     for shard, half, block in blocks:
         at = 256 * lax.rem(shard + 4, 4) + 128 * half
-        state[:, pl.ds(pl.multiple_of(at, 128), 128), :] = block[...]
+        rows = pl.ds(pl.multiple_of(at, 128), 128)
+        for n, out in enumerate(state):
+            out[rows, :] = block[n]
 
     def square(i, total):
-        wide = state[0, pl.ds(pl.multiple_of(i * 32, 32), 32), :].astype(F32)
+        wide = w_out[pl.ds(pl.multiple_of(i * 32, 32), 32), :].astype(F32)
         wide = wide * wide
         return total + (fold(wide[0:16]) + fold(wide[16:32]))
 
     weight_sq[...] = lax.fori_loop(0, D // 32, square, jnp.zeros((8, D), F32), unroll=2)
 
 
-def half_kernel(pieces, weight_sq, token, half):
+def half_kernel(pieces, weight_sq, half):
     squares = jnp.zeros((16, 128), F32)
     for j in range(16):
         for k in range(8):
@@ -348,12 +361,17 @@
 def lamb_kernel(
     mine,
     others,
-    state_hbm,
-    shard_hbm,
+    w_in,
+    m_in,
+    v_in,
+    master,
+    first,
+    second,
     weight_sq,
     vectors,
     vec_first,
     vec_second,
+    token,
     weight_hbm,
     master_hbm,
     first_hbm,
@@ -366,17 +384,8 @@
     sums,
     shard_out,
     weight,
-    state,
-    shard,
-    state_sems,
-    shard_sem,
     out_sems,
 ):
-    shard_copy = start(shard_hbm, shard, shard_sem)
-    state_copies = []
-    for n in range(4):
-        rows = pl.ds(256 * n, 256)
-        state_copies.append(start(state_hbm.at[:, rows], state.at[:, rows], state_sems.at[n]))
     core, z = lax.axis_index("c"), lax.axis_index("z")
     halves = (mine, others)
     tails = [join_vectors(half[512:528, :]) for half in halves]
@@ -387,9 +396,9 @@
         + jnp.full((1, 1), jnp.sum(grad_vectors * grad_vectors), F32)
     )
     factor = 1.0 / jnp.maximum(1.0, total / max_norm)
+    first_rate = (1.0 - beta_one) * factor
+    second_rate = (1.0 - beta_two) * (factor * factor)
     sums[...] = jnp.zeros_like(sums)
-    shard_copy.wait()
-
     for which, half in enumerate(halves):
         side = lax.rem(core + which, 2)
 
@@ -398,9 +407,9 @@
             at = pl.ds(pl.multiple_of(128 * z + i * 16, 16), 16)
             first_new, second_new, u = step_of(
                 half[at, :].astype(F32) * factor,
-                shard[1, rows, :],
-                shard[2, rows, :],
-                shard[0, rows, :],
+                first[rows, :],
+                second[rows, :],
+                master[rows, :],
                 decay_rate,
             )
             shard_out[1, rows, :] = first_new
@@ -415,20 +424,21 @@
     ]
 
     for shard_at in range(4):
-        state_copies[shard_at].wait()
         for which, half in enumerate(halves):
             side = lax.rem(core + which, 2)
 
             def full(i, total):
                 part = pl.multiple_of(i * 16, 16)
                 at = pl.ds(pl.multiple_of(256 * shard_at + 128 * side + part, 16), 16)
-                g = half[pl.ds(128 * shard_at + part, 16), :].astype(F32) * factor
-                w, m, v = [state[n, at, :].astype(F32) for n in range(3)]
-                u = step_of(g, m, v, w, decay_rate)[2]
+                g = half[pl.ds(128 * shard_at + part, 16), :].astype(F32)
+                w, m, v = [ref[at, :].astype(F32) for ref in (w_in, m_in, v_in)]
+                second_new = v + second_rate * (g * g)
+                scale = second_new * lax.rsqrt(second_new) + adam_eps
+                u = (m + first_rate * g) * pl.reciprocal(scale, approx=True) + decay_rate * w
                 update[at, :] = u
                 return total + fold(u * u)
 
-            sums[side] = lax.fori_loop(0, 8, full, sums[side], unroll=2)
+            sums[side] = lax.fori_loop(0, 8, full, sums[side], unroll=4)
 
     update_sq = jnp.full((1, 1), jnp.sum(sums[0] + sums[1]), F32)
     norm = jnp.sqrt(jnp.full((1, 1), jnp.sum(weight_sq[...]), F32))
@@ -436,7 +446,7 @@
 
     def finish_shard(i, carry):
         rows = pl.ds(pl.multiple_of(i * 32, 32), 32)
-        shard_out[0, rows, :] = shard[0, rows, :] - rate * own_update[rows, :]
+        shard_out[0, rows, :] = master[rows, :] - rate * own_update[rows, :]
         return carry
 
     lax.fori_loop(0, 8, finish_shard, 0, unroll=2)
@@ -445,7 +455,7 @@
 
         def finish(i, carry):
             rows = pl.ds(pl.multiple_of(part * 256 + i * 32, 32), 32)
-            weight[rows, :] = (state[0, rows, :].astype(F32) - rate * update[rows, :]).astype(BF16)
+            weight[rows, :] = (w_in[rows, :].astype(F32) - rate * update[rows, :]).astype(BF16)
             return carry
 
         lax.fori_loop(0, 8, finish, 0, unroll=2)
@@ -513,7 +523,8 @@
         (pieces,),
         limit=8,
     )
-    far = next_shard(lax.dynamic_index_in_dim(near, lax.axis_index("c"), keepdims=False))
+    half_at = lax.axis_index("c") + token[0, 0].astype(jnp.int32)
+    far = next_shard(lax.dynamic_index_in_dim(near, half_at, keepdims=False))
     pieces = exchange(pieces, "z")
     (pieces,) = call(
         functools.partial(sum_kernel, 4, 16),
@@ -525,28 +536,47 @@
     pieces = exchange(pieces, PLANE)
     shard = ((256, D), F32)
     rows = ((3, D), F32)
-    state, shards, weight_sq = call(
+    *state, weight_sq = call(
         stage_kernel,
-        [((3, D, D), BF16), ((3, 256, D), F32), ((8, D), F32)],
+        [((D, D), BF16)] * 3 + [((8, D), F32)],
         (near, near_other, far, far_other, master, moment_first, moment_second),
         cost=pl.CostEstimate(flops=D**3, bytes_accessed=16 * MIB, transcendentals=0),
-        limit=58,
+        limit=53,
     )
     (mine,) = call(
         half_kernel,
         [((528, D), BF16)],
-        (pieces, weight_sq, token),
-        specs=[VMEM, ANY, ANY],
+        (pieces, weight_sq),
+        specs=[VMEM, ANY],
         limit=8,
     )
     others = other_core(mine)
+    (token,) = call(
+        token_kernel,
+        [((8, 128), F32)],
+        (mine,),
+        specs=[ANY],
+        cost=pl.CostEstimate(flops=30 * D**3, bytes_accessed=0, transcendentals=0),
+        limit=16,
+    )
 
     vectors = jnp.stack([out_bias, ln_gain, ln_shift])
     outs = call(
         lamb_kernel,
         [((D, D), BF16), shard, shard, shard, rows, rows, rows],
-        (mine, others, state, shards, weight_sq, vectors, vector_first, vector_second),
-        specs=[VMEM] * 2 + [HBM] * 2 + [VMEM] * 4,
+        (
+            mine,
+            others,
+            *state,
+            master,
+            moment_first,
+            moment_second,
+            weight_sq,
+            vectors,
+            vector_first,
+            vector_second,
+            token,
+        ),
         out_specs=[HBM] * 4 + [VMEM] * 3,
         scratch=[
             pltpu.VMEM((D, D), F32),
@@ -554,13 +584,9 @@
             pltpu.VMEM((2, 8, D), F32),
             pltpu.VMEM((3, 256, D), F32),
             pltpu.VMEM((D, D), BF16),
-            pltpu.VMEM((3, D, D), BF16),
-            pltpu.VMEM((3, 256, D), F32),
-            DMA((4,)),
-            DMA,
             DMA((7,)),
         ],
-        limit=50,
+        limit=28,
     )
     return (d_context, d_resid, *outs)
 

time: 95.7 us -> 90.2 us (0.943)
  Pallas kernels: 38.8 us -> 32.3 us
  starting transfers between devices: 26 us -> 29.1 us
  waiting for transfers between devices: 16 us -> 13.4 us
    pallas_call x9 -> x10, Pallas kernels: 38.8 us -> 32.3 us  [call(): pl.pallas_call(kernel, out_shape=[jax.ShapeDtypeStruct(shape, dtype) for...]
    ppermute x6, waiting for transfers between devices: 12 us -> 7.1 us  [permute(): return lax.ppermute(value, AXES, pairs)]
    ppermute x6, starting transfers between devices: 13.1 us -> 16 us  [permute(): return lax.ppermute(value, AXES, pairs)]
    all_to_all x2, waiting for transfers between devices: 4.04 us -> 6.26 us  [exchange(): return lax.all_to_all(value, axes, split_axis=0, concat_axis=0, tiled=True)]
    unnamed x20 -> x32, local copies, waits for them, and re-layouts: 3.25 us -> 2.53 us
  transfers between devices with their start and end apart: 8 -> 8, of which waited for: 3 -> 5; matrix products, arithmetic and copies ran while one was open for 2% -> 3% of each run, Pallas kernels for 15% -> 15%
where the time goes in v4:
time: 90.2 us; the launch traced here: 89.8 us
  Pallas kernels  32.3 us (36%)
  starting transfers between devices  29.1 us (32%)
  waiting for transfers between devices  13.4 us (15%)
  blocking collectives  8.19 us (9%)
  local copies, waits for them, and re-layouts  5.11 us (6%)
  between operations  1.66 us (2%)
    pallas_call x10, Pallas kernels, call(): pl.pallas_call(kernel, out_shape=[jax.ShapeDtypeStruct(shape, dtype) for...  32.3 us
    ppermute x6, starting transfers between devices, permute(): return lax.ppermute(value, AXES, pairs)  16 us
    all_to_all x2, starting transfers between devices, exchange(): return lax.all_to_all(value, axes, split_axis=0, concat_axis=0, tiled=True)  13.1 us
    all_to_all x1, blocking collectives, exchange(): return lax.all_to_all(value, axes, split_axis=0, concat_axis=0, tiled=True)  8.19 us
    ppermute x6, waiting for transfers between devices, permute(): return lax.ppermute(value, AXES, pairs)  7.1 us
    all_to_all x2, waiting for transfers between devices, exchange(): return lax.all_to_all(value, axes, split_axis=0, concat_axis=0, tiled=True)  6.26 us
    unnamed x32, local copies, waits for them, and re-layouts  2.53 us
    squeeze x1, local copies, waits for them, and re-layouts, on_device(): far = next_shard(lax.dynamic_index_in_dim(near, half_at, keepdims=False))  2.06 us
  transfers between devices with their start and end apart: 8, of which 5 were waited for; matrix products, arithmetic and copies ran while one was open for 3% of the time, Pallas kernels for 15%

profile of v4, /device:TPU:1, one launch (start us, length us, event | category | flops | bytes accessed | tf_op | source)
XLA Modules:
  0.0 89.8 jit_solution(8016478403045046985)
XLA Ops:
  0.6 12.3 %shard_map.187 = (bf16[1024,1024]{1,0:T(8,128)(2,1)}, bf16[528,1024]{1,0:T(8,128)(2,1)}, bf16[528,1024]{1,0:T(8,128)(2,1)}, bf16[2,3,128,1024]{3,2,1,0:T(8,128)(2,1)}) custom-call(bf16[1024,1024]{1,0:T(8,128)(2,1)} %ctx_hbm.1, bf16[1024,1024]{1,0:T(8,128)(2,1)} %res_hbm.1, bf16[1024,1024]{1,0:T(8,128)(2,1)} %cot_hbm.1, bf16[1024,1024]{1,0:T(8,128)(2,1)} %weight.1, ...), custom_call_target="tpu_custom_call" | custom-call | flops 4294967296 | tf_op jit(solution)/shard_map/pallas_call | solution.py:61
  13.0 1.5 %collective-permute-start = (bf16[528,1024]{1,0:T(8,128)(2,1)}, bf16[528,1024]{1,0:T(8,128)(2,1)S(1)}, u32[]{:S(2)}, u32[]{:S(2)}) collective-permute-start(bf16[528,1024]{1,0:T(8,128)(2,1)} %get-tuple-element.29), channel_id=1, source_target_pairs={{0,4},{1,5},{2,6},{3,7},{4,0},{5,1},{6,2},{7,3},{8,12},{9,13},{10,... | collective-permute-start | bytes 3244040 | tf_op jit(solution)/shard_map/ppermute | solution.py:45
  14.5 3.8 %collective-permute-start.1 = (bf16[2,3,128,1024]{3,2,1,0:T(8,128)(2,1)}, bf16[2,3,128,1024]{3,2,1,0:T(8,128)(2,1)}, u32[]{:S(2)}, u32[]{:S(2)}) collective-permute-start(bf16[2,3,128,1024]{3,2,1,0:T(8,128)(2,1)} %shard_map.192), channel_id=1, source_target_pairs={{0,1},{1,2},{2,3},{3,0},{4,7},{5,4},{6,5},{7,6},{8,9},{9,10},{10,1... | collective-permute-start | bytes 4718600 | tf_op jit(solution)/shard_map/ppermute | solution.py:45
  18.3 0.0 collective-permute-done.got
  18.3 0.0 copy-done.6
  18.3 1.3 %shard_map.189 = bf16[16,272,128]{2,1,0:T(8,128)(2,1)} custom-call(bf16[528,1024]{1,0:T(8,128)(2,1)S(1)} %copy-done.6, bf16[528,1024]{1,0:T(8,128)(2,1)S(1)} %collective-permute-done.got), custom_call_target="tpu_custom_call" | custom-call | tf_op jit(solution)/shard_map/pallas_call | solution.py:61
  19.6 6.9 %all-to-all-start = ((bf16[16,272,128]{2,1,0:T(8,128)(2,1)}), bf16[16,272,128]{2,1,0:T(8,128)(2,1)S(1)}, u32[]{:S(2)}, u32[]{:S(2)}) async-start(bf16[16,272,128]{2,1,0:T(8,128)(2,1)} %shard_map.189), calls=%async_computation | async-start | bytes 2228224 | tf_op jit(solution)/shard_map/all_to_all | solution.py:57
  26.5 0.0 copy-done.9
  26.5 0.0 copy-start.10
  26.5 1.6 %copy-done.10 = bf16[1024,1024]{1,0:T(8,128)(2,1)S(1)} copy-done((bf16[1024,1024]{1,0:T(8,128)(2,1)S(1)}, bf16[1024,1024]{1,0:T(8,128)(2,1)}, u32[]{:S(2)}) %copy-start.10) | copy-done | bytes 2097176
  28.1 3.8 %shard_map.188 = (bf16[1024,1024]{1,0:T(8,128)(2,1)}, f32[8,128]{1,0:T(8,128)S(1)}) custom-call(bf16[1024,1024]{1,0:T(8,128)(2,1)S(1)} %copy-done.10, bf16[1024,1024]{1,0:T(8,128)(2,1)S(1)} %copy-done.9), custom_call_target="tpu_custom_call" | custom-call | flops 2147483648 | tf_op jit(solution)/shard_map/pallas_call | solution.py:61
  31.9 0.5 slice.3
  33.1 2.9 %collective-permute-done.1.near = bf16[2,3,128,1024]{3,2,1,0:T(8,128)(2,1)} collective-permute-done((bf16[2,3,128,1024]{3,2,1,0:T(8,128)(2,1)}, bf16[2,3,128,1024]{3,2,1,0:T(8,128)(2,1)}, u32[]{:S(2)}, u32[]{:S(2)}) %collective-permute-start.1) | collective-permute-done | bytes 1572896 | tf_op jit(solution)/shard_map/ppermute | solution.py:45
  36.0 2.1 %dynamic-slice_bitcast_fusion = bf16[3,128,1024]{2,1,0:T(8,128)(2,1)} fusion(bf16[2,3,128,1024]{3,2,1,0:T(8,128)(2,1)} %collective-permute-done.1.near, s32[]{:T(128)S(6)} %select_n.4), kind=kLoop, calls=%fused_computation | loop fusion | bytes 1572868 | tf_op jit(solution)/shard_map/jit(dynamic_index_in_dim)/squeeze | solution.py:527
  38.0 3.3 %collective-permute-start.3 = (bf16[3,128,1024]{2,1,0:T(8,128)(2,1)}, bf16[3,128,1024]{2,1,0:T(8,128)(2,1)S(1)}, u32[]{:S(2)}, u32[]{:S(2)}) collective-permute-start(bf16[3,128,1024]{2,1,0:T(8,128)(2,1)} %dynamic-slice_bitcast_fusion), channel_id=1, source_target_pairs={{0,1},{1,2},{2,3},{3,0},{4,7},{5,4},{6,5},{7,6},{8,9},{9,10},{10,1... | collective-permute-start | bytes 2359304 | tf_op jit(solution)/shard_map/ppermute | solution.py:45
  41.3 0.0 collective-permute-start.2
  41.3 4.2 %all-to-all-done.got = bf16[16,272,128]{2,1,0:T(8,128)(2,1)S(1)} async-done(((bf16[16,272,128]{2,1,0:T(8,128)(2,1)}), bf16[16,272,128]{2,1,0:T(8,128)(2,1)S(1)}, u32[]{:S(2)}, u32[]{:S(2)}) %all-to-all-start) | async-done | bytes 1114144 | tf_op jit(solution)/shard_map/all_to_all | solution.py:57
  45.6 0.2 shard_map.190
  45.7 8.2 %all_to_all.15.got = bf16[4,272,128]{2,1,0:T(8,128)(2,1)S(1)} all-to-all(bf16[4,272,128]{2,1,0:T(8,128)(2,1)S(1)} %shard_map.190), channel_id=1, replica_groups=mesh['x'=4,'y'=4,'c'=2,'z'=4] {'z'}, dimensions={0} | all-to-all | bytes 557056 | tf_op jit(solution)/shard_map/all_to_all | solution.py:57
  53.9 1.2 %shard_map.191 = bf16[16,272,128]{2,1,0:T(8,128)(2,1)} custom-call(bf16[4,272,128]{2,1,0:T(8,128)(2,1)S(1)} %all_to_all.15.got), custom_call_target="tpu_custom_call" | custom-call | tf_op jit(solution)/shard_map/pallas_call | solution.py:61
  55.1 6.2 %all-to-all-start.2 = ((bf16[16,272,128]{2,1,0:T(8,128)(2,1)}), bf16[16,272,128]{2,1,0:T(8,128)(2,1)S(1)}, u32[]{:S(2)}, u32[]{:S(2)}) async-start(bf16[16,272,128]{2,1,0:T(8,128)(2,1)} %shard_map.191), calls=%async_computation.2 | async-start | bytes 2228224 | tf_op jit(solution)/shard_map/all_to_all | solution.py:57
  61.3 0.0 collective-permute-done.3.far
  61.3 3.3 %collective-permute-start.4 = (bf16[3,128,1024]{2,1,0:T(8,128)(2,1)S(1)}, bf16[3,128,1024]{2,1,0:T(8,128)(2,1)S(1)}, u32[]{:S(2)}, u32[]{:S(2)}) collective-permute-start(bf16[3,128,1024]{2,1,0:T(8,128)(2,1)S(1)} %collective-permute-done.3.far), channel_id=1, source_target_pairs={{0,4},{1,5},{2,6},{3,7},{4,0},{5,1},{6,2},{7,3},{8,12},{9,13},{10,... | collective-permute-start | bytes 2359304 | tf_op jit(solution)/shard_map/ppermute | solution.py:45
  64.6 0.0 copy-done.13
  64.6 0.0 copy-done.14
  64.6 0.0 copy-done.15
  64.6 0.0 collective-permute-done.2.near_other
  64.6 0.0 copy-start.11
  64.7 1.9 %collective-permute-done.4.far_other = bf16[3,128,1024]{2,1,0:T(8,128)(2,1)S(1)} collective-permute-done((bf16[3,128,1024]{2,1,0:T(8,128)(2,1)S(1)}, bf16[3,128,1024]{2,1,0:T(8,128)(2,1)S(1)}, u32[]{:S(2)}, u32[]{:S(2)}) %collective-permute-start.4) | collective-permute-done | bytes 786464 | tf_op jit(solution)/shard_map/ppermute | solution.py:45
  66.5 0.0 copy-done.11
  66.5 0.9 copy-done.12
  67.4 6.7 %shard_map.193 = (bf16[1024,1024]{1,0:T(8,128)(2,1)}, bf16[1024,1024]{1,0:T(8,128)(2,1)}, bf16[1024,1024]{1,0:T(8,128)(2,1)}, f32[8,1024]{1,0:T(8,128)S(1)}) custom-call(bf16[2,3,128,1024]{3,2,1,0:T(8,128)(2,1)} %collective-permute-done.1.near, bf16[2,3,128,1024]{3,2,1,0:T(8,128)(2,1)} %copy-done.11, bf16[3,128,1024]{2,1,0:T(8,128)(2,1)S(1)} %collective-permute-done.3.far, ...), custom_call_target="tpu_custom_call" | custom-call | flops 1073741824 | bytes 16777216 | tf_op jit(solution)/shard_map/pallas_call | solution.py:61
  74.1 2.0 %all-to-all-done.2.pieces = bf16[16,272,128]{2,1,0:T(8,128)(2,1)S(1)} async-done(((bf16[16,272,128]{2,1,0:T(8,128)(2,1)}), bf16[16,272,128]{2,1,0:T(8,128)(2,1)S(1)}, u32[]{:S(2)}, u32[]{:S(2)}) %all-to-all-start.2) | async-done | bytes 1114144 | tf_op jit(solution)/shard_map/all_to_all | solution.py:57
  76.1 0.4 shard_map.194.value.mine
  76.5 0.0 copy-start
  76.6 0.0 copy-start.1
  76.6 0.0 copy-start.2
  76.6 0.0 copy-start.3
  76.6 0.0 copy-start.7
  76.6 0.0 copy-start.8
  76.6 4.1 %collective-permute-start.5 = (bf16[528,1024]{1,0:T(8,128)(2,1)S(1)}, bf16[528,1024]{1,0:T(8,128)(2,1)S(1)}, u32[]{:S(2)}, u32[]{:S(2)}) collective-permute-start(bf16[528,1024]{1,0:T(8,128)(2,1)S(1)} %shard_map.194.value.mine), channel_id=1, source_target_pairs={{0,4},{1,5},{2,6},{3,7},{4,0},{5,1},{6,2},{7,3},{8,12},{9,13},{10,... | collective-permute-start | bytes 3244040 | tf_op jit(solution)/shard_map/ppermute | solution.py:45
  80.7 2.3 %collective-permute-done.5.others = bf16[528,1024]{1,0:T(8,128)(2,1)S(1)} collective-permute-done((bf16[528,1024]{1,0:T(8,128)(2,1)S(1)}, bf16[528,1024]{1,0:T(8,128)(2,1)S(1)}, u32[]{:S(2)}, u32[]{:S(2)}) %collective-permute-start.5) | collective-permute-done | bytes 1081376 | tf_op jit(solution)/shard_map/ppermute | solution.py:45
  83.0 0.0 copy-done
  83.0 0.0 copy-done.4
  83.0 0.0 copy-done.5
  83.1 0.0 copy-done.7
  83.1 0.0 copy-done.8
  83.1 6.5 %shard_map.196 = (bf16[1024,1024]{1,0:T(8,128)(2,1)}, f32[256,1024]{1,0:T(8,128)}, f32[256,1024]{1,0:T(8,128)}, f32[256,1024]{1,0:T(8,128)}, f32[3,1024]{1,0:T(4...) custom-call(bf16[528,1024]{1,0:T(8,128)(2,1)S(1)} %shard_map.194.value.mine, ...), custom_call_target="tpu_custom_call" | custom-call | tf_op jit(solution)/shard_map/pallas_call | solution.py:61
  (14 shorter events, 0.0 us)
Async XLA Ops:
  13.0 5.3 %collective-permute-start = (bf16[528,1024]{1,0:T(8,128)(2,1)}, bf16[528,1024]{1,0:T(8,128)(2,1)S(1)}, u32[]{:S(2)}, u32[]{:S(2)}) collective-permute-start(bf16[528,1024]{1,0:T(8,128)(2,1)} %get-tuple-element.29), channel_id=1, source_target_pairs={{0,4},{1,5},{2,6},{3,7},{4,0},{5,1},{6,2},{7,3},{8,12},{9,13},{10,... | collective-permute-start | bytes 3244040 | tf_op jit(solution)/shard_map/ppermute | solution.py:45
  14.5 3.8 %copy-start.6 = (bf16[528,1024]{1,0:T(8,128)(2,1)S(1)}, bf16[528,1024]{1,0:T(8,128)(2,1)}, u32[]{:S(2)}) copy-start(bf16[528,1024]{1,0:T(8,128)(2,1)} %get-tuple-element.28.keep) | copy-start | bytes 3244036
  14.5 21.5 %collective-permute-start.1 = (bf16[2,3,128,1024]{3,2,1,0:T(8,128)(2,1)}, bf16[2,3,128,1024]{3,2,1,0:T(8,128)(2,1)}, u32[]{:S(2)}, u32[]{:S(2)}) collective-permute-start(bf16[2,3,128,1024]{3,2,1,0:T(8,128)(2,1)} %shard_map.192), channel_id=1, source_target_pairs={{0,1},{1,2},{2,3},{3,0},{4,7},{5,4},{6,5},{7,6},{8,9},{9,10},{10,1... | collective-permute-start | bytes 4718600 | tf_op jit(solution)/shard_map/ppermute | solution.py:45
  19.6 6.9 %copy-start.9 = (bf16[1024,1024]{1,0:T(8,128)(2,1)S(1)}, bf16[1024,1024]{1,0:T(8,128)(2,1)}, u32[]{:S(2)}) copy-start(bf16[1024,1024]{1,0:T(8,128)(2,1)} %weight.1) | copy-start | bytes 6291460
  19.6 26.0 %all-to-all-start = ((bf16[16,272,128]{2,1,0:T(8,128)(2,1)}), bf16[16,272,128]{2,1,0:T(8,128)(2,1)S(1)}, u32[]{:S(2)}, u32[]{:S(2)}) async-start(bf16[16,272,128]{2,1,0:T(8,128)(2,1)} %shard_map.189), calls=%async_computation | async-start | bytes 2228224 | tf_op jit(solution)/shard_map/all_to_all | solution.py:57
  26.5 1.6 %copy-start.10 = (bf16[1024,1024]{1,0:T(8,128)(2,1)S(1)}, bf16[1024,1024]{1,0:T(8,128)(2,1)}, u32[]{:S(2)}) copy-start(bf16[1024,1024]{1,0:T(8,128)(2,1)} %get-tuple-element.18.dres) | copy-start | bytes 6291460
  38.0 23.2 %collective-permute-start.3 = (bf16[3,128,1024]{2,1,0:T(8,128)(2,1)}, bf16[3,128,1024]{2,1,0:T(8,128)(2,1)S(1)}, u32[]{:S(2)}, u32[]{:S(2)}) collective-permute-start(bf16[3,128,1024]{2,1,0:T(8,128)(2,1)} %dynamic-slice_bitcast_fusion), channel_id=1, source_target_pairs={{0,1},{1,2},{2,3},{3,0},{4,7},{5,4},{6,5},{7,6},{8,9},{9,10},{10,1... | collective-permute-start | bytes 2359304 | tf_op jit(solution)/shard_map/ppermute | solution.py:45
  41.3 23.3 %collective-permute-start.2 = (bf16[2,3,128,1024]{3,2,1,0:T(8,128)(2,1)}, bf16[2,3,128,1024]{3,2,1,0:T(8,128)(2,1)S(1)}, u32[]{:S(2)}, u32[]{:S(2)}) collective-permute-start(bf16[2,3,128,1024]{3,2,1,0:T(8,128)(2,1)} %collective-permute-done.1.near), channel_id=1, source_target_pairs={{0,4},{1,5},{2,6},{3,7},{4,0},{5,1},{6,2},{7,3},{8,12},{9,13},{10,... | collective-permute-start | bytes 4718600 | tf_op jit(solution)/shard_map/ppermute | solution.py:45
  53.9 10.7 %copy-start.13 = (f32[1024]{0:T(1024)S(1)}, f32[1024]{0:T(1024)}, u32[]{:S(2)}) copy-start(f32[1024]{0:T(1024)} %param.19) | copy-start | bytes 12292
  53.9 10.7 %copy-start.14 = (f32[1024]{0:T(1024)S(1)}, f32[1024]{0:T(1024)}, u32[]{:S(2)}) copy-start(f32[1024]{0:T(1024)} %param.20) | copy-start | bytes 12292
  53.9 10.7 %copy-start.15 = (f32[1024]{0:T(1024)S(1)}, f32[1024]{0:T(1024)}, u32[]{:S(2)}) copy-start(f32[1024]{0:T(1024)} %param.21) | copy-start | bytes 12292
  55.1 21.0 %all-to-all-start.2 = ((bf16[16,272,128]{2,1,0:T(8,128)(2,1)}), bf16[16,272,128]{2,1,0:T(8,128)(2,1)S(1)}, u32[]{:S(2)}, u32[]{:S(2)}) async-start(bf16[16,272,128]{2,1,0:T(8,128)(2,1)} %shard_map.191), calls=%async_computation.2 | async-start | bytes 2228224 | tf_op jit(solution)/shard_map/all_to_all | solution.py:57
  61.3 5.2 %collective-permute-start.4 = (bf16[3,128,1024]{2,1,0:T(8,128)(2,1)S(1)}, bf16[3,128,1024]{2,1,0:T(8,128)(2,1)S(1)}, u32[]{:S(2)}, u32[]{:S(2)}) collective-permute-start(bf16[3,128,1024]{2,1,0:T(8,128)(2,1)S(1)} %collective-permute-done.3.far), channel_id=1, source_target_pairs={{0,4},{1,5},{2,6},{3,7},{4,0},{5,1},{6,2},{7,3},{8,12},{9,13},{10,... | collective-permute-start | bytes 2359304 | tf_op jit(solution)/shard_map/ppermute | solution.py:45
  64.6 1.9 %copy-start.11 = (bf16[2,3,128,1024]{3,2,1,0:T(8,128)(2,1)}, bf16[2,3,128,1024]{3,2,1,0:T(8,128)(2,1)S(1)}, u32[]{:S(2)}) copy-start(bf16[2,3,128,1024]{3,2,1,0:T(8,128)(2,1)S(1)} %collective-permute-done.2.near_other) | copy-start | bytes 4718596
  66.5 0.9 copy-start.12
  76.5 6.5 %copy-start = (f32[256,1024]{1,0:T(8,128)S(1)}, f32[256,1024]{1,0:T(8,128)}, u32[]{:S(2)}) copy-start(f32[256,1024]{1,0:T(8,128)} %master.3) | copy-start | bytes 3145732
  76.6 6.5 %copy-start.1 = (f32[256,1024]{1,0:T(8,128)S(1)}, f32[256,1024]{1,0:T(8,128)}, u32[]{:S(2)}) copy-start(f32[256,1024]{1,0:T(8,128)} %first.3) | copy-start | bytes 3145732
  76.6 6.5 %copy-start.2 = (f32[256,1024]{1,0:T(8,128)S(1)}, f32[256,1024]{1,0:T(8,128)}, u32[]{:S(2)}) copy-start(f32[256,1024]{1,0:T(8,128)} %second.3) | copy-start | bytes 3145732
  76.6 6.5 %copy-start.3 = (bf16[1024,1024]{1,0:T(8,128)(2,1)S(1)}, bf16[1024,1024]{1,0:T(8,128)(2,1)}, u32[]{:S(2)}) copy-start(bf16[1024,1024]{1,0:T(8,128)(2,1)} %get-tuple-element.33.w_in) | copy-start | bytes 6291460
  76.6 6.4 %copy-start.4 = (bf16[1024,1024]{1,0:T(8,128)(2,1)S(1)}, bf16[1024,1024]{1,0:T(8,128)(2,1)}, u32[]{:S(2)}) copy-start(bf16[1024,1024]{1,0:T(8,128)(2,1)} %get-tuple-element.34.m_in) | copy-start | bytes 6291460
  76.6 6.4 %copy-start.5 = (bf16[1024,1024]{1,0:T(8,128)(2,1)S(1)}, bf16[1024,1024]{1,0:T(8,128)(2,1)}, u32[]{:S(2)}) copy-start(bf16[1024,1024]{1,0:T(8,128)(2,1)} %get-tuple-element.35.v_in) | copy-start | bytes 6291460
  76.6 6.4 %copy-start.7 = (f32[3,1024]{1,0:T(4,128)S(1)}, f32[3,1024]{1,0:T(4,128)}, u32[]{:S(2)}) copy-start(f32[3,1024]{1,0:T(4,128)} %vec_first.1) | copy-start | bytes 36868
  76.6 6.4 %copy-start.8 = (f32[3,1024]{1,0:T(4,128)S(1)}, f32[3,1024]{1,0:T(4,128)}, u32[]{:S(2)}) copy-start(f32[3,1024]{1,0:T(4,128)} %vec_second.1) | copy-start | bytes 36868
  76.6 6.4 %collective-permute-start.5 = (bf16[528,1024]{1,0:T(8,128)(2,1)S(1)}, bf16[528,1024]{1,0:T(8,128)(2,1)S(1)}, u32[]{:S(2)}, u32[]{:S(2)}) collective-permute-start(bf16[528,1024]{1,0:T(8,128)(2,1)S(1)} %shard_map.194.value.mine), channel_id=1, source_target_pairs={{0,4},{1,5},{2,6},{3,7},{4,0},{5,1},{6,2},{7,3},{8,12},{9,13},{10,... | collective-permute-start | bytes 3244040 | tf_op jit(solution)/shard_map/ppermute | solution.py:45

commit v5 on v4

--- a/solution.py
+++ b/solution.py
@@ -21,7 +21,6 @@
 BF16 = jnp.bfloat16
 MIB = 1024 * 1024
 AXES = ("x", "y", "c", "z")
-PLANE = ("x", "y")
 VMEM = pl.BlockSpec(memory_space=pltpu.VMEM)
 ANY = pl.BlockSpec(memory_space=pl.ANY)
 HBM = pl.BlockSpec(memory_space=pltpu.HBM)
@@ -53,8 +52,33 @@
     return permute(value, lambda x, y, c, z: (x, y, c, z + 1 - 2 * c))
 
 
-def exchange(value, axes):
-    return lax.all_to_all(value, axes, split_axis=0, concat_axis=0, tiled=True)
+def order(n, core):
+    return range(n - 1, -1, -1) if core else range(n)
+
+
+def exchange(value, groups):
+    return lax.all_to_all(
+        value, AXES, split_axis=0, concat_axis=0, axis_index_groups=groups, tiled=True
+    )
+
+
+def exchange_plane(value):
+    return exchange(
+        value,
+        [[place(n // 4, n % 4, c, z) for n in order(16, c)] for c in range(2) for z in range(4)],
+    )
+
+
+def exchange_z(value):
+    return exchange(
+        value,
+        [
+            [place(x, y, c, z) for z in order(4, c)]
+            for x in range(4)
+            for y in range(4)
+            for c in range(2)
+        ],
+    )
 
 
 def call(kernel, outs, ins, specs=None, scratch=(), cost=None, limit=58, **more):
@@ -389,7 +413,7 @@
     core, z = lax.axis_index("c"), lax.axis_index("z")
     halves = (mine, others)
     tails = [join_vectors(half[512:528, :]) for half in halves]
-    grad_vectors = tails[0][0:3]
+    grad_vectors = jnp.where(core == 0, tails[0], tails[1])[0:3]
     total = jnp.sqrt(
         tails[0][3:4, 0:1]
         + tails[1][3:4, 0:1]
@@ -516,7 +540,7 @@
     d_context, token = context_grad(d_resid, weight)
 
     (pieces,) = call(core_kernel, [((16, PIECE, 128), BF16)], (keep, got), limit=8)
-    pieces = exchange(pieces, PLANE)
+    pieces = exchange_plane(pieces)
     (pieces,) = call(
         functools.partial(sum_kernel, 16, 4),
         [((4, PIECE, 128), BF16)],
@@ -525,7 +549,7 @@
     )
     half_at = lax.axis_index("c") + token[0, 0].astype(jnp.int32)
     far = next_shard(lax.dynamic_index_in_dim(near, half_at, keepdims=False))
-    pieces = exchange(pieces, "z")
+    pieces = exchange_z(pieces)
     (pieces,) = call(
         functools.partial(sum_kernel, 4, 16),
         [((16, PIECE, 128), BF16)],
@@ -533,7 +557,7 @@
         limit=8,
     )
     near_other, far_other = other_core(near), other_core(far)
-    pieces = exchange(pieces, PLANE)
+    pieces = exchange_plane(pieces)
     shard = ((256, D), F32)
     rows = ((3, D), F32)
     *state, weight_sq = call(

time: 90.2 us -> 88.3 us (0.979)
  waiting for transfers between devices: 13.4 us -> 6.08 us
  blocking collectives: 8.19 us -> 12 us
  starting transfers between devices: 29.1 us -> 30.7 us
    all_to_all x2, waiting for transfers between devices: 6.26 us -> 0.71 us  [exchange(): lax.all_to_all(value, AXES, split_axis=0, concat_axis=0, axis_index_group...]
    all_to_all x2, starting transfers between devices: 13.1 us -> 17.2 us  [exchange(): lax.all_to_all(value, AXES, split_axis=0, concat_axis=0, axis_index_group...]
    all_to_all x1, blocking collectives: 8.19 us -> 12 us  [exchange(): lax.all_to_all(value, AXES, split_axis=0, concat_axis=0, axis_index_group...]
    ppermute x6, starting transfers between devices: 16 us -> 13.5 us  [permute(): return lax.ppermute(value, AXES, pairs)]
    ppermute x6, waiting for transfers between devices: 7.1 us -> 5.37 us  [permute(): return lax.ppermute(value, AXES, pairs)]
  transfers between devices with their start and end apart: 8 -> 8, of which waited for: 5 -> 4; matrix products, arithmetic and copies ran while one was open for 3% -> 3% of each run, Pallas kernels for 15% -> 15%
where the time goes in v5:
time: 88.3 us; the launch traced here: 87.8 us
  Pallas kernels  32.3 us (37%)
  starting transfers between devices  30.7 us (35%)
  blocking collectives  12 us (14%)
  waiting for transfers between devices  6.08 us (7%)
  local copies, waits for them, and re-layouts  5.11 us (6%)
  between operations  1.63 us (2%)
    pallas_call x10, Pallas kernels, call(): pl.pallas_call(kernel, out_shape=[jax.ShapeDtypeStruct(shape, dtype) for...  32.3 us
    all_to_all x2, starting transfers between devices, exchange(): lax.all_to_all(value, AXES, split_axis=0, concat_axis=0, axis_index_group...  17.2 us
    ppermute x6, starting transfers between devices, permute(): return lax.ppermute(value, AXES, pairs)  13.5 us
    all_to_all x1, blocking collectives, exchange(): lax.all_to_all(value, AXES, split_axis=0, concat_axis=0, axis_index_group...  12 us
    ppermute x6, waiting for transfers between devices, permute(): return lax.ppermute(value, AXES, pairs)  5.37 us
    unnamed x32, local copies, waits for them, and re-layouts  2.53 us
    squeeze x1, local copies, waits for them, and re-layouts, on_device(): far = next_shard(lax.dynamic_index_in_dim(near, half_at, keepdims=False))  2.06 us
  transfers between devices with their start and end apart: 8, of which 4 were waited for; matrix products, arithmetic and copies ran while one was open for 3% of the time, Pallas kernels for 15%

profile of v5, /device:TPU:1, one launch (start us, length us, event | category | flops | bytes accessed | tf_op | source)
XLA Modules:
  0.0 87.8 jit_solution(8844166472820430987)
XLA Ops:
  0.6 12.3 %shard_map.187 = (bf16[1024,1024]{1,0:T(8,128)(2,1)}, bf16[528,1024]{1,0:T(8,128)(2,1)}, bf16[528,1024]{1,0:T(8,128)(2,1)}, bf16[2,3,128,1024]{3,2,1,0:T(8,128)(2,1)}) custom-call(bf16[1024,1024]{1,0:T(8,128)(2,1)} %ctx_hbm.1, bf16[1024,1024]{1,0:T(8,128)(2,1)} %res_hbm.1, bf16[1024,1024]{1,0:T(8,128)(2,1)} %cot_hbm.1, bf16[1024,1024]{1,0:T(8,128)(2,1)} %weight.1, ...), custom_call_target="tpu_custom_call" | custom-call | flops 4294967296 | tf_op jit(solution)/shard_map/pallas_call | solution.py:85
  13.0 1.5 %collective-permute-start = (bf16[528,1024]{1,0:T(8,128)(2,1)}, bf16[528,1024]{1,0:T(8,128)(2,1)S(1)}, u32[]{:S(2)}, u32[]{:S(2)}) collective-permute-start(bf16[528,1024]{1,0:T(8,128)(2,1)} %get-tuple-element.29), channel_id=1, source_target_pairs={{0,4},{1,5},{2,6},{3,7},{4,0},{5,1},{6,2},{7,3},{8,12},{9,13},{10,... | collective-permute-start | bytes 3244040 | tf_op jit(solution)/shard_map/ppermute | solution.py:44
  14.5 3.8 %collective-permute-start.1 = (bf16[2,3,128,1024]{3,2,1,0:T(8,128)(2,1)}, bf16[2,3,128,1024]{3,2,1,0:T(8,128)(2,1)}, u32[]{:S(2)}, u32[]{:S(2)}) collective-permute-start(bf16[2,3,128,1024]{3,2,1,0:T(8,128)(2,1)} %shard_map.192), channel_id=1, source_target_pairs={{0,1},{1,2},{2,3},{3,0},{4,7},{5,4},{6,5},{7,6},{8,9},{9,10},{10,1... | collective-permute-start | bytes 4718600 | tf_op jit(solution)/shard_map/ppermute | solution.py:44
  18.3 0.0 collective-permute-done.got
  18.3 0.0 copy-done.6
  18.3 1.3 %shard_map.189 = bf16[16,272,128]{2,1,0:T(8,128)(2,1)} custom-call(bf16[528,1024]{1,0:T(8,128)(2,1)S(1)} %copy-done.6, bf16[528,1024]{1,0:T(8,128)(2,1)S(1)} %collective-permute-done.got), custom_call_target="tpu_custom_call" | custom-call | tf_op jit(solution)/shard_map/pallas_call | solution.py:85
  19.6 8.6 %all-to-all-start = ((bf16[16,272,128]{2,1,0:T(8,128)(2,1)}), bf16[16,272,128]{2,1,0:T(8,128)(2,1)S(1)}, u32[]{:S(2)}, u32[]{:S(2)}) async-start(bf16[16,272,128]{2,1,0:T(8,128)(2,1)} %shard_map.189), calls=%async_computation | async-start | bytes 2228224 | tf_op jit(solution)/shard_map/all_to_all | solution.py:60
  28.2 0.0 copy-done.9
  28.2 0.0 copy-start.10
  28.2 1.6 %copy-done.10 = bf16[1024,1024]{1,0:T(8,128)(2,1)S(1)} copy-done((bf16[1024,1024]{1,0:T(8,128)(2,1)S(1)}, bf16[1024,1024]{1,0:T(8,128)(2,1)}, u32[]{:S(2)}) %copy-start.10) | copy-done | bytes 2097176
  29.8 3.8 %shard_map.188 = (bf16[1024,1024]{1,0:T(8,128)(2,1)}, f32[8,128]{1,0:T(8,128)S(1)}) custom-call(bf16[1024,1024]{1,0:T(8,128)(2,1)S(1)} %copy-done.10, bf16[1024,1024]{1,0:T(8,128)(2,1)S(1)} %copy-done.9), custom_call_target="tpu_custom_call" | custom-call | flops 2147483648 | tf_op jit(solution)/shard_map/pallas_call | solution.py:85
  33.6 0.5 slice.3
  34.8 1.2 %collective-permute-done.1.near = bf16[2,3,128,1024]{3,2,1,0:T(8,128)(2,1)} collective-permute-done((bf16[2,3,128,1024]{3,2,1,0:T(8,128)(2,1)}, bf16[2,3,128,1024]{3,2,1,0:T(8,128)(2,1)}, u32[]{:S(2)}, u32[]{:S(2)}) %collective-permute-start.1) | collective-permute-done | bytes 1572896 | tf_op jit(solution)/shard_map/ppermute | solution.py:44
  36.0 2.1 %dynamic-slice_bitcast_fusion = bf16[3,128,1024]{2,1,0:T(8,128)(2,1)} fusion(bf16[2,3,128,1024]{3,2,1,0:T(8,128)(2,1)} %collective-permute-done.1.near, s32[]{:T(128)S(6)} %select_n.4), kind=kLoop, calls=%fused_computation | loop fusion | bytes 1572868 | tf_op jit(solution)/shard_map/jit(dynamic_index_in_dim)/squeeze | solution.py:551
  38.0 3.3 %collective-permute-start.3 = (bf16[3,128,1024]{2,1,0:T(8,128)(2,1)}, bf16[3,128,1024]{2,1,0:T(8,128)(2,1)S(1)}, u32[]{:S(2)}, u32[]{:S(2)}) collective-permute-start(bf16[3,128,1024]{2,1,0:T(8,128)(2,1)} %dynamic-slice_bitcast_fusion), channel_id=1, source_target_pairs={{0,1},{1,2},{2,3},{3,0},{4,7},{5,4},{6,5},{7,6},{8,9},{9,10},{10,1... | collective-permute-start | bytes 2359304 | tf_op jit(solution)/shard_map/ppermute | solution.py:44
  41.3 0.0 collective-permute-start.2
  41.3 0.0 all-to-all-done.got
  41.3 0.2 shard_map.190
  41.5 12.0 %all_to_all.15.got = bf16[4,272,128]{2,1,0:T(8,128)(2,1)S(1)} all-to-all(bf16[4,272,128]{2,1,0:T(8,128)(2,1)S(1)} %shard_map.190), channel_id=1, replica_groups={{0,1,2,3},{7,6,5,4},{8,9,10,11},{15,14,13,12},{16,17,18,19},{23,22,21,2..., dimensions={0} | all-to-all | bytes 557056 | tf_op jit(solution)/shard_map/all_to_all | solution.py:60
  53.5 1.2 %shard_map.191 = bf16[16,272,128]{2,1,0:T(8,128)(2,1)} custom-call(bf16[4,272,128]{2,1,0:T(8,128)(2,1)S(1)} %all_to_all.15.got), custom_call_target="tpu_custom_call" | custom-call | tf_op jit(solution)/shard_map/pallas_call | solution.py:85
  54.7 8.5 %all-to-all-start.2 = ((bf16[16,272,128]{2,1,0:T(8,128)(2,1)}), bf16[16,272,128]{2,1,0:T(8,128)(2,1)S(1)}, u32[]{:S(2)}, u32[]{:S(2)}) async-start(bf16[16,272,128]{2,1,0:T(8,128)(2,1)} %shard_map.191), calls=%async_computation.2 | async-start | bytes 2228224 | tf_op jit(solution)/shard_map/all_to_all | solution.py:60
  63.2 0.0 collective-permute-done.3.far
  63.2 1.4 %collective-permute-start.4 = (bf16[3,128,1024]{2,1,0:T(8,128)(2,1)S(1)}, bf16[3,128,1024]{2,1,0:T(8,128)(2,1)S(1)}, u32[]{:S(2)}, u32[]{:S(2)}) collective-permute-start(bf16[3,128,1024]{2,1,0:T(8,128)(2,1)S(1)} %collective-permute-done.3.far), channel_id=1, source_target_pairs={{0,4},{1,5},{2,6},{3,7},{4,0},{5,1},{6,2},{7,3},{8,12},{9,13},{10,... | collective-permute-start | bytes 2359304 | tf_op jit(solution)/shard_map/ppermute | solution.py:44
  64.6 0.0 copy-done.13
  64.6 0.0 copy-done.14
  64.6 0.0 copy-done.15
  64.6 0.0 collective-permute-done.2.near_other
  64.6 0.0 copy-start.11
  64.7 1.9 %collective-permute-done.4.far_other = bf16[3,128,1024]{2,1,0:T(8,128)(2,1)S(1)} collective-permute-done((bf16[3,128,1024]{2,1,0:T(8,128)(2,1)S(1)}, bf16[3,128,1024]{2,1,0:T(8,128)(2,1)S(1)}, u32[]{:S(2)}, u32[]{:S(2)}) %collective-permute-start.4) | collective-permute-done | bytes 786464 | tf_op jit(solution)/shard_map/ppermute | solution.py:44
  66.5 0.0 copy-done.11
  66.5 0.9 copy-done.12
  67.4 6.7 %shard_map.193 = (bf16[1024,1024]{1,0:T(8,128)(2,1)}, bf16[1024,1024]{1,0:T(8,128)(2,1)}, bf16[1024,1024]{1,0:T(8,128)(2,1)}, f32[8,1024]{1,0:T(8,128)S(1)}) custom-call(bf16[2,3,128,1024]{3,2,1,0:T(8,128)(2,1)} %collective-permute-done.1.near, bf16[2,3,128,1024]{3,2,1,0:T(8,128)(2,1)} %copy-done.11, bf16[3,128,1024]{2,1,0:T(8,128)(2,1)S(1)} %collective-permute-done.3.far, ...), custom_call_target="tpu_custom_call" | custom-call | flops 1073741824 | bytes 16777216 | tf_op jit(solution)/shard_map/pallas_call | solution.py:85
  74.1 0.7 all-to-all-done.2.pieces
  74.8 0.4 shard_map.194.value.mine
  75.2 0.0 copy-start
  75.2 0.0 copy-start.1
  75.2 0.0 copy-start.2
  75.2 0.0 copy-start.3
  75.3 0.0 copy-start.4
  75.3 0.0 copy-start.5
  75.3 0.0 copy-start.7
  75.3 0.0 copy-start.8
  75.3 3.5 %collective-permute-start.5 = (bf16[528,1024]{1,0:T(8,128)(2,1)S(1)}, bf16[528,1024]{1,0:T(8,128)(2,1)S(1)}, u32[]{:S(2)}, u32[]{:S(2)}) collective-permute-start(bf16[528,1024]{1,0:T(8,128)(2,1)S(1)} %shard_map.194.value.mine), channel_id=1, source_target_pairs={{0,4},{1,5},{2,6},{3,7},{4,0},{5,1},{6,2},{7,3},{8,12},{9,13},{10,... | collective-permute-start | bytes 3244040 | tf_op jit(solution)/shard_map/ppermute | solution.py:44
  78.8 2.3 %collective-permute-done.5.others = bf16[528,1024]{1,0:T(8,128)(2,1)S(1)} collective-permute-done((bf16[528,1024]{1,0:T(8,128)(2,1)S(1)}, bf16[528,1024]{1,0:T(8,128)(2,1)S(1)}, u32[]{:S(2)}, u32[]{:S(2)}) %collective-permute-start.5) | collective-permute-done | bytes 1081376 | tf_op jit(solution)/shard_map/ppermute | solution.py:44
  81.1 0.0 copy-done
  81.1 0.0 copy-done.1
  81.1 0.0 copy-done.2
  81.2 6.5 %shard_map.196 = (bf16[1024,1024]{1,0:T(8,128)(2,1)}, f32[256,1024]{1,0:T(8,128)}, f32[256,1024]{1,0:T(8,128)}, f32[256,1024]{1,0:T(8,128)}, f32[3,1024]{1,0:T(4...) custom-call(bf16[528,1024]{1,0:T(8,128)(2,1)S(1)} %shard_map.194.value.mine, ...), custom_call_target="tpu_custom_call" | custom-call | tf_op jit(solution)/shard_map/pallas_call | solution.py:85
  (14 shorter events, 0.0 us)
Async XLA Ops:
  13.0 5.3 %collective-permute-start = (bf16[528,1024]{1,0:T(8,128)(2,1)}, bf16[528,1024]{1,0:T(8,128)(2,1)S(1)}, u32[]{:S(2)}, u32[]{:S(2)}) collective-permute-start(bf16[528,1024]{1,0:T(8,128)(2,1)} %get-tuple-element.29), channel_id=1, source_target_pairs={{0,4},{1,5},{2,6},{3,7},{4,0},{5,1},{6,2},{7,3},{8,12},{9,13},{10,... | collective-permute-start | bytes 3244040 | tf_op jit(solution)/shard_map/ppermute | solution.py:44
  14.5 3.8 %copy-start.6 = (bf16[528,1024]{1,0:T(8,128)(2,1)S(1)}, bf16[528,1024]{1,0:T(8,128)(2,1)}, u32[]{:S(2)}) copy-start(bf16[528,1024]{1,0:T(8,128)(2,1)} %get-tuple-element.28.keep) | copy-start | bytes 3244036
  14.5 21.5 %collective-permute-start.1 = (bf16[2,3,128,1024]{3,2,1,0:T(8,128)(2,1)}, bf16[2,3,128,1024]{3,2,1,0:T(8,128)(2,1)}, u32[]{:S(2)}, u32[]{:S(2)}) collective-permute-start(bf16[2,3,128,1024]{3,2,1,0:T(8,128)(2,1)} %shard_map.192), channel_id=1, source_target_pairs={{0,1},{1,2},{2,3},{3,0},{4,7},{5,4},{6,5},{7,6},{8,9},{9,10},{10,1... | collective-permute-start | bytes 4718600 | tf_op jit(solution)/shard_map/ppermute | solution.py:44
  19.6 8.6 %copy-start.9 = (bf16[1024,1024]{1,0:T(8,128)(2,1)S(1)}, bf16[1024,1024]{1,0:T(8,128)(2,1)}, u32[]{:S(2)}) copy-start(bf16[1024,1024]{1,0:T(8,128)(2,1)} %weight.1) | copy-start | bytes 6291460
  19.6 21.8 %all-to-all-start = ((bf16[16,272,128]{2,1,0:T(8,128)(2,1)}), bf16[16,272,128]{2,1,0:T(8,128)(2,1)S(1)}, u32[]{:S(2)}, u32[]{:S(2)}) async-start(bf16[16,272,128]{2,1,0:T(8,128)(2,1)} %shard_map.189), calls=%async_computation | async-start | bytes 2228224 | tf_op jit(solution)/shard_map/all_to_all | solution.py:60
  28.2 1.6 %copy-start.10 = (bf16[1024,1024]{1,0:T(8,128)(2,1)S(1)}, bf16[1024,1024]{1,0:T(8,128)(2,1)}, u32[]{:S(2)}) copy-start(bf16[1024,1024]{1,0:T(8,128)(2,1)} %get-tuple-element.18.dres) | copy-start | bytes 6291460
  38.0 25.1 %collective-permute-start.3 = (bf16[3,128,1024]{2,1,0:T(8,128)(2,1)}, bf16[3,128,1024]{2,1,0:T(8,128)(2,1)S(1)}, u32[]{:S(2)}, u32[]{:S(2)}) collective-permute-start(bf16[3,128,1024]{2,1,0:T(8,128)(2,1)} %dynamic-slice_bitcast_fusion), channel_id=1, source_target_pairs={{0,1},{1,2},{2,3},{3,0},{4,7},{5,4},{6,5},{7,6},{8,9},{9,10},{10,1... | collective-permute-start | bytes 2359304 | tf_op jit(solution)/shard_map/ppermute | solution.py:44
  41.3 23.3 %collective-permute-start.2 = (bf16[2,3,128,1024]{3,2,1,0:T(8,128)(2,1)}, bf16[2,3,128,1024]{3,2,1,0:T(8,128)(2,1)S(1)}, u32[]{:S(2)}, u32[]{:S(2)}) collective-permute-start(bf16[2,3,128,1024]{3,2,1,0:T(8,128)(2,1)} %collective-permute-done.1.near), channel_id=1, source_target_pairs={{0,4},{1,5},{2,6},{3,7},{4,0},{5,1},{6,2},{7,3},{8,12},{9,13},{10,... | collective-permute-start | bytes 4718600 | tf_op jit(solution)/shard_map/ppermute | solution.py:44
  53.5 11.1 %copy-start.13 = (f32[1024]{0:T(1024)S(1)}, f32[1024]{0:T(1024)}, u32[]{:S(2)}) copy-start(f32[1024]{0:T(1024)} %param.19) | copy-start | bytes 12292
  53.5 11.1 %copy-start.14 = (f32[1024]{0:T(1024)S(1)}, f32[1024]{0:T(1024)}, u32[]{:S(2)}) copy-start(f32[1024]{0:T(1024)} %param.20) | copy-start | bytes 12292
  53.5 11.1 %copy-start.15 = (f32[1024]{0:T(1024)S(1)}, f32[1024]{0:T(1024)}, u32[]{:S(2)}) copy-start(f32[1024]{0:T(1024)} %param.21) | copy-start | bytes 12292
  54.7 20.1 %all-to-all-start.2 = ((bf16[16,272,128]{2,1,0:T(8,128)(2,1)}), bf16[16,272,128]{2,1,0:T(8,128)(2,1)S(1)}, u32[]{:S(2)}, u32[]{:S(2)}) async-start(bf16[16,272,128]{2,1,0:T(8,128)(2,1)} %shard_map.191), calls=%async_computation.2 | async-start | bytes 2228224 | tf_op jit(solution)/shard_map/all_to_all | solution.py:60
  63.2 3.3 %collective-permute-start.4 = (bf16[3,128,1024]{2,1,0:T(8,128)(2,1)S(1)}, bf16[3,128,1024]{2,1,0:T(8,128)(2,1)S(1)}, u32[]{:S(2)}, u32[]{:S(2)}) collective-permute-start(bf16[3,128,1024]{2,1,0:T(8,128)(2,1)S(1)} %collective-permute-done.3.far), channel_id=1, source_target_pairs={{0,4},{1,5},{2,6},{3,7},{4,0},{5,1},{6,2},{7,3},{8,12},{9,13},{10,... | collective-permute-start | bytes 2359304 | tf_op jit(solution)/shard_map/ppermute | solution.py:44
  64.6 1.9 %copy-start.11 = (bf16[2,3,128,1024]{3,2,1,0:T(8,128)(2,1)}, bf16[2,3,128,1024]{3,2,1,0:T(8,128)(2,1)S(1)}, u32[]{:S(2)}) copy-start(bf16[2,3,128,1024]{3,2,1,0:T(8,128)(2,1)S(1)} %collective-permute-done.2.near_other) | copy-start | bytes 4718596
  66.5 0.9 %copy-start.12 = (bf16[3,128,1024]{2,1,0:T(8,128)(2,1)}, bf16[3,128,1024]{2,1,0:T(8,128)(2,1)S(1)}, u32[]{:S(2)}) copy-start(bf16[3,128,1024]{2,1,0:T(8,128)(2,1)S(1)} %collective-permute-done.4.far_other) | copy-start | bytes 2359300
  75.2 5.9 %copy-start = (f32[256,1024]{1,0:T(8,128)S(1)}, f32[256,1024]{1,0:T(8,128)}, u32[]{:S(2)}) copy-start(f32[256,1024]{1,0:T(8,128)} %master.3) | copy-start | bytes 3145732
  75.2 5.9 %copy-start.1 = (f32[256,1024]{1,0:T(8,128)S(1)}, f32[256,1024]{1,0:T(8,128)}, u32[]{:S(2)}) copy-start(f32[256,1024]{1,0:T(8,128)} %first.3) | copy-start | bytes 3145732
  75.2 5.9 %copy-start.2 = (f32[256,1024]{1,0:T(8,128)S(1)}, f32[256,1024]{1,0:T(8,128)}, u32[]{:S(2)}) copy-start(f32[256,1024]{1,0:T(8,128)} %second.3) | copy-start | bytes 3145732
  75.2 5.9 %copy-start.3 = (bf16[1024,1024]{1,0:T(8,128)(2,1)S(1)}, bf16[1024,1024]{1,0:T(8,128)(2,1)}, u32[]{:S(2)}) copy-start(bf16[1024,1024]{1,0:T(8,128)(2,1)} %get-tuple-element.33.w_in) | copy-start | bytes 6291460
  75.3 5.9 %copy-start.4 = (bf16[1024,1024]{1,0:T(8,128)(2,1)S(1)}, bf16[1024,1024]{1,0:T(8,128)(2,1)}, u32[]{:S(2)}) copy-start(bf16[1024,1024]{1,0:T(8,128)(2,1)} %get-tuple-element.34.m_in) | copy-start | bytes 6291460
  75.3 5.9 %copy-start.5 = (bf16[1024,1024]{1,0:T(8,128)(2,1)S(1)}, bf16[1024,1024]{1,0:T(8,128)(2,1)}, u32[]{:S(2)}) copy-start(bf16[1024,1024]{1,0:T(8,128)(2,1)} %get-tuple-element.35.v_in) | copy-start | bytes 6291460
  75.3 5.9 %copy-start.7 = (f32[3,1024]{1,0:T(4,128)S(1)}, f32[3,1024]{1,0:T(4,128)}, u32[]{:S(2)}) copy-start(f32[3,1024]{1,0:T(4,128)} %vec_first.1) | copy-start | bytes 36868
  75.3 5.9 %copy-start.8 = (f32[3,1024]{1,0:T(4,128)S(1)}, f32[3,1024]{1,0:T(4,128)}, u32[]{:S(2)}) copy-start(f32[3,1024]{1,0:T(4,128)} %vec_second.1) | copy-start | bytes 36868
  75.3 5.8 %collective-permute-start.5 = (bf16[528,1024]{1,0:T(8,128)(2,1)S(1)}, bf16[528,1024]{1,0:T(8,128)(2,1)S(1)}, u32[]{:S(2)}, u32[]{:S(2)}) collective-permute-start(bf16[528,1024]{1,0:T(8,128)(2,1)S(1)} %shard_map.194.value.mine), channel_id=1, source_target_pairs={{0,4},{1,5},{2,6},{3,7},{4,0},{5,1},{6,2},{7,3},{8,12},{9,13},{10,... | collective-permute-start | bytes 3244040 | tf_op jit(solution)/shard_map/ppermute | solution.py:44

commit v6 on v5

--- a/solution.py
+++ b/solution.py
@@ -154,7 +154,7 @@
     state,
     sums,
     token_sems,
-    weight_sem,
+    weight_sems,
     state_sems,
     out_sems,
 ):
@@ -175,12 +175,16 @@
         )
 
     first_ctx = fetch(0, 0)
-    weight_copy = start(weight_hbm, weight, weight_sem)
+    weight_copies = []
+    for b in range(blocks):
+        rows = rows_of_block(b)
+        weight_copies.append(start(weight_hbm.at[rows], weight.at[rows], weight_sems.at[b]))
     copies = [[first_ctx, fetch(0, 1), fetch(0, 2)]]
     bias_row = bias[...]
     gain_row = gain[...]
     sums[...] = jnp.zeros_like(sums)
-    weight_copy.wait()
+    for copy in weight_copies:
+        copy.wait()
     copies[0][0].wait()
     copies += [[fetch(b, n) for n in range(3)] for b in range(1, blocks)]
     product(0)
@@ -188,12 +192,19 @@
     for b in range(blocks):
         copies[b][1].wait()
         copies[b][2].wait()
-        if b == 2:
+        if b == 1:
             shards = (master_hbm, first_hbm, second_hbm)
             state_copies = [start(r, state.at[n], state_sems.at[n]) for n, r in enumerate(shards)]
         if b + 1 < blocks:
             copies[b + 1][0].wait()
             product(b + 1)
+        if b + 1 == blocks:
+            for n, copy in enumerate(state_copies):
+                copy.wait()
+                for half in range(2):
+                    rows = slice(128 * half, 128 * half + 128)
+                    packed[half, n] = (state[n, rows, :] * carried[n]).astype(BF16)
+            outs.append(start(packed, packed_hbm, out_sems.at[blocks]))
         for i in range(0, BLOCK, 64):
             totals = None
             for j in range(i, i + 64, 16):
@@ -207,13 +218,6 @@
                 sums[k] += totals[k]
         rows = rows_of_block(b)
         outs.append(start(dres.at[rows], dres_hbm.at[rows], out_sems.at[b]))
-
-    for n, copy in enumerate(state_copies):
-        copy.wait()
-        for half in range(2):
-            rows = slice(128 * half, 128 * half + 128)
-            packed[half, n] = (state[n, rows, :] * carried[n]).astype(BF16)
-    outs.append(start(packed, packed_hbm, out_sems.at[blocks]))
 
     core = lax.axis_index("c")
 
@@ -256,7 +260,7 @@
             pltpu.VMEM((3, 256, D), F32),
             pltpu.VMEM((3, 8, D), F32),
             DMA((3, D // BLOCK)),
-            DMA,
+            DMA((D // BLOCK,)),
             DMA((3,)),
             DMA((D // BLOCK + 5,)),
         ],
@@ -462,7 +466,7 @@
                 update[at, :] = u
                 return total + fold(u * u)
 
-            sums[side] = lax.fori_loop(0, 8, full, sums[side], unroll=4)
+            sums[side] = lax.fori_loop(0, 8, full, sums[side], unroll=8)
 
     update_sq = jnp.full((1, 1), jnp.sum(sums[0] + sums[1]), F32)
     norm = jnp.sqrt(jnp.full((1, 1), jnp.sum(weight_sq[...]), F32))

time: 88.3 us -> 88.7 us (level)
  no operation moved by 1% of the time
where the time goes in v6:
time: 88.7 us; the launch traced here: 88.2 us
  Pallas kernels  32.5 us (37%)
  starting transfers between devices  30.7 us (35%)
  blocking collectives  12 us (14%)
  waiting for transfers between devices  6.25 us (7%)
  local copies, waits for them, and re-layouts  5.11 us (6%)
  between operations  1.63 us (2%)
    pallas_call x10, Pallas kernels, call(): pl.pallas_call(kernel, out_shape=[jax.ShapeDtypeStruct(shape, dtype) for...  32.5 us
    all_to_all x2, starting transfers between devices, exchange(): lax.all_to_all(value, AXES, split_axis=0, concat_axis=0, axis_index_group...  17.2 us
    ppermute x6, starting transfers between devices, permute(): return lax.ppermute(value, AXES, pairs)  13.6 us
    all_to_all x1, blocking collectives, exchange(): lax.all_to_all(value, AXES, split_axis=0, concat_axis=0, axis_index_group...  12 us
    ppermute x6, waiting for transfers between devices, permute(): return lax.ppermute(value, AXES, pairs)  5.37 us
    unnamed x32, local copies, waits for them, and re-layouts  2.53 us
    squeeze x1, local copies, waits for them, and re-layouts, on_device(): far = next_shard(lax.dynamic_index_in_dim(near, half_at, keepdims=False))  2.06 us
  transfers between devices with their start and end apart: 8, of which 4 were waited for; matrix products, arithmetic and copies ran while one was open for 3% of the time, Pallas kernels for 15%

profile of v6, /device:TPU:1, one launch (start us, length us, event | category | flops | bytes accessed | tf_op | source)
XLA Modules:
  0.0 88.2 jit_solution(6230538350531300380)
XLA Ops:
  0.6 12.2 %shard_map.187 = (bf16[1024,1024]{1,0:T(8,128)(2,1)}, bf16[528,1024]{1,0:T(8,128)(2,1)}, bf16[528,1024]{1,0:T(8,128)(2,1)}, bf16[2,3,128,1024]{3,2,1,0:T(8,128)(2,1)}) custom-call(bf16[1024,1024]{1,0:T(8,128)(2,1)} %ctx_hbm.1, bf16[1024,1024]{1,0:T(8,128)(2,1)} %res_hbm.1, bf16[1024,1024]{1,0:T(8,128)(2,1)} %cot_hbm.1, bf16[1024,1024]{1,0:T(8,128)(2,1)} %weight.1, ...), custom_call_target="tpu_custom_call" | custom-call | flops 4294967296 | tf_op jit(solution)/shard_map/pallas_call | solution.py:85
  12.9 1.5 %collective-permute-start = (bf16[528,1024]{1,0:T(8,128)(2,1)}, bf16[528,1024]{1,0:T(8,128)(2,1)S(1)}, u32[]{:S(2)}, u32[]{:S(2)}) collective-permute-start(bf16[528,1024]{1,0:T(8,128)(2,1)} %get-tuple-element.29), channel_id=1, source_target_pairs={{0,4},{1,5},{2,6},{3,7},{4,0},{5,1},{6,2},{7,3},{8,12},{9,13},{10,... | collective-permute-start | bytes 3244040 | tf_op jit(solution)/shard_map/ppermute | solution.py:44
  14.4 3.8 %collective-permute-start.1 = (bf16[2,3,128,1024]{3,2,1,0:T(8,128)(2,1)}, bf16[2,3,128,1024]{3,2,1,0:T(8,128)(2,1)}, u32[]{:S(2)}, u32[]{:S(2)}) collective-permute-start(bf16[2,3,128,1024]{3,2,1,0:T(8,128)(2,1)} %shard_map.192), channel_id=1, source_target_pairs={{0,1},{1,2},{2,3},{3,0},{4,7},{5,4},{6,5},{7,6},{8,9},{9,10},{10,1... | collective-permute-start | bytes 4718600 | tf_op jit(solution)/shard_map/ppermute | solution.py:44
  18.2 0.0 collective-permute-done.got
  18.2 0.0 copy-done.6
  18.2 1.3 %shard_map.189 = bf16[16,272,128]{2,1,0:T(8,128)(2,1)} custom-call(bf16[528,1024]{1,0:T(8,128)(2,1)S(1)} %copy-done.6, bf16[528,1024]{1,0:T(8,128)(2,1)S(1)} %collective-permute-done.got), custom_call_target="tpu_custom_call" | custom-call | tf_op jit(solution)/shard_map/pallas_call | solution.py:85
  19.5 8.6 %all-to-all-start = ((bf16[16,272,128]{2,1,0:T(8,128)(2,1)}), bf16[16,272,128]{2,1,0:T(8,128)(2,1)S(1)}, u32[]{:S(2)}, u32[]{:S(2)}) async-start(bf16[16,272,128]{2,1,0:T(8,128)(2,1)} %shard_map.189), calls=%async_computation | async-start | bytes 2228224 | tf_op jit(solution)/shard_map/all_to_all | solution.py:60
  28.1 0.0 copy-done.9
  28.1 0.0 copy-start.10
  28.1 1.6 %copy-done.10 = bf16[1024,1024]{1,0:T(8,128)(2,1)S(1)} copy-done((bf16[1024,1024]{1,0:T(8,128)(2,1)S(1)}, bf16[1024,1024]{1,0:T(8,128)(2,1)}, u32[]{:S(2)}) %copy-start.10) | copy-done | bytes 2097176
  29.7 3.8 %shard_map.188 = (bf16[1024,1024]{1,0:T(8,128)(2,1)}, f32[8,128]{1,0:T(8,128)S(1)}) custom-call(bf16[1024,1024]{1,0:T(8,128)(2,1)S(1)} %copy-done.10, bf16[1024,1024]{1,0:T(8,128)(2,1)S(1)} %copy-done.9), custom_call_target="tpu_custom_call" | custom-call | flops 2147483648 | tf_op jit(solution)/shard_map/pallas_call | solution.py:85
  33.5 0.5 slice.3
  34.7 1.2 %collective-permute-done.1.near = bf16[2,3,128,1024]{3,2,1,0:T(8,128)(2,1)} collective-permute-done((bf16[2,3,128,1024]{3,2,1,0:T(8,128)(2,1)}, bf16[2,3,128,1024]{3,2,1,0:T(8,128)(2,1)}, u32[]{:S(2)}, u32[]{:S(2)}) %collective-permute-start.1) | collective-permute-done | bytes 1572896 | tf_op jit(solution)/shard_map/ppermute | solution.py:44
  35.9 2.1 %dynamic-slice_bitcast_fusion = bf16[3,128,1024]{2,1,0:T(8,128)(2,1)} fusion(bf16[2,3,128,1024]{3,2,1,0:T(8,128)(2,1)} %collective-permute-done.1.near, s32[]{:T(128)S(6)} %select_n.4), kind=kLoop, calls=%fused_computation | loop fusion | bytes 1572868 | tf_op jit(solution)/shard_map/jit(dynamic_index_in_dim)/squeeze | solution.py:555
  37.9 3.3 %collective-permute-start.3 = (bf16[3,128,1024]{2,1,0:T(8,128)(2,1)}, bf16[3,128,1024]{2,1,0:T(8,128)(2,1)S(1)}, u32[]{:S(2)}, u32[]{:S(2)}) collective-permute-start(bf16[3,128,1024]{2,1,0:T(8,128)(2,1)} %dynamic-slice_bitcast_fusion), channel_id=1, source_target_pairs={{0,1},{1,2},{2,3},{3,0},{4,7},{5,4},{6,5},{7,6},{8,9},{9,10},{10,1... | collective-permute-start | bytes 2359304 | tf_op jit(solution)/shard_map/ppermute | solution.py:44
  41.2 0.0 collective-permute-start.2
  41.2 0.0 all-to-all-done.got
  41.2 0.2 shard_map.190
  41.4 12.0 %all_to_all.15.got = bf16[4,272,128]{2,1,0:T(8,128)(2,1)S(1)} all-to-all(bf16[4,272,128]{2,1,0:T(8,128)(2,1)S(1)} %shard_map.190), channel_id=1, replica_groups={{0,1,2,3},{7,6,5,4},{8,9,10,11},{15,14,13,12},{16,17,18,19},{23,22,21,2..., dimensions={0} | all-to-all | bytes 557056 | tf_op jit(solution)/shard_map/all_to_all | solution.py:60
  53.4 1.2 %shard_map.191 = bf16[16,272,128]{2,1,0:T(8,128)(2,1)} custom-call(bf16[4,272,128]{2,1,0:T(8,128)(2,1)S(1)} %all_to_all.15.got), custom_call_target="tpu_custom_call" | custom-call | tf_op jit(solution)/shard_map/pallas_call | solution.py:85
  54.6 8.5 %all-to-all-start.2 = ((bf16[16,272,128]{2,1,0:T(8,128)(2,1)}), bf16[16,272,128]{2,1,0:T(8,128)(2,1)S(1)}, u32[]{:S(2)}, u32[]{:S(2)}) async-start(bf16[16,272,128]{2,1,0:T(8,128)(2,1)} %shard_map.191), calls=%async_computation.2 | async-start | bytes 2228224 | tf_op jit(solution)/shard_map/all_to_all | solution.py:60
  63.1 0.0 collective-permute-done.3.far
  63.1 1.3 %collective-permute-start.4 = (bf16[3,128,1024]{2,1,0:T(8,128)(2,1)S(1)}, bf16[3,128,1024]{2,1,0:T(8,128)(2,1)S(1)}, u32[]{:S(2)}, u32[]{:S(2)}) collective-permute-start(bf16[3,128,1024]{2,1,0:T(8,128)(2,1)S(1)} %collective-permute-done.3.far), channel_id=1, source_target_pairs={{0,4},{1,5},{2,6},{3,7},{4,0},{5,1},{6,2},{7,3},{8,12},{9,13},{10,... | collective-permute-start | bytes 2359304 | tf_op jit(solution)/shard_map/ppermute | solution.py:44
  64.3 0.0 copy-done.13
  64.3 0.0 copy-done.14
  64.3 0.0 copy-done.15
  64.4 0.0 collective-permute-done.2.near_other
  64.4 0.0 copy-start.11
  64.4 1.9 %collective-permute-done.4.far_other = bf16[3,128,1024]{2,1,0:T(8,128)(2,1)S(1)} collective-permute-done((bf16[3,128,1024]{2,1,0:T(8,128)(2,1)S(1)}, bf16[3,128,1024]{2,1,0:T(8,128)(2,1)S(1)}, u32[]{:S(2)}, u32[]{:S(2)}) %collective-permute-start.4) | collective-permute-done | bytes 786464 | tf_op jit(solution)/shard_map/ppermute | solution.py:44
  66.2 0.0 copy-done.11
  66.2 0.9 copy-done.12
  67.1 6.7 %shard_map.193 = (bf16[1024,1024]{1,0:T(8,128)(2,1)}, bf16[1024,1024]{1,0:T(8,128)(2,1)}, bf16[1024,1024]{1,0:T(8,128)(2,1)}, f32[8,1024]{1,0:T(8,128)S(1)}) custom-call(bf16[2,3,128,1024]{3,2,1,0:T(8,128)(2,1)} %collective-permute-done.1.near, bf16[2,3,128,1024]{3,2,1,0:T(8,128)(2,1)} %copy-done.11, bf16[3,128,1024]{2,1,0:T(8,128)(2,1)S(1)} %collective-permute-done.3.far, ...), custom_call_target="tpu_custom_call" | custom-call | flops 1073741824 | bytes 16777216 | tf_op jit(solution)/shard_map/pallas_call | solution.py:85
  73.8 0.9 all-to-all-done.2.pieces
  74.7 0.4 shard_map.194.value.mine
  75.1 0.0 copy-start
  75.1 0.0 copy-start.1
  75.1 0.0 copy-start.2
  75.1 0.0 copy-start.3
  75.2 0.0 copy-start.4
  75.2 0.0 copy-start.5
  75.2 0.0 copy-start.7
  75.2 0.0 copy-start.8
  75.2 3.7 %collective-permute-start.5 = (bf16[528,1024]{1,0:T(8,128)(2,1)S(1)}, bf16[528,1024]{1,0:T(8,128)(2,1)S(1)}, u32[]{:S(2)}, u32[]{:S(2)}) collective-permute-start(bf16[528,1024]{1,0:T(8,128)(2,1)S(1)} %shard_map.194.value.mine), channel_id=1, source_target_pairs={{0,4},{1,5},{2,6},{3,7},{4,0},{5,1},{6,2},{7,3},{8,12},{9,13},{10,... | collective-permute-start | bytes 3244040 | tf_op jit(solution)/shard_map/ppermute | solution.py:44
  78.9 2.3 %collective-permute-done.5.others = bf16[528,1024]{1,0:T(8,128)(2,1)S(1)} collective-permute-done((bf16[528,1024]{1,0:T(8,128)(2,1)S(1)}, bf16[528,1024]{1,0:T(8,128)(2,1)S(1)}, u32[]{:S(2)}, u32[]{:S(2)}) %collective-permute-start.5) | collective-permute-done | bytes 1081376 | tf_op jit(solution)/shard_map/ppermute | solution.py:44
  81.2 0.0 copy-done
  81.2 0.0 copy-done.1
  81.2 0.0 copy-done.2
  81.2 6.8 %shard_map.196 = (bf16[1024,1024]{1,0:T(8,128)(2,1)}, f32[256,1024]{1,0:T(8,128)}, f32[256,1024]{1,0:T(8,128)}, f32[256,1024]{1,0:T(8,128)}, f32[3,1024]{1,0:T(4...) custom-call(bf16[528,1024]{1,0:T(8,128)(2,1)S(1)} %shard_map.194.value.mine, ...), custom_call_target="tpu_custom_call" | custom-call | tf_op jit(solution)/shard_map/pallas_call | solution.py:85
  (14 shorter events, 0.0 us)
Async XLA Ops:
  12.9 5.3 %collective-permute-start = (bf16[528,1024]{1,0:T(8,128)(2,1)}, bf16[528,1024]{1,0:T(8,128)(2,1)S(1)}, u32[]{:S(2)}, u32[]{:S(2)}) collective-permute-start(bf16[528,1024]{1,0:T(8,128)(2,1)} %get-tuple-element.29), channel_id=1, source_target_pairs={{0,4},{1,5},{2,6},{3,7},{4,0},{5,1},{6,2},{7,3},{8,12},{9,13},{10,... | collective-permute-start | bytes 3244040 | tf_op jit(solution)/shard_map/ppermute | solution.py:44
  14.4 3.8 %copy-start.6 = (bf16[528,1024]{1,0:T(8,128)(2,1)S(1)}, bf16[528,1024]{1,0:T(8,128)(2,1)}, u32[]{:S(2)}) copy-start(bf16[528,1024]{1,0:T(8,128)(2,1)} %get-tuple-element.28.keep) | copy-start | bytes 3244036
  14.4 21.5 %collective-permute-start.1 = (bf16[2,3,128,1024]{3,2,1,0:T(8,128)(2,1)}, bf16[2,3,128,1024]{3,2,1,0:T(8,128)(2,1)}, u32[]{:S(2)}, u32[]{:S(2)}) collective-permute-start(bf16[2,3,128,1024]{3,2,1,0:T(8,128)(2,1)} %shard_map.192), channel_id=1, source_target_pairs={{0,1},{1,2},{2,3},{3,0},{4,7},{5,4},{6,5},{7,6},{8,9},{9,10},{10,1... | collective-permute-start | bytes 4718600 | tf_op jit(solution)/shard_map/ppermute | solution.py:44
  19.5 8.6 %copy-start.9 = (bf16[1024,1024]{1,0:T(8,128)(2,1)S(1)}, bf16[1024,1024]{1,0:T(8,128)(2,1)}, u32[]{:S(2)}) copy-start(bf16[1024,1024]{1,0:T(8,128)(2,1)} %weight.1) | copy-start | bytes 6291460
  19.5 21.8 %all-to-all-start = ((bf16[16,272,128]{2,1,0:T(8,128)(2,1)}), bf16[16,272,128]{2,1,0:T(8,128)(2,1)S(1)}, u32[]{:S(2)}, u32[]{:S(2)}) async-start(bf16[16,272,128]{2,1,0:T(8,128)(2,1)} %shard_map.189), calls=%async_computation | async-start | bytes 2228224 | tf_op jit(solution)/shard_map/all_to_all | solution.py:60
  28.1 1.6 %copy-start.10 = (bf16[1024,1024]{1,0:T(8,128)(2,1)S(1)}, bf16[1024,1024]{1,0:T(8,128)(2,1)}, u32[]{:S(2)}) copy-start(bf16[1024,1024]{1,0:T(8,128)(2,1)} %get-tuple-element.18.dres) | copy-start | bytes 6291460
  37.9 25.1 %collective-permute-start.3 = (bf16[3,128,1024]{2,1,0:T(8,128)(2,1)}, bf16[3,128,1024]{2,1,0:T(8,128)(2,1)S(1)}, u32[]{:S(2)}, u32[]{:S(2)}) collective-permute-start(bf16[3,128,1024]{2,1,0:T(8,128)(2,1)} %dynamic-slice_bitcast_fusion), channel_id=1, source_target_pairs={{0,1},{1,2},{2,3},{3,0},{4,7},{5,4},{6,5},{7,6},{8,9},{9,10},{10,1... | collective-permute-start | bytes 2359304 | tf_op jit(solution)/shard_map/ppermute | solution.py:44
  41.2 23.1 %collective-permute-start.2 = (bf16[2,3,128,1024]{3,2,1,0:T(8,128)(2,1)}, bf16[2,3,128,1024]{3,2,1,0:T(8,128)(2,1)S(1)}, u32[]{:S(2)}, u32[]{:S(2)}) collective-permute-start(bf16[2,3,128,1024]{3,2,1,0:T(8,128)(2,1)} %collective-permute-done.1.near), channel_id=1, source_target_pairs={{0,4},{1,5},{2,6},{3,7},{4,0},{5,1},{6,2},{7,3},{8,12},{9,13},{10,... | collective-permute-start | bytes 4718600 | tf_op jit(solution)/shard_map/ppermute | solution.py:44
  53.4 11.0 %copy-start.13 = (f32[1024]{0:T(1024)S(1)}, f32[1024]{0:T(1024)}, u32[]{:S(2)}) copy-start(f32[1024]{0:T(1024)} %param.19) | copy-start | bytes 12292
  53.4 11.0 %copy-start.14 = (f32[1024]{0:T(1024)S(1)}, f32[1024]{0:T(1024)}, u32[]{:S(2)}) copy-start(f32[1024]{0:T(1024)} %param.20) | copy-start | bytes 12292
  53.4 11.0 %copy-start.15 = (f32[1024]{0:T(1024)S(1)}, f32[1024]{0:T(1024)}, u32[]{:S(2)}) copy-start(f32[1024]{0:T(1024)} %param.21) | copy-start | bytes 12292
  54.6 20.1 %all-to-all-start.2 = ((bf16[16,272,128]{2,1,0:T(8,128)(2,1)}), bf16[16,272,128]{2,1,0:T(8,128)(2,1)S(1)}, u32[]{:S(2)}, u32[]{:S(2)}) async-start(bf16[16,272,128]{2,1,0:T(8,128)(2,1)} %shard_map.191), calls=%async_computation.2 | async-start | bytes 2228224 | tf_op jit(solution)/shard_map/all_to_all | solution.py:60
  63.1 3.2 %collective-permute-start.4 = (bf16[3,128,1024]{2,1,0:T(8,128)(2,1)S(1)}, bf16[3,128,1024]{2,1,0:T(8,128)(2,1)S(1)}, u32[]{:S(2)}, u32[]{:S(2)}) collective-permute-start(bf16[3,128,1024]{2,1,0:T(8,128)(2,1)S(1)} %collective-permute-done.3.far), channel_id=1, source_target_pairs={{0,4},{1,5},{2,6},{3,7},{4,0},{5,1},{6,2},{7,3},{8,12},{9,13},{10,... | collective-permute-start | bytes 2359304 | tf_op jit(solution)/shard_map/ppermute | solution.py:44
  64.4 1.9 %copy-start.11 = (bf16[2,3,128,1024]{3,2,1,0:T(8,128)(2,1)}, bf16[2,3,128,1024]{3,2,1,0:T(8,128)(2,1)S(1)}, u32[]{:S(2)}) copy-start(bf16[2,3,128,1024]{3,2,1,0:T(8,128)(2,1)S(1)} %collective-permute-done.2.near_other) | copy-start | bytes 4718596
  66.2 0.9 copy-start.12
  75.1 6.1 %copy-start = (f32[256,1024]{1,0:T(8,128)S(1)}, f32[256,1024]{1,0:T(8,128)}, u32[]{:S(2)}) copy-start(f32[256,1024]{1,0:T(8,128)} %master.3) | copy-start | bytes 3145732
  75.1 6.1 %copy-start.1 = (f32[256,1024]{1,0:T(8,128)S(1)}, f32[256,1024]{1,0:T(8,128)}, u32[]{:S(2)}) copy-start(f32[256,1024]{1,0:T(8,128)} %first.3) | copy-start | bytes 3145732
  75.1 6.1 %copy-start.2 = (f32[256,1024]{1,0:T(8,128)S(1)}, f32[256,1024]{1,0:T(8,128)}, u32[]{:S(2)}) copy-start(f32[256,1024]{1,0:T(8,128)} %second.3) | copy-start | bytes 3145732
  75.1 6.1 %copy-start.3 = (bf16[1024,1024]{1,0:T(8,128)(2,1)S(1)}, bf16[1024,1024]{1,0:T(8,128)(2,1)}, u32[]{:S(2)}) copy-start(bf16[1024,1024]{1,0:T(8,128)(2,1)} %get-tuple-element.33.w_in) | copy-start | bytes 6291460
  75.2 6.1 %copy-start.4 = (bf16[1024,1024]{1,0:T(8,128)(2,1)S(1)}, bf16[1024,1024]{1,0:T(8,128)(2,1)}, u32[]{:S(2)}) copy-start(bf16[1024,1024]{1,0:T(8,128)(2,1)} %get-tuple-element.34.m_in) | copy-start | bytes 6291460
  75.2 6.1 %copy-start.5 = (bf16[1024,1024]{1,0:T(8,128)(2,1)S(1)}, bf16[1024,1024]{1,0:T(8,128)(2,1)}, u32[]{:S(2)}) copy-start(bf16[1024,1024]{1,0:T(8,128)(2,1)} %get-tuple-element.35.v_in) | copy-start | bytes 6291460
  75.2 6.1 %copy-start.7 = (f32[3,1024]{1,0:T(4,128)S(1)}, f32[3,1024]{1,0:T(4,128)}, u32[]{:S(2)}) copy-start(f32[3,1024]{1,0:T(4,128)} %vec_first.1) | copy-start | bytes 36868
  75.2 6.1 %copy-start.8 = (f32[3,1024]{1,0:T(4,128)S(1)}, f32[3,1024]{1,0:T(4,128)}, u32[]{:S(2)}) copy-start(f32[3,1024]{1,0:T(4,128)} %vec_second.1) | copy-start | bytes 36868
  75.2 6.0 %collective-permute-start.5 = (bf16[528,1024]{1,0:T(8,128)(2,1)S(1)}, bf16[528,1024]{1,0:T(8,128)(2,1)S(1)}, u32[]{:S(2)}, u32[]{:S(2)}) collective-permute-start(bf16[528,1024]{1,0:T(8,128)(2,1)S(1)} %shard_map.194.value.mine), channel_id=1, source_target_pairs={{0,4},{1,5},{2,6},{3,7},{4,0},{5,1},{6,2},{7,3},{8,12},{9,13},{10,... | collective-permute-start | bytes 3244040 | tf_op jit(solution)/shard_map/ppermute | solution.py:44
